TPU v7x, 256 devices: a whole 4x4x8 slice. The times are simulated.
256 devices in a mesh: region: 8 (over x_hi, y), dev: 32 (over z, x_lo, core).
Axes of the slice: x: 4 (x_hi: 2, x_lo: 2; x = x_hi * 2 + x_lo), y: 4, z: 8, core: 2. Of those that a mesh axis runs over, the one named last changes fastest.
Arguments:
- acts: bfloat16 [8, 2048, 2048], P('region', 'dev'), may hold values from -6 to 6
- cotan: bfloat16 [8, 2048, 2048], P('region', 'dev'), may hold values from -6 to 6
- w_up: bfloat16 [8, 2048, 4096], P('region', None, 'dev'), may hold values from -6 to 6
- w_down: bfloat16 [8, 4096, 2048], P('region', 'dev'), may hold values from -6 to 6
- drift_up: bfloat16 [8, 2048, 4096], P('region', None, 'dev'), may hold values from -4 to 4
- drift_down: bfloat16 [8, 4096, 2048], P('region', 'dev'), may hold values from -4 to 4
- path: int32 [8], replicated, may hold values from 0 to 15
- slot_of: int32 [16], replicated, may hold values from 0 to 15, each once
- global_up: bfloat16 [16, 2048, 4096], P('region', None, 'dev'), may hold values from -6 to 6
- global_down: bfloat16 [16, 4096, 2048], P('region', 'dev'), may hold values from -6 to 6
- mom_up: float32 [16, 2048, 4096], P('region', None, 'dev'), may hold values from -4 to 4
- mom_down: float32 [16, 4096, 2048], P('region', 'dev'), may hold values from -4 to 4
Outputs:
- new_up: bfloat16 [16, 2048, 4096], P('region', None, 'dev')
- new_down: bfloat16 [16, 4096, 2048], P('region', 'dev')
- region_up: bfloat16 [8, 2048, 4096], P('region', None, 'dev')
- region_down: bfloat16 [8, 4096, 2048], P('region', 'dev')
Inputs may be any that keep to these rules, and one draw needn't show every extreme that they name: `slot_of`: each module's slot once; slot s lies in region s // 2.
All inputs are finite; a program needn't handle non-finite values.
Results may differ from a plain program's by a relative error of at most 0.0035.
Values may be sent and summed in bfloat16 or wider, within the bound.
No kernel may reach another device: no remote copies, remote signals or barrier semaphores. Data moves between devices by JAX's collectives and lax.ppermute only.
A program may use at most 128 MiB of HBM per device.

v0:
```python
import jax
import jax.numpy as jnp
from jax import lax
from jax.sharding import PartitionSpec as P

D = 2048
FF = 4096


def gelu_tanh(value):
    return jax.nn.gelu(value, approximate=True)


def on_device(
    acts,
    cotan,
    w_up,
    w_down,
    drift_up,
    drift_down,
    path,
    slot_of,
    global_up,
    global_down,
    mom_up,
    mom_down,
):
    weight_up = w_up[0]
    weight_down = w_down[0]
    pieces = (
        lax.all_gather(acts, "dev", axis=1, tiled=True),
        lax.all_gather(cotan, "dev", axis=1, tiled=True),
    )
    inputs = pieces[0][0]
    cotangent = pieces[1][0]
    hidden = jnp.dot(inputs, weight_up, preferred_element_type=jnp.float32) * D ** (-0.5)
    active, pullback = jax.vjp(gelu_tanh, hidden)
    active_b = active.astype(jnp.bfloat16)
    dactive = jnp.dot(cotangent, weight_down.T, preferred_element_type=jnp.float32) * FF ** (-0.5)
    dhidden = pullback(dactive)[0].astype(jnp.bfloat16)
    grad_down = jnp.dot(active_b.T, cotangent, preferred_element_type=jnp.float32) * FF ** (-0.5)
    grad_up = jnp.dot(inputs.T, dhidden, preferred_element_type=jnp.float32) * D ** (-0.5)
    grad_up, grad_down = (grad_up, grad_down)
    pseudo_up = (drift_up[0].astype(jnp.float32) + 0.5 * grad_up).astype(jnp.bfloat16)[None]
    pseudo_down = (drift_down[0].astype(jnp.float32) + 0.5 * grad_down).astype(jnp.bfloat16)[None]
    my_region = lax.axis_index("region")
    owned = global_up.shape[0]
    module_ids = jnp.arange(slot_of.shape[0], dtype=jnp.int32)
    target = jnp.sum(jnp.where(path[:, None] == module_ids[None, :], slot_of[None, :], 0), axis=1)
    local_slots = my_region * owned + jnp.arange(owned, dtype=jnp.int32)
    chosen = (target[:, None] == local_slots[None, :]).astype(jnp.float32)
    chosen_b = chosen.astype(jnp.bfloat16)
    count = jnp.sum(chosen, axis=0)
    pieces = (
        lax.all_gather(pseudo_up, "region", axis=0, tiled=True),
        lax.all_gather(pseudo_down, "region", axis=0, tiled=True),
    )
    more_up = jnp.einsum("ko,kdf->odf", chosen_b, pieces[0], preferred_element_type=jnp.float32)
    more_down = jnp.einsum("ko,kfd->ofd", chosen_b, pieces[1], preferred_element_type=jnp.float32)
    divisor = jnp.maximum(count, 1.0)[:, None, None]
    delta_up = more_up / divisor
    delta_down = more_down / divisor
    moment_up = 0.9 * mom_up + delta_up
    moment_down = 0.9 * mom_down + delta_down
    new_up = (global_up.astype(jnp.float32) - 0.7 * (delta_up + 0.9 * moment_up)).astype(
        jnp.bfloat16
    )
    new_down = (global_down.astype(jnp.float32) - 0.7 * (delta_down + 0.9 * moment_down)).astype(
        jnp.bfloat16
    )
    reply_up = jnp.einsum(
        "ro,odf->rdf", chosen_b, new_up, preferred_element_type=jnp.float32
    ).astype(jnp.bfloat16)
    reply_down = jnp.einsum(
        "ro,ofd->rfd", chosen_b, new_down, preferred_element_type=jnp.float32
    ).astype(jnp.bfloat16)
    back_up, back_down = (
        lax.all_to_all(reply_up, "region", split_axis=0, concat_axis=0, tiled=True),
        lax.all_to_all(reply_down, "region", split_axis=0, concat_axis=0, tiled=True),
    )
    region_up = jnp.sum(back_up.astype(jnp.float32), axis=0, keepdims=True).astype(jnp.bfloat16)
    region_down = jnp.sum(back_down.astype(jnp.float32), axis=0, keepdims=True).astype(jnp.bfloat16)
    return (new_up, new_down, region_up, region_down)


def solution(mesh):
    placed = (
        P("region", "dev", None),
        P("region", "dev", None),
        P("region", None, "dev"),
        P("region", "dev", None),
        P("region", None, "dev"),
        P("region", "dev", None),
        P(),
        P(),
        P("region", None, "dev"),
        P("region", "dev", None),
        P("region", None, "dev"),
        P("region", "dev", None),
    )
    return jax.shard_map(
        on_device,
        mesh=mesh,
        in_specs=placed,
        out_specs=(
            P("region", None, "dev"),
            P("region", "dev", None),
            P("region", None, "dev"),
            P("region", "dev", None),
        ),
        check_vma=False,
    )
```

profile of v0, /device:TPU:1, one launch (start us, length us, event | category | flops | bytes accessed | tf_op | source)
XLA Modules:
  0.0 450.8 jit_solution(2669533854706898795)
XLA Ops:
  7.2 0.0 copy-start
  7.2 0.0 all-gather.9.cloned.1.call-start
  7.2 0.7 all-gather.9.cloned.1.call-update
  7.9 0.0 all-gather.7.cloned.1.call-start
  8.0 0.7 all-gather.7.cloned.1.call-update
  8.7 0.0 copy-start.2
  8.7 0.0 all-gather.13.cloned.1.call-start
  8.7 77.7 %all-gather.9.cloned.1.call-done = bf16[1,2048,2048]{2,1,0:T(8,128)(2,1)} async-done(((bf16[1,64,2048]{2,1,0:T(8,128)(2,1)}), bf16[1,2048,2048]{2,1,0:T(8,128)(2,1)}) %all-gather.9.cloned.1.call-update) | async-done | bytes 8388624 | tf_op jit(solution)/shard_map/all_gather | solution.py:31
  86.4 0.0 copy-done
  86.4 5.7 %fusion.16 = f32[2048,128]{1,0:T(8,128)S(1)} fusion(bf16[1,2048,2048]{2,1,0:T(8,128)(2,1)} %all-gather.9.cloned.1.call-done, bf16[1,2048,128]{2,1,0:T(8,128)(2,1)S(1)} %copy-done), kind=kOutput, calls=%fused_computation.14 | convolution fusion | flops 1074003968 | bytes 9961472 | tf_op jit(solution)/shard_map/dot_general | solution.py:36
  92.1 0.0 copy-start.3
  92.2 68.3 %all-gather.7.cloned.1.call-done = bf16[1,2048,2048]{2,1,0:T(8,128)(2,1)} async-done(((bf16[1,64,2048]{2,1,0:T(8,128)(2,1)}), bf16[1,2048,2048]{2,1,0:T(8,128)(2,1)}) %all-gather.7.cloned.1.call-update) | async-done | bytes 8388624 | tf_op jit(solution)/shard_map/all_gather | solution.py:32
  160.5 0.0 copy-done.2
  160.5 5.6 %fusion.31 = bf16[128,2048]{1,0:T(8,128)(2,1)} fusion(bf16[1,2048,2048]{2,1,0:T(8,128)(2,1)} %all-gather.7.cloned.1.call-done, f32[2048,128]{1,0:T(8,128)S(1)} %fusion.16, bf16[1,128,2048]{2,1,0:T(8,128)(2,1)S(1)} %copy-done.2), kind=kOutput, calls=%fused_computation.19 | convolution fusion | flops 1077149696 | bytes 10485760 | tf_op jit(solution)/shard_map/dot_general | solution.py:41
  166.1 0.0 all-gather.13.cloned.1.call-update
  166.2 0.0 all-gather.11.cloned.1.call-start
  166.2 0.0 copy-done.3
  166.2 0.2 copy.37
  166.4 0.0 copy-start.5
  166.4 0.0 copy-start.6
  166.5 0.0 copy-start.4
  166.5 12.4 %fusion.34 = bf16[2048,128]{0,1:T(8,128)(2,1)} fusion(bf16[1,2048,2048]{2,1,0:T(8,128)(2,1)} %all-gather.9.cloned.1.call-done, f32[2048,128]{1,0:T(8,128)S(1)} %fusion.16, bf16[1,2048,2048]{2,1,0:T(8,128)(2,1)} %all-gather.7.cloned.1.call-done, bf16[1,2048,128]{1,2,0:T(8,128)(2,1)S(1)} %copy.37, bf16[1,128,2048]{2,1,0:T(8,128)(2,1)} %param.15), kind=kOutput, calls=%fused_computation.20 | convolution fusion | flops 2154037248 | bytes 19398656 | tf_op jit(solution)/shard_map/dot_general | solution.py:42
  178.9 0.0 all-gather.11.cloned.1.call-update
  178.9 0.0 copy-done.5
  178.9 0.0 copy-done.6
  178.9 0.2 select_reduce_fusion
  179.1 0.2 fusion.70
  179.3 0.1 fusion.72
  179.4 62.5 %all-gather.13.cloned.1.call-done = bf16[1024,2048]{1,0:T(8,128)(2,1)} async-done(((bf16[128,2048]{1,0:T(8,128)(2,1)}), bf16[1024,2048]{1,0:T(8,128)(2,1)}) %all-gather.13.cloned.1.call-update) | async-done | bytes 4194320 | tf_op jit(solution)/shard_map/all_gather | solution.py:56
  241.8 0.0 copy-done.4
  241.8 9.1 %subtract_convert_fusion = bf16[2,128,2048]{2,0,1:T(2,128)(2,1)S(1)} fusion(f32[2,128,2048]{2,1,0:T(8,128)} %param.23, f32[2]{0:T(128)S(1)} %broadcast_maximum_fusion, bf16[2,128,2048]{2,1,0:T(8,128)(2,1)S(1)} %copy-done.4, bf16[8,2,1]{0,1,2:T(2,128)(2,1)S(1)} %fusion.72, bf16[8,128,2048]{2,1,0:T(8,128)(2,1)} %bitcast.71), kind=kOutput, calls=%fused_computation.29 | convolution fusion | flops 13107200 | bytes 8388648 | tf_op jit(solution)/shard_map/ko,kfd->ofd/dot_general | solution.py:59
  251.0 1.6 convolution_convert_fusion
  252.6 4.3 copy.44
  256.9 4.8 %all-to-all-start.1 = ((bf16[8,128,2048]{2,1,0:T(8,128)(2,1)}), bf16[8,128,2048]{2,1,0:T(8,128)(2,1)}, u32[]{:S(2)}, u32[]{:S(2)}) async-start(bf16[8,128,2048]{2,1,0:T(8,128)(2,1)} %copy.44), calls=%async_computation.1 | async-start | bytes 8388608 | tf_op jit(solution)/shard_map/all_to_all | solution.py:79
  261.7 99.6 %all-gather.11.cloned.1.call-done = bf16[16384,128]{0,1:T(8,128)(2,1)} async-done(((bf16[2048,128]{0,1:T(8,128)(2,1)}), bf16[16384,128]{0,1:T(8,128)(2,1)}) %all-gather.11.cloned.1.call-update) | async-done | bytes 4194320 | tf_op jit(solution)/shard_map/all_gather | solution.py:55
  361.3 7.3 %copy.47 = bf16[16,8,8,2048]{3,2,1,0:T(8,128)(2,1)} copy(bf16[16,8,8,2048]{3,1,2,0:T(8,128)(2,1)} %bitcast.68) | data formatting | bytes 8388608
  368.6 7.2 %copy.38 = bf16[8,2048,128]{2,0,1:T(8,128)(2,1)} copy(bf16[8,2048,128]{1,0,2:T(8,128)(2,1)} %bitcast.67) | data formatting | bytes 8388608 | tf_op jit(solution)/shard_map/all_gather | solution.py:55
  375.8 7.3 %subtract_convert_fusion.1 = bf16[2,2048,128]{2,0,1:T(2,128)(2,1)S(1)} fusion(f32[2,2048,128]{2,1,0:T(8,128)} %param.22, bf16[8,2,1]{0,1,2:T(2,128)(2,1)S(1)} %fusion.72, bf16[8,2048,128]{2,0,1:T(8,128)(2,1)} %copy.38, f32[2]{0:T(128)S(1)} %broadcast_maximum_fusion, bf16[2,2048,128]{2,1,0:T(8,128)(2,1)} %param.20), kind=kOutput, calls=%fused_computation.30 | convolution fusion | flops 13107200 | bytes 8388648 | tf_op jit(solution)/shard_map/ko,kdf->odf/dot_general | solution.py:58
  383.1 1.6 convolution_convert_fusion.1
  384.8 2.6 copy.43
  387.4 0.0 all-to-all-done.1
  387.4 4.6 %all-to-all-start = ((bf16[8,2048,128]{2,1,0:T(8,128)(2,1)}), bf16[8,2048,128]{2,1,0:T(8,128)(2,1)}, u32[]{:S(2)}, u32[]{:S(2)}) async-start(bf16[8,2048,128]{2,1,0:T(8,128)(2,1)} %copy.43), calls=%async_computation | async-start | bytes 8388608 | tf_op jit(solution)/shard_map/all_to_all | solution.py:78
  392.0 1.1 copy.45
  393.1 0.0 copy-start.1
  393.1 1.3 copy.46
  394.4 3.8 reduce_sum.45
  398.2 42.3 %all-to-all-done = bf16[8,2048,128]{2,1,0:T(8,128)(2,1)} async-done(((bf16[8,2048,128]{2,1,0:T(8,128)(2,1)}), bf16[8,2048,128]{2,1,0:T(8,128)(2,1)}, u32[]{:S(2)}, u32[]{:S(2)}) %all-to-all-start) | async-done | bytes 4194336 | tf_op jit(solution)/shard_map/all_to_all | solution.py:78
  440.6 3.7 reduce_sum.44
  444.3 0.0 copy-done.1
  (2 shorter events, 0.0 us)
Async XLA Ops:
  7.2 79.3 %copy-start = (bf16[1,2048,128]{2,1,0:T(8,128)(2,1)S(1)}, bf16[1,2048,128]{2,1,0:T(8,128)(2,1)}, u32[]{:S(2)}) copy-start(bf16[1,2048,128]{2,1,0:T(8,128)(2,1)} %param.14) | copy-start | bytes 1572868
  7.2 79.2 %all-gather.9.cloned.1.call-start = ((), (), s32[]{:S(2)}) async-start(), calls=%async_computation.3 | async-start | bytes 8650752 | tf_op jit(solution)/shard_map/all_gather | solution.py:31
  7.9 152.6 %all-gather.7.cloned.1.call-start = ((), (), s32[]{:S(2)}) async-start(), calls=%async_computation.2 | async-start | bytes 8650752 | tf_op jit(solution)/shard_map/all_gather | solution.py:32
  8.7 151.8 %copy-start.2 = (bf16[1,128,2048]{2,1,0:T(8,128)(2,1)S(1)}, bf16[1,128,2048]{2,1,0:T(8,128)(2,1)}, u32[]{:S(2)}) copy-start(bf16[1,128,2048]{2,1,0:T(8,128)(2,1)} %param.17) | copy-start | bytes 1572868
  8.7 233.2 %all-gather.13.cloned.1.call-start = ((), (), s32[]{:S(2)}) async-start(), calls=%async_computation.5 | async-start | bytes 4718592 | tf_op jit(solution)/shard_map/all_gather | solution.py:56
  92.1 74.1 %copy-start.3 = (bf16[1,2048,128]{2,1,0:T(8,128)(2,1)S(1)}, bf16[1,2048,128]{2,1,0:T(8,128)(2,1)}, u32[]{:S(2)}) copy-start(bf16[1,2048,128]{2,1,0:T(8,128)(2,1)} %param.16) | copy-start | bytes 1572868
  166.2 195.2 %all-gather.11.cloned.1.call-start = ((), (), s32[]{:S(2)}) async-start(), calls=%async_computation.4 | async-start | bytes 4718592 | tf_op jit(solution)/shard_map/all_gather | solution.py:55
  166.4 12.5 %copy-start.5 = (s32[16]{0:T(128)S(1)}, s32[16]{0:T(128)}, u32[]{:S(2)}) copy-start(s32[16]{0:T(128)} %param.19) | copy-start | bytes 196
  166.4 12.5 %copy-start.6 = (s32[8]{0:T(128)S(1)}, s32[8]{0:T(128)}, u32[]{:S(2)}) copy-start(s32[8]{0:T(128)} %param.18) | copy-start | bytes 100
  166.5 75.4 %copy-start.4 = (bf16[2,128,2048]{2,1,0:T(8,128)(2,1)S(1)}, bf16[2,128,2048]{2,1,0:T(8,128)(2,1)}, u32[]{:S(2)}) copy-start(bf16[2,128,2048]{2,1,0:T(8,128)(2,1)} %param.21) | copy-start | bytes 3145732
  256.9 130.5 %all-to-all-start.1 = ((bf16[8,128,2048]{2,1,0:T(8,128)(2,1)}), bf16[8,128,2048]{2,1,0:T(8,128)(2,1)}, u32[]{:S(2)}, u32[]{:S(2)}) async-start(bf16[8,128,2048]{2,1,0:T(8,128)(2,1)} %copy.44), calls=%async_computation.1 | async-start | bytes 8388608 | tf_op jit(solution)/shard_map/all_to_all | solution.py:79
  387.4 53.2 %all-to-all-start = ((bf16[8,2048,128]{2,1,0:T(8,128)(2,1)}), bf16[8,2048,128]{2,1,0:T(8,128)(2,1)}, u32[]{:S(2)}, u32[]{:S(2)}) async-start(bf16[8,2048,128]{2,1,0:T(8,128)(2,1)} %copy.43), calls=%async_computation | async-start | bytes 8388608 | tf_op jit(solution)/shard_map/all_to_all | solution.py:78
  393.1 51.2 %copy-start.1 = (bf16[1,2048,128]{2,1,0:T(8,128)(2,1)S(1)}, bf16[1,2048,128]{2,1,0:T(8,128)(2,1)}, u32[]{:S(2)}) copy-start(bf16[1,2048,128]{2,1,0:T(8,128)(2,1)} %param.14) | copy-start | bytes 1572868
Sparse Core Ops, SparseCore 0:
  9.9 76.4 all-gather.8
  88.3 72.1 all-gather.6
  166.3 75.5 all-gather.12
  244.9 116.3 all-gather.10
where the time goes:
time: 451 us
  waiting for transfers between devices  352 us (78%)
  matrix products  43.5 us (10%)
  local copies, waits for them, and re-layouts  24.1 us (5%)
  between operations  13.9 us (3%)
  starting transfers between devices  9.47 us (2%)
  other arithmetic  7.99 us (2%)
    all_gather x1, waiting for transfers between devices, on_device(): lax.all_gather(pseudo_up, 'region', axis=0, tiled=True)  99.6 us
    all_gather x1, waiting for transfers between devices, on_device(): lax.all_gather(acts, 'dev', axis=1, tiled=True)  77.7 us
    all_gather x1, waiting for transfers between devices, on_device(): lax.all_gather(cotan, 'dev', axis=1, tiled=True)  68.3 us
    all_gather x1, waiting for transfers between devices, on_device(): lax.all_gather(pseudo_down, 'region', axis=0, tiled=True)  62.5 us
    all_to_all x1, waiting for transfers between devices, on_device(): lax.all_to_all(reply_up, 'region', split_axis=0, concat_axis=0, tiled=True)  42.3 us
    dot_general x1, matrix products, on_device(): jnp.dot(inputs.T, dhidden, preferred_element_type=jnp.float32) * D ** (-0.5)  12.4 us
    unnamed x18, local copies, waits for them, and re-layouts  10 us
    dot_general x1, matrix products, on_device(): jnp.einsum('ko,kfd->ofd', chosen_b, pieces[1], preferred_element_type=jnp...  9.13 us
  transfers between devices with their start and end apart: 6, of which 5 were waited for; matrix products, arithmetic and copies ran while one was open for 15% of the time, Pallas kernels for 0%

commit v1 on v0

v1 whole, which is shorter than its diff:
```python
import functools
import math

import jax
import jax.numpy as jnp
from jax import lax
from jax.experimental import pallas as pl
from jax.experimental.pallas import tpu as pltpu
from jax.sharding import Mesh
from jax.sharding import PartitionSpec as P

D = 2048
FF = 4096
REGION = ("xh", "y")
DEV = ("z", "xl", "c")
NR = 8
BF = jnp.bfloat16
F32 = jnp.float32
MIB = 1 << 20


def params(mib=48):
    return pltpu.CompilerParams(vmem_limit_bytes=mib * MIB)


def whole(count):
    return [pl.BlockSpec(memory_space=pltpu.VMEM)] * count


def grads_kernel(n_blocks, first, *refs):
    blocks = refs[:n_blocks]
    up_ref, down_ref = refs[n_blocks : n_blocks + 2]
    outs = refs[-2:]
    olds = None if first else refs[n_blocks + 2 : n_blocks + 4]
    x = jnp.concatenate([b[0] for b in blocks], axis=0)
    g = jnp.concatenate([b[1] for b in blocks], axis=0)
    hid = jnp.dot(x, up_ref[...], preferred_element_type=F32) * D ** (-0.5)
    dact = lax.dot_general(
        g, down_ref[...], (((1,), (1,)), ((), ())), preferred_element_type=F32
    ) * FF ** (-0.5)
    root = math.sqrt(2.0 / math.pi)
    sq = hid * hid
    t = jnp.tanh(root * (hid + 0.044715 * (sq * hid)))
    act = (0.5 * hid * (1.0 + t)).astype(BF)
    slope = 0.5 * (1.0 + t) + 0.5 * hid * (1.0 - t * t) * (root * (1.0 + 3 * 0.044715 * sq))
    dhid = (dact * slope).astype(BF)
    gd = lax.dot_general(act, g, (((0,), (0,)), ((), ())), preferred_element_type=F32)
    gu = lax.dot_general(dhid, x, (((0,), (0,)), ((), ())), preferred_element_type=F32)
    if not first:
        gd = gd + olds[0][...]
        gu = gu + olds[1][...]
    outs[0][...] = gd
    outs[1][...] = gu


def grads_step(blocks, up2, down2, sums):
    n = len(blocks)
    first = sums is None
    tokens = sum(b.shape[1] for b in blocks)
    operands = list(blocks) + [up2, down2] + ([] if first else list(sums))
    shape = jax.ShapeDtypeStruct((256, D), F32)
    return pl.pallas_call(
        functools.partial(grads_kernel, n, first),
        out_shape=(shape, shape),
        in_specs=whole(len(operands)),
        out_specs=tuple(whole(2)),
        input_output_aliases={} if first else {n + 2: 0, n + 3: 1},
        compiler_params=params(),
        cost_estimate=pl.CostEstimate(
            flops=8 * tokens * D * 256, bytes_accessed=12 * MIB, transcendentals=tokens * 256
        ),
    )(*operands)


def part_kernel(gd_ref, gu_ref, out_ref):
    out_ref[0] = (gd_ref[128:256, :] * (0.5 * FF ** (-0.5))).astype(BF)
    out_ref[1] = (gu_ref[128:256, :] * (0.5 * D ** (-0.5))).astype(BF)


def part(sums):
    return pl.pallas_call(
        part_kernel,
        out_shape=jax.ShapeDtypeStruct((2, 128, D), BF),
        in_specs=whole(2),
        out_specs=pl.BlockSpec(memory_space=pltpu.VMEM),
        compiler_params=params(),
    )(*sums)


def down_in(eighth):
    return jnp.concatenate([eighth[:, j * 128 : (j + 1) * 128] for j in range(16)], axis=0)


def pseudo_kernel(gd_ref, gu_ref, got_ref, du_ref, dd_ref, out_ref):
    down = gd_ref[0:128, :] * (0.5 * FF ** (-0.5)) + got_ref[0].astype(F32)
    down = (down + dd_ref[0].astype(F32)).astype(BF)
    up = gu_ref[0:128, :] * (0.5 * D ** (-0.5)) + got_ref[1].astype(F32)
    for r in range(NR):
        mine = up[:, r * 256 : (r + 1) * 256].T + du_ref[0, r * 256 : (r + 1) * 256, :].astype(F32)
        out_ref[r, 0:256, :] = mine.astype(BF)
        out_ref[r, 256:512, :] = down_in(down[r * 16 : (r + 1) * 16, :])


def pseudo(sums, got, drift_up, drift_down):
    return pl.pallas_call(
        pseudo_kernel,
        out_shape=jax.ShapeDtypeStruct((NR, 512, 128), BF),
        in_specs=whole(5),
        out_specs=pl.BlockSpec(memory_space=pltpu.VMEM),
        compiler_params=params(),
    )(*sums, got, drift_up, drift_down)


def state_kernel(gu_ref, gd_ref, mu_ref, md_ref, out_ref):
    for s in range(2):
        out_ref[0, s, 0:256, :] = gu_ref[s].astype(F32) - 0.567 * mu_ref[s]
        out_ref[0, s, 256:512, :] = down_in(gd_ref[s].astype(F32) - 0.567 * md_ref[s])


def state(global_up, global_down, mom_up, mom_down):
    up = pl.BlockSpec((2, 256, 128), lambda i: (0, i, 0))
    down = pl.BlockSpec((2, 16, D), lambda i: (0, i, 0))
    return pl.pallas_call(
        state_kernel,
        grid=(NR,),
        out_shape=jax.ShapeDtypeStruct((NR, 2, 512, 128), F32),
        in_specs=[up, down, up, down],
        out_specs=pl.BlockSpec((1, 2, 512, 128), lambda i: (i, 0, 0, 0)),
        compiler_params=params(),
        cost_estimate=pl.CostEstimate(flops=4 * MIB, bytes_accessed=10 * MIB, transcendentals=0),
    )(global_up, global_down, mom_up, mom_down)


def step_kernel(target_ref, weight_ref, p_ref, a_ref, out_ref):
    for o in range(NR):
        for s in range(2):
            slot = 2 * o + s
            delta = weight_ref[0, slot] * p_ref[0].astype(F32)
            for r in range(1, NR):
                delta = delta + weight_ref[r, slot] * p_ref[r].astype(F32)
            out_ref[o, s] = (a_ref[o, s] - 1.33 * delta).astype(BF)
    for r in range(NR):
        at = target_ref[r]
        out_ref[r, 2] = out_ref[at // 2, at % 2]


def step(target, weight, pieces, base):
    rows = 128
    return pl.pallas_call(
        step_kernel,
        grid=(512 // rows,),
        out_shape=jax.ShapeDtypeStruct((NR, 3, 512, 128), BF),
        in_specs=[
            pl.BlockSpec(memory_space=pltpu.SMEM),
            pl.BlockSpec(memory_space=pltpu.SMEM),
            pl.BlockSpec((NR, rows, 128), lambda i: (0, i, 0)),
            pl.BlockSpec((NR, 2, rows, 128), lambda i: (0, 0, i, 0)),
        ],
        out_specs=pl.BlockSpec((NR, 3, rows, 128), lambda i: (0, 0, i, 0)),
        compiler_params=params(),
    )(target, weight, pieces, base)


def place_kernel(got_ref, nu_ref, nd_ref, ru_ref, rd_ref):
    def down_out(s):
        return jnp.concatenate(
            [got_ref[0, s, 256 + j * 16 : 272 + j * 16, :] for j in range(16)], axis=1
        )

    for s in range(2):
        nu_ref[s] = got_ref[0, s, 0:256, :]
        nd_ref[s] = down_out(s)
    ru_ref[0] = got_ref[0, 2, 0:256, :]
    rd_ref[0] = down_out(2)


def place(got):
    def up(n):
        return pl.BlockSpec((n, 256, 128), lambda i: (0, i, 0))

    def down(n):
        return pl.BlockSpec((n, 16, D), lambda i: (0, i, 0))

    return pl.pallas_call(
        place_kernel,
        grid=(NR,),
        out_shape=(
            jax.ShapeDtypeStruct((2, D, 128), BF),
            jax.ShapeDtypeStruct((2, 128, D), BF),
            jax.ShapeDtypeStruct((1, D, 128), BF),
            jax.ShapeDtypeStruct((1, 128, D), BF),
        ),
        in_specs=[pl.BlockSpec((1, 3, 512, 128), lambda i: (i, 0, 0, 0))],
        out_specs=(up(2), down(2), up(1), down(1)),
        compiler_params=params(),
    )(got)


RIGHT = [(i, (i + 1) % 8) for i in range(8)]
LEFT = [(i, (i + 7) % 8) for i in range(8)]
SWAP = [(0, 1), (1, 0)]


def on_device(
    acts,
    cotan,
    w_up,
    w_down,
    drift_up,
    drift_down,
    path,
    slot_of,
    global_up,
    global_down,
    mom_up,
    mom_down,
):
    module_ids = jnp.arange(slot_of.shape[0], dtype=jnp.int32)
    target = jnp.sum(jnp.where(path[:, None] == module_ids[None, :], slot_of[None, :], 0), axis=1)
    chosen = (target[:, None] == module_ids[None, :]).astype(F32)
    weight = chosen / jnp.maximum(jnp.sum(chosen, axis=0), 1.0)[None, :]

    base = state(global_up, global_down, mom_up, mom_down)
    base = lax.all_to_all(base, REGION, 0, 0, tiled=True)

    own = jnp.concatenate([acts, cotan], axis=0)
    other = lax.ppermute(own, "xl", SWAP)
    up2 = jnp.concatenate([w_up[0], lax.ppermute(w_up, "c", SWAP)[0]], axis=1)
    down2 = jnp.concatenate([w_down[0], lax.ppermute(w_down, "c", SWAP)[0]], axis=0)

    heads = [(own, own), (other, other)]
    sums = grads_step([own, other], up2, down2, None)
    for hop in range(4):
        blocks = []
        for k in range(2):
            right, left = heads[k]
            if hop == 3:
                right, left = right[:, :32], left[:, 32:]
            right = lax.ppermute(right, "z", RIGHT)
            left = lax.ppermute(left, "z", LEFT)
            heads[k] = (right, left)
            blocks += [right, left]
        sums = grads_step(blocks, up2, down2, sums)

    got = lax.ppermute(part(sums), "c", SWAP)
    pieces = pseudo(sums, got, drift_up, drift_down)
    pieces = lax.all_to_all(pieces, REGION, 0, 0, tiled=True)
    reply = step(target, weight, pieces, base)
    reply = lax.all_to_all(reply, REGION, 0, 0, tiled=True)
    return place(reply)


def solution(mesh):
    fine = Mesh(mesh.devices.reshape(2, 4, 8, 2, 2), REGION + DEV)
    rows = P(REGION, DEV, None)
    cols = P(REGION, None, DEV)
    return jax.shard_map(
        on_device,
        mesh=fine,
        in_specs=(rows, rows, cols, rows, cols, rows, P(), P(), cols, rows, cols, rows),
        out_specs=(cols, rows, cols, rows),
        check_vma=False,
    )
```

time: 451 us -> 252 us (0.56)
  waiting for transfers between devices: 352 us -> 98.6 us
  starting transfers between devices: 9.47 us -> 54 us
  matrix products: 43.5 us -> 0 us
  blocking collectives: 0 us -> 43.5 us
  Pallas kernels: 0 us -> 42.3 us
  between operations: 13.9 us -> 0.84 us
  local copies, waits for them, and re-layouts: 24.1 us -> 11.7 us
  other arithmetic: 7.99 us -> 0.54 us
    all_gather x4 -> x0, waiting for transfers between devices: 308 us -> none  [the longest x1 99.6 us: on_device(): lax.all_gather(pseudo_up, 'region', axis=0, tiled=True)]
    ppermute x0 -> x20, waiting for transfers between devices: none -> 84.4 us  [the longest x1 50.8 us: on_device(): other = lax.ppermute(own, 'xl', SWAP)]
    all_to_all x0 -> x1, blocking collectives: none -> 43.5 us  [on_device(): reply = lax.all_to_all(reply, REGION, 0, 0, tiled=True)]
    dot_general x7 -> x0, matrix products: 43.5 us -> none  [the longest x1 12.4 us: on_device(): jnp.dot(inputs.T, dhidden, preferred_element_type=jnp.float32) * D ** (-0.5)]
    pallas_call x0 -> x10, Pallas kernels: none -> 42.3 us  [the longest x5 23.9 us: grads_step(): pl.pallas_call(functools.partial(grads_kernel, n, first), out_shape=(shap...]
    ppermute x0 -> x20, starting transfers between devices: none -> 38.9 us  [the longest x8 24 us: on_device(): left = lax.ppermute(left, 'z', LEFT)]
    all_to_all x2, waiting for transfers between devices: 42.3 us -> 14.2 us  [the longest x1 14.2 us: on_device(): pieces = lax.all_to_all(pieces, REGION, 0, 0, tiled=True)]
    reduce_sum x3 -> x1, other arithmetic: 7.73 us -> 0.09 us  [on_device(): weight = chosen / jnp.maximum(jnp.sum(chosen, axis=0), 1.0)[None, :]]
  transfers between devices with their start and end apart: 6 -> 22, of which waited for: 5 -> 8; matrix products, arithmetic and copies ran while one was open for 15% -> 0% of each run, Pallas kernels for 0% -> 11%
where the time goes in v1:
time: 252 us; the launch traced here: 251 us
  waiting for transfers between devices  98.6 us (39%)
  starting transfers between devices  54 us (21%)
  blocking collectives  43.5 us (17%)
  Pallas kernels  42.3 us (17%)
  local copies, waits for them, and re-layouts  11.7 us (5%)
    ppermute x1, waiting for transfers between devices, on_device(): other = lax.ppermute(own, 'xl', SWAP)  50.8 us
    all_to_all x1, blocking collectives, on_device(): reply = lax.all_to_all(reply, REGION, 0, 0, tiled=True)  43.5 us
    ppermute x8, waiting for transfers between devices, on_device(): right = lax.ppermute(right, 'z', RIGHT)  31.3 us
    ppermute x8, starting transfers between devices, on_device(): left = lax.ppermute(left, 'z', LEFT)  24 us
    pallas_call x5, Pallas kernels, grads_step(): pl.pallas_call(functools.partial(grads_kernel, n, first), out_shape=(shap...  23.9 us
    all_to_all x1, waiting for transfers between devices, on_device(): pieces = lax.all_to_all(pieces, REGION, 0, 0, tiled=True)  14.2 us
    unnamed x33, local copies, waits for them, and re-layouts  11.6 us
    all_to_all x1, starting transfers between devices, on_device(): base = lax.all_to_all(base, REGION, 0, 0, tiled=True)  7.62 us
  transfers between devices with their start and end apart: 22, of which 8 were waited for; matrix products, arithmetic and copies ran while one was open for 0% of the time, Pallas kernels for 11%

profile of v1, /device:TPU:1, one launch (start us, length us, event | category | flops | bytes accessed | tf_op | source)
XLA Modules:
  0.0 251.4 jit_solution(2432625857125927195)
XLA Ops:
  0.6 1.6 copy-done.5
  2.2 1.2 copy-done.6
  3.5 1.2 copy-done.7
  4.7 6.2 %shard_map.154 = f32[8,2,512,128]{3,2,1,0:T(8,128)} custom-call(bf16[2,2048,128]{2,1,0:T(8,128)(2,1)S(1)} %copy-done.6, bf16[2,128,2048]{2,1,0:T(8,128)(2,1)S(1)} %copy-done.7, f32[2,2048,128]{2,1,0:T(8,128)S(1)} %copy-done.5, f32[2,128,2048]{2,1,0:T(8,128)} %md_ref.1), custom_call_target="tpu_custom_call" | custom-call | flops 4194304 | bytes 10485760 | tf_op jit(solution)/shard_map/pallas_call | solution.py:123
  10.9 7.6 %all-to-all-start.1 = ((f32[8,2,512,128]{3,2,1,0:T(8,128)}), f32[8,2,512,128]{3,2,1,0:T(8,128)}, u32[]{:S(2)}, u32[]{:S(2)}) async-start(f32[8,2,512,128]{3,2,1,0:T(8,128)} %shard_map.154), calls=%async_computation.1 | async-start | bytes 8388608 | tf_op jit(solution)/shard_map/all_to_all | solution.py:224
  18.6 0.4 collective-permute-start.8
  19.0 1.6 collective-permute-start
  20.6 3.9 %collective-permute-start.4 = (bf16[2,64,2048]{2,1,0:T(8,128)(2,1)S(1)}, bf16[2,64,2048]{2,1,0:T(8,128)(2,1)S(1)}, u32[]{:S(2)}, u32[]{:S(2)}) collective-permute-start(bf16[2,64,2048]{2,1,0:T(8,128)(2,1)S(1)} %constant_dynamic-update-slice_fusion.refs_0_), channel_id=1, source_target_pairs={{0,28},{4,0},{8,4},{12,8},{16,12},{20,16},{24,20},{28,24},{1,29},{... | collective-permute-start | bytes 1572872 | tf_op jit(solution)/shard_map/ppermute | solution.py:240
  24.6 50.8 %collective-permute-done.8.refs_1_ = bf16[2,64,2048]{2,1,0:T(8,128)(2,1)S(1)} collective-permute-done((bf16[2,64,2048]{2,1,0:T(8,128)(2,1)S(1)}, bf16[2,64,2048]{2,1,0:T(8,128)(2,1)S(1)}, u32[]{:S(2)}, u32[]{:S(2)}) %collective-permute-start.8) | collective-permute-done | bytes 524320 | tf_op jit(solution)/shard_map/ppermute | solution.py:227
  75.4 1.6 collective-permute-start.9
  77.0 3.9 %collective-permute-start.13 = (bf16[2,64,2048]{2,1,0:T(8,128)(2,1)S(1)}, bf16[2,64,2048]{2,1,0:T(8,128)(2,1)S(1)}, u32[]{:S(2)}, u32[]{:S(2)}) collective-permute-start(bf16[2,64,2048]{2,1,0:T(8,128)(2,1)S(1)} %collective-permute-done.8.refs_1_), channel_id=1, source_target_pairs={{0,28},{4,0},{8,4},{12,8},{16,12},{20,16},{24,20},{28,24},{1,29},{... | collective-permute-start | bytes 1572872 | tf_op jit(solution)/shard_map/ppermute | solution.py:240
  80.9 1.8 collective-permute-start.17
  82.8 0.0 collective-permute-done.refs_0_
  82.8 0.0 collective-permute-start.1
  82.8 0.0 collective-permute-done.4.refs_1_
  82.8 2.7 %collective-permute-start.5 = (bf16[2,64,2048]{2,1,0:T(8,128)(2,1)S(1)}, bf16[2,64,2048]{2,1,0:T(8,128)(2,1)S(1)}, u32[]{:S(2)}, u32[]{:S(2)}) collective-permute-start(bf16[2,64,2048]{2,1,0:T(8,128)(2,1)S(1)} %collective-permute-done.4.refs_1_), channel_id=1, source_target_pairs={{0,28},{4,0},{8,4},{12,8},{16,12},{20,16},{24,20},{28,24},{1,29},{... | collective-permute-start | bytes 1572872 | tf_op jit(solution)/shard_map/ppermute | solution.py:240
  85.5 6.2 %collective-permute-done.9.refs_2_ = bf16[2,64,2048]{2,1,0:T(8,128)(2,1)S(1)} collective-permute-done((bf16[2,64,2048]{2,1,0:T(8,128)(2,1)S(1)}, bf16[2,64,2048]{2,1,0:T(8,128)(2,1)S(1)}, u32[]{:S(2)}, u32[]{:S(2)}) %collective-permute-start.9) | collective-permute-done | bytes 524320 | tf_op jit(solution)/shard_map/ppermute | solution.py:239
  91.6 0.0 collective-permute-start.10
  91.6 0.0 collective-permute-done.13.refs_3_
  91.6 2.7 %collective-permute-start.14 = (bf16[2,64,2048]{2,1,0:T(8,128)(2,1)S(1)}, bf16[2,64,2048]{2,1,0:T(8,128)(2,1)S(1)}, u32[]{:S(2)}, u32[]{:S(2)}) collective-permute-start(bf16[2,64,2048]{2,1,0:T(8,128)(2,1)S(1)} %collective-permute-done.13.refs_3_), channel_id=1, source_target_pairs={{0,28},{4,0},{8,4},{12,8},{16,12},{20,16},{24,20},{28,24},{1,29},{... | collective-permute-start | bytes 1572872 | tf_op jit(solution)/shard_map/ppermute | solution.py:240
  94.3 0.0 collective-permute-done.17
  94.3 4.5 %collective-permute-start.18 = (bf16[1,128,2048]{2,1,0:T(8,128)(2,1)S(1)}, bf16[1,128,2048]{2,1,0:T(8,128)(2,1)S(1)}, u32[]{:S(2)}, u32[]{:S(2)}) collective-permute-start(bf16[1,128,2048]{2,1,0:T(8,128)(2,1)S(1)} %copy-done.11), channel_id=1, source_target_pairs={{0,1},{1,0},{2,3},{3,2},{4,5},{5,4},{6,7},{7,6},{8,9},{9,8},{10,11... | collective-permute-start | bytes 1572872 | tf_op jit(solution)/shard_map/ppermute | solution.py:229
  98.8 4.0 %collective-permute-done.1.refs_0_ = bf16[2,64,2048]{2,1,0:T(8,128)(2,1)S(1)} collective-permute-done((bf16[2,64,2048]{2,1,0:T(8,128)(2,1)S(1)}, bf16[2,64,2048]{2,1,0:T(8,128)(2,1)S(1)}, u32[]{:S(2)}, u32[]{:S(2)}) %collective-permute-start.1) | collective-permute-done | bytes 524320 | tf_op jit(solution)/shard_map/ppermute | solution.py:239
  102.9 0.0 collective-permute-start.2
  102.9 0.0 collective-permute-done.5.refs_1_
  102.9 2.7 %collective-permute-start.6 = (bf16[2,64,2048]{2,1,0:T(8,128)(2,1)S(1)}, bf16[2,64,2048]{2,1,0:T(8,128)(2,1)S(1)}, u32[]{:S(2)}, u32[]{:S(2)}) collective-permute-start(bf16[2,64,2048]{2,1,0:T(8,128)(2,1)S(1)} %collective-permute-done.5.refs_1_), channel_id=1, source_target_pairs={{0,28},{4,0},{8,4},{12,8},{16,12},{20,16},{24,20},{28,24},{1,29},{... | collective-permute-start | bytes 1572872 | tf_op jit(solution)/shard_map/ppermute | solution.py:240
  105.5 8.6 %collective-permute-done.10.refs_2_ = bf16[2,64,2048]{2,1,0:T(8,128)(2,1)S(1)} collective-permute-done((bf16[2,64,2048]{2,1,0:T(8,128)(2,1)S(1)}, bf16[2,64,2048]{2,1,0:T(8,128)(2,1)S(1)}, u32[]{:S(2)}, u32[]{:S(2)}) %collective-permute-start.10) | collective-permute-done | bytes 524320 | tf_op jit(solution)/shard_map/ppermute | solution.py:239
  114.1 0.0 collective-permute-start.11
  114.1 0.0 collective-permute-done.14.refs_3_
  114.1 2.7 %collective-permute-start.15 = (bf16[2,64,2048]{2,1,0:T(8,128)(2,1)S(1)}, bf16[2,64,2048]{2,1,0:T(8,128)(2,1)S(1)}, u32[]{:S(2)}, u32[]{:S(2)}) collective-permute-start(bf16[2,64,2048]{2,1,0:T(8,128)(2,1)S(1)} %collective-permute-done.14.refs_3_), channel_id=1, source_target_pairs={{0,28},{4,0},{8,4},{12,8},{16,12},{20,16},{24,20},{28,24},{1,29},{... | collective-permute-start | bytes 1572872 | tf_op jit(solution)/shard_map/ppermute | solution.py:240
  116.8 0.1 pad_maximum_fusion.refs_2_.refs_4_
  116.9 0.0 collective-permute-done.18
  116.9 0.1 pad_maximum_fusion.1.refs_3_.refs_5_
  117.0 2.7 %shard_map.147 = (f32[256,2048]{1,0:T(8,128)S(1)}, f32[256,2048]{1,0:T(8,128)}) custom-call(bf16[2,64,2048]{2,1,0:T(8,128)(2,1)S(1)} %constant_dynamic-update-slice_fusion.refs_0_, bf16[2,64,2048]{2,1,0:T(8,128)(2,1)S(1)} %collective-permute-done.8.refs_1_, bf16[2048,256]{1,0:T(8,128)(2,1)S(1)} %pad_maximum_fusion.refs_2_.refs_4_, ...), custom_call_target="tpu_custom_call" | custom-call | flops 536870912 | bytes 12582912 | tf_op jit(solution)/shard_map/pallas_call | solution.py:62
  119.7 1.4 copy-done
  121.1 4.2 %collective-permute-done.2.refs_0_ = bf16[2,64,2048]{2,1,0:T(8,128)(2,1)S(1)} collective-permute-done((bf16[2,64,2048]{2,1,0:T(8,128)(2,1)S(1)}, bf16[2,64,2048]{2,1,0:T(8,128)(2,1)S(1)}, u32[]{:S(2)}, u32[]{:S(2)}) %collective-permute-start.2) | collective-permute-done | bytes 524320 | tf_op jit(solution)/shard_map/ppermute | solution.py:239
  125.3 0.1 collective-permute-start.3
  125.4 0.0 collective-permute-done.6.refs_1_
  125.5 2.7 %collective-permute-start.7 = (bf16[2,32,2048]{2,1,0:T(8,128)(2,1)S(1)}, bf16[2,32,2048]{2,1,0:T(8,128)(2,1)S(1)}, u32[]{:S(2)}, u32[]{:S(2)}) collective-permute-start(bf16[2,32,2048]{2,1,0:T(8,128)(2,1)S(1)} %slice.17), channel_id=1, source_target_pairs={{0,28},{4,0},{8,4},{12,8},{16,12},{20,16},{24,20},{28,24},{1,29},{... | collective-permute-start | bytes 786440 | tf_op jit(solution)/shard_map/ppermute | solution.py:240
  128.2 8.4 %collective-permute-done.11.refs_2_ = bf16[2,64,2048]{2,1,0:T(8,128)(2,1)S(1)} collective-permute-done((bf16[2,64,2048]{2,1,0:T(8,128)(2,1)S(1)}, bf16[2,64,2048]{2,1,0:T(8,128)(2,1)S(1)}, u32[]{:S(2)}, u32[]{:S(2)}) %collective-permute-start.11) | collective-permute-done | bytes 524320 | tf_op jit(solution)/shard_map/ppermute | solution.py:239
  136.6 0.1 collective-permute-start.12
  136.7 2.7 %collective-permute-start.16 = (bf16[2,32,2048]{2,1,0:T(8,128)(2,1)S(1)}, bf16[2,32,2048]{2,1,0:T(8,128)(2,1)S(1)}, u32[]{:S(2)}, u32[]{:S(2)}) collective-permute-start(bf16[2,32,2048]{2,1,0:T(8,128)(2,1)S(1)} %slice.19), channel_id=1, source_target_pairs={{0,28},{4,0},{8,4},{12,8},{16,12},{20,16},{24,20},{28,24},{1,29},{... | collective-permute-start | bytes 786440 | tf_op jit(solution)/shard_map/ppermute | solution.py:240
  139.4 5.5 %shard_map.148 = (f32[256,2048]{1,0:T(8,128)}, f32[256,2048]{1,0:T(8,128)}) custom-call(bf16[2,64,2048]{2,1,0:T(8,128)(2,1)S(1)} %collective-permute-done.refs_0_, bf16[2,64,2048]{2,1,0:T(8,128)(2,1)S(1)} %collective-permute-done.4.refs_1_, bf16[2,64,2048]{2,1,0:T(8,128)(2,1)S(1)} %collective-permute-done.9.refs_2_, ...), custom_call_target="tpu_custom_call", output_to_operand_aliasing={{0}: (6, {}), {1}: (7, {})} | custom-call | flops 1073741824 | bytes 12582912 | tf_op jit(solution)/shard_map/pallas_call | solution.py:62
  145.0 5.5 %shard_map.149 = (f32[256,2048]{1,0:T(8,128)}, f32[256,2048]{1,0:T(8,128)}) custom-call(bf16[2,64,2048]{2,1,0:T(8,128)(2,1)S(1)} %collective-permute-done.1.refs_0_, bf16[2,64,2048]{2,1,0:T(8,128)(2,1)S(1)} %collective-permute-done.5.refs_1_, bf16[2,64,2048]{2,1,0:T(8,128)(2,1)S(1)} %collective-permute-done.10.refs_2_, ...), custom_call_target="tpu_custom_call", output_to_operand_aliasing={{0}: (6, {}), {1}: (7, {})} | custom-call | flops 1073741824 | bytes 12582912 | tf_op jit(solution)/shard_map/pallas_call | solution.py:62
  150.5 5.5 %shard_map.150 = (f32[256,2048]{1,0:T(8,128)}, f32[256,2048]{1,0:T(8,128)}) custom-call(bf16[2,64,2048]{2,1,0:T(8,128)(2,1)S(1)} %collective-permute-done.2.refs_0_, bf16[2,64,2048]{2,1,0:T(8,128)(2,1)S(1)} %collective-permute-done.6.refs_1_, bf16[2,64,2048]{2,1,0:T(8,128)(2,1)S(1)} %collective-permute-done.11.refs_2_, ...), custom_call_target="tpu_custom_call", output_to_operand_aliasing={{0}: (6, {}), {1}: (7, {})} | custom-call | flops 1073741824 | bytes 12582912 | tf_op jit(solution)/shard_map/pallas_call | solution.py:62
  156.0 0.0 collective-permute-done.7.refs_1_
  156.0 0.0 collective-permute-done.12.refs_2_
  156.1 1.6 copy-done.1
  157.6 4.6 %shard_map.151 = (f32[256,2048]{1,0:T(8,128)S(1)}, f32[256,2048]{1,0:T(8,128)}) custom-call(bf16[2,32,2048]{2,1,0:T(8,128)(2,1)S(1)} %collective-permute-done.3.refs_0_, bf16[2,32,2048]{2,1,0:T(8,128)(2,1)S(1)} %collective-permute-done.7.refs_1_, ...), custom_call_target="tpu_custom_call", output_to_operand_aliasing={{0}: (6, {}), {1}: (7, {})} | custom-call | flops 536870912 | bytes 12582912 | tf_op jit(solution)/shard_map/pallas_call | solution.py:62
  162.2 1.4 copy-done.2
  163.6 1.6 copy-done.3
  165.2 1.6 copy-done.4
  166.8 0.1 shard_map.152
  166.9 4.6 %collective-permute-start.19 = (bf16[2,128,2048]{2,1,0:T(8,128)(2,1)S(1)}, bf16[2,128,2048]{2,1,0:T(8,128)(2,1)S(1)}, u32[]{:S(2)}, u32[]{:S(2)}) collective-permute-start(bf16[2,128,2048]{2,1,0:T(8,128)(2,1)S(1)} %shard_map.152), channel_id=1, source_target_pairs={{0,1},{1,0},{2,3},{3,2},{4,5},{5,4},{6,7},{7,6},{8,9},{9,8},{10,11... | collective-permute-start | bytes 3145736 | tf_op jit(solution)/shard_map/ppermute | solution.py:245
  171.6 2.3 collective-permute-done.19.got_ref
  173.9 3.2 %shard_map.153 = bf16[8,512,128]{2,1,0:T(8,128)(2,1)} custom-call(f32[256,2048]{1,0:T(8,128)S(1)} %copy-done.3, f32[256,2048]{1,0:T(8,128)} %get-tuple-element.23.gu_ref, bf16[2,128,2048]{2,1,0:T(8,128)(2,1)S(1)} %collective-permute-done.19.got_ref, bf16[1,2048,128]{2,1,0:T(8,128)(2,1)S(1)} %copy-done.8, bf16[1,128,2048]{2,1,0:T(8,128)(2,1)S(1)} %copy-done.9), custom_call_target="tpu_custom_call" | custom-call | tf_op jit(solution)/shard_map/pallas_call | solution.py:105
  177.1 7.4 %all-to-all-start = ((bf16[8,512,128]{2,1,0:T(8,128)(2,1)}), bf16[8,512,128]{2,1,0:T(8,128)(2,1)S(1)}, u32[]{:S(2)}, u32[]{:S(2)}) async-start(bf16[8,512,128]{2,1,0:T(8,128)(2,1)} %shard_map.153), calls=%async_computation | async-start | bytes 2097152 | tf_op jit(solution)/shard_map/all_to_all | solution.py:247
  184.5 0.2 select_reduce_fusion.target_ref
  184.7 0.1 convert_reduce_fusion
  184.8 0.1 convert_divide_fusion.weight_ref
  184.9 14.2 %all-to-all-done.p_ref = bf16[8,512,128]{2,1,0:T(8,128)(2,1)S(1)} async-done(((bf16[8,512,128]{2,1,0:T(8,128)(2,1)}), bf16[8,512,128]{2,1,0:T(8,128)(2,1)S(1)}, u32[]{:S(2)}, u32[]{:S(2)}) %all-to-all-start) | async-done | bytes 1048608 | tf_op jit(solution)/shard_map/all_to_all | solution.py:247
  199.1 5.6 %shard_map.155 = bf16[8,3,512,128]{3,2,1,0:T(8,128)(2,1)S(1)} custom-call(s32[8]{0:T(128)S(1)} %select_reduce_fusion.target_ref, f32[8,16]{1,0:T(8,128)S(1)} %convert_divide_fusion.weight_ref, bf16[8,512,128]{2,1,0:T(8,128)(2,1)S(1)} %all-to-all-done.p_ref, f32[8,2,512,128]{3,2,1,0:T(8,128)} %all-to-all-done.1.a_ref), custom_call_target="tpu_custom_call" | custom-call | tf_op jit(solution)/shard_map/pallas_call | solution.py:149
  204.7 43.5 %all_to_all.15.got_ref = bf16[8,3,512,128]{3,2,1,0:T(8,128)(2,1)S(1)} all-to-all(bf16[8,3,512,128]{3,2,1,0:T(8,128)(2,1)S(1)} %shard_map.155), channel_id=1, replica_groups=mesh['xh'=2,'y'=4,'z'=8,'xl'=2,'c'=2] {'xh','y'}, dimensions={0} | all-to-all | bytes 6291456 | tf_op jit(solution)/shard_map/all_to_all | solution.py:249
  248.2 3.2 %shard_map.156 = (bf16[2,2048,128]{2,1,0:T(8,128)(2,1)}, bf16[2,128,2048]{2,1,0:T(8,128)(2,1)}, bf16[1,2048,128]{2,1,0:T(8,128)(2,1)}, bf16[1,128,2048]{2,1,0:T(8,128)(2,1)}) custom-call(bf16[8,3,512,128]{3,2,1,0:T(8,128)(2,1)S(1)} %all_to_all.15.got_ref), custom_call_target="tpu_custom_call" | custom-call | tf_op jit(solution)/shard_map/pallas_call | solution.py:184
  (35 shorter events, 0.2 us)
Async XLA Ops:
  0.6 1.6 copy-start.5
  2.2 1.2 copy-start.6
  3.4 1.2 copy-start.7
  10.9 7.6 %copy-start.12 = (bf16[1,64,2048]{2,1,0:T(8,128)(2,1)S(1)}, bf16[1,64,2048]{2,1,0:T(8,128)(2,1)}, u32[]{:S(2)}) copy-start(bf16[1,64,2048]{2,1,0:T(8,128)(2,1)} %param.12) | copy-start | bytes 786436
  10.9 7.7 %copy-start.13 = (bf16[1,64,2048]{2,1,0:T(8,128)(2,1)S(1)}, bf16[1,64,2048]{2,1,0:T(8,128)(2,1)}, u32[]{:S(2)}) copy-start(bf16[1,64,2048]{2,1,0:T(8,128)(2,1)} %param.13) | copy-start | bytes 786436
  10.9 70.0 %copy-start.10 = (bf16[1,2048,128]{2,1,0:T(8,128)(2,1)S(1)}, bf16[1,2048,128]{2,1,0:T(8,128)(2,1)}, u32[]{:S(2)}) copy-start(bf16[1,2048,128]{2,1,0:T(8,128)(2,1)} %param.14) | copy-start | bytes 1572868
  10.9 83.4 %copy-start.11 = (bf16[1,128,2048]{2,1,0:T(8,128)(2,1)S(1)}, bf16[1,128,2048]{2,1,0:T(8,128)(2,1)}, u32[]{:S(2)}) copy-start(bf16[1,128,2048]{2,1,0:T(8,128)(2,1)} %param.15) | copy-start | bytes 1572868
  10.9 166.2 %all-to-all-start.1 = ((f32[8,2,512,128]{3,2,1,0:T(8,128)}), f32[8,2,512,128]{3,2,1,0:T(8,128)}, u32[]{:S(2)}, u32[]{:S(2)}) async-start(f32[8,2,512,128]{3,2,1,0:T(8,128)} %shard_map.154), calls=%async_computation.1 | async-start | bytes 8388608 | tf_op jit(solution)/shard_map/all_to_all | solution.py:224
  18.6 56.7 %collective-permute-start.8 = (bf16[2,64,2048]{2,1,0:T(8,128)(2,1)S(1)}, bf16[2,64,2048]{2,1,0:T(8,128)(2,1)S(1)}, u32[]{:S(2)}, u32[]{:S(2)}) collective-permute-start(bf16[2,64,2048]{2,1,0:T(8,128)(2,1)S(1)} %constant_dynamic-update-slice_fusion.refs_0_), channel_id=1, source_target_pairs={{0,2},{2,0},{1,3},{3,1},{4,6},{6,4},{5,7},{7,5},{8,10},{10,8},{9,1... | collective-permute-start | bytes 1572872 | tf_op jit(solution)/shard_map/ppermute | solution.py:227
  19.0 63.8 %collective-permute-start = (bf16[2,64,2048]{2,1,0:T(8,128)(2,1)S(1)}, bf16[2,64,2048]{2,1,0:T(8,128)(2,1)S(1)}, u32[]{:S(2)}, u32[]{:S(2)}) collective-permute-start(bf16[2,64,2048]{2,1,0:T(8,128)(2,1)S(1)} %constant_dynamic-update-slice_fusion.refs_0_), channel_id=1, source_target_pairs={{0,4},{4,8},{8,12},{12,16},{16,20},{20,24},{24,28},{28,0},{1,5},{5... | collective-permute-start | bytes 1572872 | tf_op jit(solution)/shard_map/ppermute | solution.py:239
  20.6 62.1 %collective-permute-start.4 = (bf16[2,64,2048]{2,1,0:T(8,128)(2,1)S(1)}, bf16[2,64,2048]{2,1,0:T(8,128)(2,1)S(1)}, u32[]{:S(2)}, u32[]{:S(2)}) collective-permute-start(bf16[2,64,2048]{2,1,0:T(8,128)(2,1)S(1)} %constant_dynamic-update-slice_fusion.refs_0_), channel_id=1, source_target_pairs={{0,28},{4,0},{8,4},{12,8},{16,12},{20,16},{24,20},{28,24},{1,29},{... | collective-permute-start | bytes 1572872 | tf_op jit(solution)/shard_map/ppermute | solution.py:240
  75.4 16.3 %collective-permute-start.9 = (bf16[2,64,2048]{2,1,0:T(8,128)(2,1)S(1)}, bf16[2,64,2048]{2,1,0:T(8,128)(2,1)S(1)}, u32[]{:S(2)}, u32[]{:S(2)}) collective-permute-start(bf16[2,64,2048]{2,1,0:T(8,128)(2,1)S(1)} %collective-permute-done.8.refs_1_), channel_id=1, source_target_pairs={{0,4},{4,8},{8,12},{12,16},{16,20},{20,24},{24,28},{28,0},{1,5},{5... | collective-permute-start | bytes 1572872 | tf_op jit(solution)/shard_map/ppermute | solution.py:239
  77.0 14.6 %collective-permute-start.13 = (bf16[2,64,2048]{2,1,0:T(8,128)(2,1)S(1)}, bf16[2,64,2048]{2,1,0:T(8,128)(2,1)S(1)}, u32[]{:S(2)}, u32[]{:S(2)}) collective-permute-start(bf16[2,64,2048]{2,1,0:T(8,128)(2,1)S(1)} %collective-permute-done.8.refs_1_), channel_id=1, source_target_pairs={{0,28},{4,0},{8,4},{12,8},{16,12},{20,16},{24,20},{28,24},{1,29},{... | collective-permute-start | bytes 1572872 | tf_op jit(solution)/shard_map/ppermute | solution.py:240
  80.9 13.4 %collective-permute-start.17 = (bf16[1,2048,128]{2,1,0:T(8,128)(2,1)S(1)}, bf16[1,2048,128]{2,1,0:T(8,128)(2,1)S(1)}, u32[]{:S(2)}, u32[]{:S(2)}) collective-permute-start(bf16[1,2048,128]{2,1,0:T(8,128)(2,1)S(1)} %copy-done.10), channel_id=1, source_target_pairs={{0,1},{1,0},{2,3},{3,2},{4,5},{5,4},{6,7},{7,6},{8,9},{9,8},{10,11... | collective-permute-start | bytes 1572872 | tf_op jit(solution)/shard_map/ppermute | solution.py:228
  82.8 20.1 %collective-permute-start.1 = (bf16[2,64,2048]{2,1,0:T(8,128)(2,1)S(1)}, bf16[2,64,2048]{2,1,0:T(8,128)(2,1)S(1)}, u32[]{:S(2)}, u32[]{:S(2)}) collective-permute-start(bf16[2,64,2048]{2,1,0:T(8,128)(2,1)S(1)} %collective-permute-done.refs_0_), channel_id=1, source_target_pairs={{0,4},{4,8},{8,12},{12,16},{16,20},{20,24},{24,28},{28,0},{1,5},{5... | collective-permute-start | bytes 1572872 | tf_op jit(solution)/shard_map/ppermute | solution.py:239
  82.8 20.1 %collective-permute-start.5 = (bf16[2,64,2048]{2,1,0:T(8,128)(2,1)S(1)}, bf16[2,64,2048]{2,1,0:T(8,128)(2,1)S(1)}, u32[]{:S(2)}, u32[]{:S(2)}) collective-permute-start(bf16[2,64,2048]{2,1,0:T(8,128)(2,1)S(1)} %collective-permute-done.4.refs_1_), channel_id=1, source_target_pairs={{0,28},{4,0},{8,4},{12,8},{16,12},{20,16},{24,20},{28,24},{1,29},{... | collective-permute-start | bytes 1572872 | tf_op jit(solution)/shard_map/ppermute | solution.py:240
  91.6 22.5 %collective-permute-start.10 = (bf16[2,64,2048]{2,1,0:T(8,128)(2,1)S(1)}, bf16[2,64,2048]{2,1,0:T(8,128)(2,1)S(1)}, u32[]{:S(2)}, u32[]{:S(2)}) collective-permute-start(bf16[2,64,2048]{2,1,0:T(8,128)(2,1)S(1)} %collective-permute-done.9.refs_2_), channel_id=1, source_target_pairs={{0,4},{4,8},{8,12},{12,16},{16,20},{20,24},{24,28},{28,0},{1,5},{5... | collective-permute-start | bytes 1572872 | tf_op jit(solution)/shard_map/ppermute | solution.py:239
  91.6 22.5 %collective-permute-start.14 = (bf16[2,64,2048]{2,1,0:T(8,128)(2,1)S(1)}, bf16[2,64,2048]{2,1,0:T(8,128)(2,1)S(1)}, u32[]{:S(2)}, u32[]{:S(2)}) collective-permute-start(bf16[2,64,2048]{2,1,0:T(8,128)(2,1)S(1)} %collective-permute-done.13.refs_3_), channel_id=1, source_target_pairs={{0,28},{4,0},{8,4},{12,8},{16,12},{20,16},{24,20},{28,24},{1,29},{... | collective-permute-start | bytes 1572872 | tf_op jit(solution)/shard_map/ppermute | solution.py:240
  94.3 22.6 %collective-permute-start.18 = (bf16[1,128,2048]{2,1,0:T(8,128)(2,1)S(1)}, bf16[1,128,2048]{2,1,0:T(8,128)(2,1)S(1)}, u32[]{:S(2)}, u32[]{:S(2)}) collective-permute-start(bf16[1,128,2048]{2,1,0:T(8,128)(2,1)S(1)} %copy-done.11), channel_id=1, source_target_pairs={{0,1},{1,0},{2,3},{3,2},{4,5},{5,4},{6,7},{7,6},{8,9},{9,8},{10,11... | collective-permute-start | bytes 1572872 | tf_op jit(solution)/shard_map/ppermute | solution.py:229
  102.9 22.5 %collective-permute-start.2 = (bf16[2,64,2048]{2,1,0:T(8,128)(2,1)S(1)}, bf16[2,64,2048]{2,1,0:T(8,128)(2,1)S(1)}, u32[]{:S(2)}, u32[]{:S(2)}) collective-permute-start(bf16[2,64,2048]{2,1,0:T(8,128)(2,1)S(1)} %collective-permute-done.1.refs_0_), channel_id=1, source_target_pairs={{0,4},{4,8},{8,12},{12,16},{16,20},{20,24},{24,28},{28,0},{1,5},{5... | collective-permute-start | bytes 1572872 | tf_op jit(solution)/shard_map/ppermute | solution.py:239
  102.9 22.6 %collective-permute-start.6 = (bf16[2,64,2048]{2,1,0:T(8,128)(2,1)S(1)}, bf16[2,64,2048]{2,1,0:T(8,128)(2,1)S(1)}, u32[]{:S(2)}, u32[]{:S(2)}) collective-permute-start(bf16[2,64,2048]{2,1,0:T(8,128)(2,1)S(1)} %collective-permute-done.5.refs_1_), channel_id=1, source_target_pairs={{0,28},{4,0},{8,4},{12,8},{16,12},{20,16},{24,20},{28,24},{1,29},{... | collective-permute-start | bytes 1572872 | tf_op jit(solution)/shard_map/ppermute | solution.py:240
  114.1 22.5 %collective-permute-start.11 = (bf16[2,64,2048]{2,1,0:T(8,128)(2,1)S(1)}, bf16[2,64,2048]{2,1,0:T(8,128)(2,1)S(1)}, u32[]{:S(2)}, u32[]{:S(2)}) collective-permute-start(bf16[2,64,2048]{2,1,0:T(8,128)(2,1)S(1)} %collective-permute-done.10.refs_2_), channel_id=1, source_target_pairs={{0,4},{4,8},{8,12},{12,16},{16,20},{20,24},{24,28},{28,0},{1,5},{5... | collective-permute-start | bytes 1572872 | tf_op jit(solution)/shard_map/ppermute | solution.py:239
  114.1 22.6 %collective-permute-start.15 = (bf16[2,64,2048]{2,1,0:T(8,128)(2,1)S(1)}, bf16[2,64,2048]{2,1,0:T(8,128)(2,1)S(1)}, u32[]{:S(2)}, u32[]{:S(2)}) collective-permute-start(bf16[2,64,2048]{2,1,0:T(8,128)(2,1)S(1)} %collective-permute-done.14.refs_3_), channel_id=1, source_target_pairs={{0,28},{4,0},{8,4},{12,8},{16,12},{20,16},{24,20},{28,24},{1,29},{... | collective-permute-start | bytes 1572872 | tf_op jit(solution)/shard_map/ppermute | solution.py:240
  119.7 1.4 copy-start
  125.3 30.7 %collective-permute-start.3 = (bf16[2,32,2048]{2,1,0:T(8,128)(2,1)S(1)}, bf16[2,32,2048]{2,1,0:T(8,128)(2,1)S(1)}, u32[]{:S(2)}, u32[]{:S(2)}) collective-permute-start(bf16[2,32,2048]{2,1,0:T(8,128)(2,1)S(1)} %slice.16), channel_id=1, source_target_pairs={{0,4},{4,8},{8,12},{12,16},{16,20},{20,24},{24,28},{28,0},{1,5},{5... | collective-permute-start | bytes 786440 | tf_op jit(solution)/shard_map/ppermute | solution.py:239
  125.5 30.6 %collective-permute-start.7 = (bf16[2,32,2048]{2,1,0:T(8,128)(2,1)S(1)}, bf16[2,32,2048]{2,1,0:T(8,128)(2,1)S(1)}, u32[]{:S(2)}, u32[]{:S(2)}) collective-permute-start(bf16[2,32,2048]{2,1,0:T(8,128)(2,1)S(1)} %slice.17), channel_id=1, source_target_pairs={{0,28},{4,0},{8,4},{12,8},{16,12},{20,16},{24,20},{28,24},{1,29},{... | collective-permute-start | bytes 786440 | tf_op jit(solution)/shard_map/ppermute | solution.py:240
  136.6 19.5 %collective-permute-start.12 = (bf16[2,32,2048]{2,1,0:T(8,128)(2,1)S(1)}, bf16[2,32,2048]{2,1,0:T(8,128)(2,1)S(1)}, u32[]{:S(2)}, u32[]{:S(2)}) collective-permute-start(bf16[2,32,2048]{2,1,0:T(8,128)(2,1)S(1)} %slice.18), channel_id=1, source_target_pairs={{0,4},{4,8},{8,12},{12,16},{16,20},{20,24},{24,28},{28,0},{1,5},{5... | collective-permute-start | bytes 786440 | tf_op jit(solution)/shard_map/ppermute | solution.py:239
  136.7 19.3 %collective-permute-start.16 = (bf16[2,32,2048]{2,1,0:T(8,128)(2,1)S(1)}, bf16[2,32,2048]{2,1,0:T(8,128)(2,1)S(1)}, u32[]{:S(2)}, u32[]{:S(2)}) collective-permute-start(bf16[2,32,2048]{2,1,0:T(8,128)(2,1)S(1)} %slice.19), channel_id=1, source_target_pairs={{0,28},{4,0},{8,4},{12,8},{16,12},{20,16},{24,20},{28,24},{1,29},{... | collective-permute-start | bytes 786440 | tf_op jit(solution)/shard_map/ppermute | solution.py:240
  156.1 1.6 copy-start.1
  162.2 1.4 copy-start.2
  163.6 1.6 copy-start.3
  165.2 1.6 copy-start.4
  166.8 7.1 %copy-start.8 = (bf16[1,2048,128]{2,1,0:T(8,128)(2,1)S(1)}, bf16[1,2048,128]{2,1,0:T(8,128)(2,1)}, u32[]{:S(2)}) copy-start(bf16[1,2048,128]{2,1,0:T(8,128)(2,1)} %du_ref.1) | copy-start | bytes 1572868
  166.8 7.1 %copy-start.9 = (bf16[1,128,2048]{2,1,0:T(8,128)(2,1)S(1)}, bf16[1,128,2048]{2,1,0:T(8,128)(2,1)}, u32[]{:S(2)}) copy-start(bf16[1,128,2048]{2,1,0:T(8,128)(2,1)} %dd_ref.1) | copy-start | bytes 1572868
  166.9 6.9 %collective-permute-start.19 = (bf16[2,128,2048]{2,1,0:T(8,128)(2,1)S(1)}, bf16[2,128,2048]{2,1,0:T(8,128)(2,1)S(1)}, u32[]{:S(2)}, u32[]{:S(2)}) collective-permute-start(bf16[2,128,2048]{2,1,0:T(8,128)(2,1)S(1)} %shard_map.152), channel_id=1, source_target_pairs={{0,1},{1,0},{2,3},{3,2},{4,5},{5,4},{6,7},{7,6},{8,9},{9,8},{10,11... | collective-permute-start | bytes 3145736 | tf_op jit(solution)/shard_map/ppermute | solution.py:245
  177.1 7.5 %copy-start.14 = (s32[16]{0:T(128)S(1)}, s32[16]{0:T(128)}, u32[]{:S(2)}) copy-start(s32[16]{0:T(128)} %param.19) | copy-start | bytes 196
  177.1 7.5 %copy-start.15 = (s32[8]{0:T(128)S(1)}, s32[8]{0:T(128)}, u32[]{:S(2)}) copy-start(s32[8]{0:T(128)} %param.18) | copy-start | bytes 100
  177.1 22.0 %all-to-all-start = ((bf16[8,512,128]{2,1,0:T(8,128)(2,1)}), bf16[8,512,128]{2,1,0:T(8,128)(2,1)S(1)}, u32[]{:S(2)}, u32[]{:S(2)}) async-start(bf16[8,512,128]{2,1,0:T(8,128)(2,1)} %shard_map.153), calls=%async_computation | async-start | bytes 2097152 | tf_op jit(solution)/shard_map/all_to_all | solution.py:247

commit v2 on v1

v2 whole, which is shorter than its diff:
```python
import functools
import math

import jax
import jax.numpy as jnp
from jax import lax
from jax.experimental import pallas as pl
from jax.experimental.pallas import tpu as pltpu
from jax.sharding import Mesh
from jax.sharding import PartitionSpec as P

D = 2048
FF = 4096
REGION = ("xh", "y")
DEV = ("z", "xl", "c")
NR = 8
BF = jnp.bfloat16
F32 = jnp.float32
MIB = 1 << 20


def params(mib=16):
    return pltpu.CompilerParams(vmem_limit_bytes=mib * MIB)


def whole(count):
    return [pl.BlockSpec(memory_space=pltpu.VMEM)] * count


def grads_kernel(n_blocks, first, last, *refs):
    refs, (held, sems) = refs[:-2], refs[-2:]
    blocks = refs[:n_blocks]
    up_ref, down_ref = refs[n_blocks : n_blocks + 2]
    outs = refs[-2:]
    coming = []
    if not first:
        olds = refs[n_blocks + 2 : n_blocks + 4]
        coming = [pltpu.make_async_copy(olds[i], held.at[i], sems.at[i]) for i in range(2)]
    for copy in coming:
        copy.start()
    x = jnp.concatenate([b[0] for b in blocks], axis=0)
    g = jnp.concatenate([b[1] for b in blocks], axis=0)
    hid = jnp.dot(x, up_ref[...], preferred_element_type=F32) * D ** (-0.5)
    dact = lax.dot_general(
        g, down_ref[...], (((1,), (1,)), ((), ())), preferred_element_type=F32
    ) * FF ** (-0.5)
    root = math.sqrt(2.0 / math.pi)
    sq = hid * hid
    t = jnp.tanh(root * (hid + 0.044715 * (sq * hid)))
    act = (0.5 * hid * (1.0 + t)).astype(BF)
    slope = 0.5 * (1.0 + t) + 0.5 * hid * (1.0 - t * t) * (root * (1.0 + 3 * 0.044715 * sq))
    dhid = (dact * slope).astype(BF)
    for copy in coming:
        copy.wait()
    for i, (left, right, scale) in enumerate(((act, g, FF), (dhid, x, D))):
        total = lax.dot_general(left, right, (((0,), (0,)), ((), ())), preferred_element_type=F32)
        total = total * (0.5 * scale ** (-0.5))
        if not first:
            total = total + held[i]
        if last:
            outs[0][i] = total[0:128]
            outs[1][i] = total[128:256].astype(BF)
        else:
            held[i] = total
            pltpu.make_async_copy(held.at[i], outs[i], sems.at[i]).start()
    if not last:
        for i in range(2):
            pltpu.make_async_copy(held.at[i], outs[i], sems.at[i]).wait()


def grads_step(blocks, up2, down2, sums, last=False):
    n = len(blocks)
    first = sums is None
    tokens = sum(b.shape[1] for b in blocks)
    operands = list(blocks) + [up2, down2] + ([] if first else list(sums))
    shape = jax.ShapeDtypeStruct((256, D), F32)
    half = jax.ShapeDtypeStruct((2, 128, D), F32), jax.ShapeDtypeStruct((2, 128, D), BF)
    far = [pl.BlockSpec(memory_space=pltpu.HBM)] * 2
    return pl.pallas_call(
        functools.partial(grads_kernel, n, first, last),
        out_shape=half if last else (shape, shape),
        in_specs=whole(n + 2) + ([] if first else far),
        out_specs=tuple(whole(2) if last else far),
        scratch_shapes=[pltpu.VMEM((2, 256, D), F32), pltpu.SemaphoreType.DMA((2,))],
        compiler_params=params(18),
        cost_estimate=pl.CostEstimate(
            flops=20 * 10**9, bytes_accessed=64 * MIB, transcendentals=tokens * 256
        ),
    )(*operands)


def down_in(eighth):
    return jnp.concatenate([eighth[:, j * 128 : (j + 1) * 128] for j in range(16)], axis=0)


def pseudo_kernel(kept_ref, got_ref, du_ref, dd_ref, out_ref):
    down = kept_ref[0] + got_ref[0].astype(F32)
    down = (down + dd_ref[0].astype(F32)).astype(BF)
    up = kept_ref[1] + got_ref[1].astype(F32)
    for r in range(NR):
        mine = up[:, r * 256 : (r + 1) * 256].T + du_ref[0, r * 256 : (r + 1) * 256, :].astype(F32)
        out_ref[r, 0:256, :] = mine.astype(BF)
        out_ref[r, 256:512, :] = down_in(down[r * 16 : (r + 1) * 16, :])


def pseudo(kept, got, drift_up, drift_down):
    return pl.pallas_call(
        pseudo_kernel,
        out_shape=jax.ShapeDtypeStruct((NR, 512, 128), BF),
        in_specs=whole(4),
        out_specs=pl.BlockSpec(memory_space=pltpu.VMEM),
        compiler_params=params(),
    )(kept, got, drift_up, drift_down)


def state_kernel(gu_ref, gd_ref, mu_ref, md_ref, out_ref):
    for s in range(2):
        out_ref[0, s, 0:256, :] = gu_ref[s].astype(F32) - 0.567 * mu_ref[s]
        out_ref[0, s, 256:512, :] = down_in(gd_ref[s].astype(F32) - 0.567 * md_ref[s])


def state(global_up, global_down, mom_up, mom_down):
    up = pl.BlockSpec((2, 256, 128), lambda i: (0, i, 0))
    down = pl.BlockSpec((2, 16, D), lambda i: (0, i, 0))
    return pl.pallas_call(
        state_kernel,
        grid=(NR,),
        out_shape=jax.ShapeDtypeStruct((NR, 2, 512, 128), F32),
        in_specs=[up, down, up, down],
        out_specs=pl.BlockSpec((1, 2, 512, 128), lambda i: (i, 0, 0, 0)),
        compiler_params=params(),
        cost_estimate=pl.CostEstimate(flops=4 * MIB, bytes_accessed=10 * MIB, transcendentals=0),
    )(global_up, global_down, mom_up, mom_down)


def step_kernel(target_ref, factor_ref, p_ref, a_ref, out_ref, sum_ref):
    sum_ref[...] = jnp.zeros_like(sum_ref)
    for r in range(NR):
        at = target_ref[r]
        sum_ref[at] = sum_ref[at] + p_ref[r].astype(F32)
    for o in range(NR):
        for s in range(2):
            slot = 2 * o + s
            out_ref[o, s] = (a_ref[o, s] - factor_ref[slot] * sum_ref[slot]).astype(BF)
    for r in range(NR):
        at = target_ref[r]
        out_ref[r, 2] = out_ref[at // 2, at % 2]


def step(target, factor, pieces, base):
    rows = 128
    return pl.pallas_call(
        step_kernel,
        grid=(512 // rows,),
        out_shape=jax.ShapeDtypeStruct((NR, 3, 512, 128), BF),
        in_specs=[
            pl.BlockSpec(memory_space=pltpu.SMEM),
            pl.BlockSpec(memory_space=pltpu.SMEM),
            pl.BlockSpec((NR, rows, 128), lambda i: (0, i, 0)),
            pl.BlockSpec((NR, 2, rows, 128), lambda i: (0, 0, i, 0)),
        ],
        out_specs=pl.BlockSpec((NR, 3, rows, 128), lambda i: (0, 0, i, 0)),
        scratch_shapes=[pltpu.VMEM((16, rows, 128), F32)],
        compiler_params=params(16),
    )(target, factor, pieces, base)


def place_kernel(got_ref, nu_ref, nd_ref, ru_ref, rd_ref):
    for p in range(2):
        up, down = slice(p * 256, p * 256 + 256), slice(p * 16, p * 16 + 16)
        for s in range(3):
            to_up, to_down = (nu_ref, nd_ref) if s < 2 else (ru_ref, rd_ref)
            to_up[s % 2, up] = got_ref[p, s, 0:256]
            to_down[s % 2, down] = jnp.concatenate(
                [got_ref[p, s, 256 + j * 16 : 272 + j * 16, :] for j in range(16)], axis=1
            )


def place(got):
    def up(n):
        return pl.BlockSpec((n, 512, 128), lambda i: (0, i, 0))

    def down(n):
        return pl.BlockSpec((n, 32, D), lambda i: (0, i, 0))

    return pl.pallas_call(
        place_kernel,
        grid=(NR // 2,),
        out_shape=(
            jax.ShapeDtypeStruct((2, D, 128), BF),
            jax.ShapeDtypeStruct((2, 128, D), BF),
            jax.ShapeDtypeStruct((1, D, 128), BF),
            jax.ShapeDtypeStruct((1, 128, D), BF),
        ),
        in_specs=[pl.BlockSpec((2, 3, 512, 128), lambda i: (i, 0, 0, 0))],
        out_specs=(up(2), down(2), up(1), down(1)),
        compiler_params=params(16),
    )(got)


RIGHT = [(i, (i + 1) % 8) for i in range(8)]
LEFT = [(i, (i + 7) % 8) for i in range(8)]
SWAP = [(0, 1), (1, 0)]


def on_device(
    acts,
    cotan,
    w_up,
    w_down,
    drift_up,
    drift_down,
    path,
    slot_of,
    global_up,
    global_down,
    mom_up,
    mom_down,
):
    module_ids = jnp.arange(slot_of.shape[0], dtype=jnp.int32)
    target = jnp.sum(jnp.where(path[:, None] == module_ids[None, :], slot_of[None, :], 0), axis=1)
    chosen = (target[:, None] == module_ids[None, :]).astype(F32)
    factor = 1.33 / jnp.maximum(jnp.sum(chosen, axis=0), 1.0)

    own = jnp.concatenate([acts, cotan], axis=0)
    other = lax.ppermute(own, "xl", SWAP)
    up2 = jnp.concatenate([w_up[0], lax.ppermute(w_up, "c", SWAP)[0]], axis=1)
    down2 = jnp.concatenate([w_down[0], lax.ppermute(w_down, "c", SWAP)[0]], axis=0)

    base = state(global_up, global_down, mom_up, mom_down)
    heads = [(own, own), (other, other)]
    sums = grads_step([own, other], up2, down2, None)
    for hop in range(4):
        blocks = []
        for k in range(2):
            right, left = heads[k]
            if hop == 3:
                right, left = right[:, :32], left[:, 32:]
            right = lax.ppermute(right, "z", RIGHT)
            left = lax.ppermute(left, "z", LEFT)
            if k == 0 and hop == 0:
                right, left, other = lax.optimization_barrier((right, left, other))
                heads[1] = (other, other)
            if k == 1 and hop == 0:
                right, left, base = lax.optimization_barrier((right, left, base))
                base = lax.all_to_all(base, REGION, 0, 0, tiled=True)
            if k == 1 and hop == 3:
                right, base = lax.optimization_barrier((right, base))
            if k == 1 and hop < 3:
                right, left, sums = lax.optimization_barrier((right, left, sums))
            heads[k] = (right, left)
            blocks += [right, left]
        sums = grads_step(blocks, up2, down2, sums, last=hop == 3)

    kept, sent = sums
    got = lax.ppermute(sent, "c", SWAP)
    pieces = pseudo(kept, got, drift_up, drift_down)
    pieces = lax.all_to_all(pieces, REGION, 0, 0, tiled=True)
    reply = step(target, factor, pieces, base)
    reply = lax.all_to_all(reply, REGION, 0, 0, tiled=True)
    return place(reply)


def solution(mesh):
    fine = Mesh(mesh.devices.reshape(2, 4, 8, 2, 2), REGION + DEV)
    rows = P(REGION, DEV, None)
    cols = P(REGION, None, DEV)
    return jax.shard_map(
        on_device,
        mesh=fine,
        in_specs=(rows, rows, cols, rows, cols, rows, P(), P(), cols, rows, cols, rows),
        out_specs=(cols, rows, cols, rows),
        check_vma=False,
    )
```

time: 252 us -> 177 us (0.70)
  waiting for transfers between devices: 98.6 us -> 42.5 us
  Pallas kernels: 42.3 us -> 22 us
  local copies, waits for them, and re-layouts: 11.7 us -> 22.9 us
  starting transfers between devices: 54 us -> 43.6 us
    ppermute x1, waiting for transfers between devices: 50.8 us -> 0.01 us  [on_device(): other = lax.ppermute(own, 'xl', SWAP)]
    pallas_call x7 -> x6, Pallas kernels: 27.2 us -> 15.7 us  [the longest x5 13.6 us: grads_step(): pl.pallas_call(functools.partial(grads_kernel, n, first, last), out_shape...]
    unnamed x33 -> x39, local copies, waits for them, and re-layouts: 11.6 us -> 20.4 us
    ppermute x8, waiting for transfers between devices: 31.3 us -> 23.5 us  [on_device(): right = lax.ppermute(right, 'z', RIGHT)]
    pallas_call x1, Pallas kernels: 6.22 us -> 1.02 us  [state(): pl.pallas_call(state_kernel, grid=(NR,), out_shape=jax.ShapeDtypeStruct((...]
    ppermute x1, starting transfers between devices: 4.54 us -> 0.01 us  [on_device(): lax.ppermute(w_down, 'c', SWAP)[0]]
  transfers between devices with their start and end apart: 22 -> 22, of which waited for: 8 -> 11; matrix products, arithmetic and copies ran while one was open for 0% -> 1% of each run, Pallas kernels for 11% -> 7%
where the time goes in v2:
time: 177 us; the launch traced here: 176 us
  starting transfers between devices  43.6 us (25%)
  blocking collectives  43.5 us (25%)
  waiting for transfers between devices  42.5 us (24%)
  local copies, waits for them, and re-layouts  22.9 us (13%)
  Pallas kernels  22 us (12%)
    all_to_all x1, blocking collectives, on_device(): reply = lax.all_to_all(reply, REGION, 0, 0, tiled=True)  43.5 us
    ppermute x8, waiting for transfers between devices, on_device(): right = lax.ppermute(right, 'z', RIGHT)  23.5 us
    ppermute x8, starting transfers between devices, on_device(): left = lax.ppermute(left, 'z', LEFT)  22.4 us
    unnamed x39, local copies, waits for them, and re-layouts  20.4 us
    all_to_all x1, waiting for transfers between devices, on_device(): pieces = lax.all_to_all(pieces, REGION, 0, 0, tiled=True)  14.2 us
    pallas_call x5, Pallas kernels, grads_step(): pl.pallas_call(functools.partial(grads_kernel, n, first, last), out_shape...  13.6 us
    all_to_all x1, starting transfers between devices, on_device(): pieces = lax.all_to_all(pieces, REGION, 0, 0, tiled=True)  6.48 us
    all_to_all x1, starting transfers between devices, on_device(): base = lax.all_to_all(base, REGION, 0, 0, tiled=True)  6.36 us
  transfers between devices with their start and end apart: 22, of which 11 were waited for; matrix products, arithmetic and copies ran while one was open for 1% of the time, Pallas kernels for 7%

profile of v2, /device:TPU:1, one launch (start us, length us, event | category | flops | bytes accessed | tf_op | source)
XLA Modules:
  0.0 175.9 jit_solution(17328961789543530547)
XLA Ops:
  0.6 1.0 constant_dynamic-update-slice_fusion.1
  1.6 0.0 copy-start.15
  1.6 1.0 constant_dynamic-update-slice_fusion.refs_0_
  2.6 2.1 %collective-permute-start.2 = (bf16[2,64,2048]{2,1,0:T(8,128)(2,1)S(1)}, bf16[2,64,2048]{2,1,0:T(8,128)(2,1)S(1)}, u32[]{:S(2)}, u32[]{:S(2)}) collective-permute-start(bf16[2,64,2048]{2,1,0:T(8,128)(2,1)S(1)} %constant_dynamic-update-slice_fusion.refs_0_), channel_id=1, source_target_pairs={{0,2},{2,0},{1,3},{3,1},{4,6},{6,4},{5,7},{7,5},{8,10},{10,8},{9,1... | collective-permute-start | bytes 1572872 | tf_op jit(solution)/shard_map/ppermute | solution.py:226
  4.8 1.6 collective-permute-start
  6.4 3.9 %collective-permute-start.1 = (bf16[2,64,2048]{2,1,0:T(8,128)(2,1)S(1)}, bf16[2,64,2048]{2,1,0:T(8,128)(2,1)}, u32[]{:S(2)}, u32[]{:S(2)}) collective-permute-start(bf16[2,64,2048]{2,1,0:T(8,128)(2,1)S(1)} %constant_dynamic-update-slice_fusion.refs_0_), channel_id=1, source_target_pairs={{0,28},{4,0},{8,4},{12,8},{16,12},{20,16},{24,20},{28,24},{1,29},{... | collective-permute-start | bytes 1572872 | tf_op jit(solution)/shard_map/ppermute | solution.py:240
  10.4 1.2 collective-permute-start.11
  11.6 0.0 collective-permute-start.12
  11.6 1.6 copy-done.1
  13.2 1.6 copy-done.2
  14.8 1.2 copy-done.3
  16.0 1.2 copy-done.4
  17.2 1.0 shard_map.147
  18.3 2.0 %copy-done = f32[8,2,512,128]{3,2,1,0:T(8,128)} copy-done((f32[8,2,512,128]{3,2,1,0:T(8,128)}, f32[8,2,512,128]{3,2,1,0:T(8,128)S(1)}, u32[]{:S(2)}) %copy-start) | copy-done | bytes 4194328
  20.2 0.0 collective-permute-done.2.refs_1_
  20.2 1.4 collective-permute-done.refs_0_
  21.7 0.0 collective-permute-done.1.refs_1_
  21.7 2.5 %collective-permute-start.10 = (bf16[2,64,2048]{2,1,0:T(8,128)(2,1)S(1)}, bf16[2,64,2048]{2,1,0:T(8,128)(2,1)}, u32[]{:S(2)}, u32[]{:S(2)}) collective-permute-start(bf16[2,64,2048]{2,1,0:T(8,128)(2,1)S(1)} %collective-permute-done.2.refs_1_), channel_id=1, source_target_pairs={{0,28},{4,0},{8,4},{12,8},{16,12},{20,16},{24,20},{28,24},{1,29},{... | collective-permute-start | bytes 1572872 | tf_op jit(solution)/shard_map/ppermute | solution.py:240
  24.2 2.7 %collective-permute-start.6 = (bf16[2,64,2048]{2,1,0:T(8,128)(2,1)}, bf16[2,64,2048]{2,1,0:T(8,128)(2,1)}, u32[]{:S(2)}, u32[]{:S(2)}) collective-permute-start(bf16[2,64,2048]{2,1,0:T(8,128)(2,1)} %collective-permute-done.1.refs_1_), channel_id=1, source_target_pairs={{0,28},{4,0},{8,4},{12,8},{16,12},{20,16},{24,20},{28,24},{1,29},{... | collective-permute-start | bytes 1572872 | tf_op jit(solution)/shard_map/ppermute | solution.py:240
  26.9 0.1 pad_maximum_fusion.refs_2_.refs_4_
  27.0 0.1 pad_maximum_fusion.1.refs_3_.refs_5_
  27.1 1.9 %shard_map.148 = (f32[256,2048]{1,0:T(8,128)S(1)}, f32[256,2048]{1,0:T(8,128)S(1)}) custom-call(bf16[2,64,2048]{2,1,0:T(8,128)(2,1)S(1)} %constant_dynamic-update-slice_fusion.refs_0_, bf16[2,64,2048]{2,1,0:T(8,128)(2,1)S(1)} %collective-permute-done.2.refs_1_, bf16[2048,256]{1,0:T(8,128)(2,1)S(1)} %pad_maximum_fusion.refs_2_.refs_4_, ...), custom_call_target="tpu_custom_call" | custom-call | flops 20000000000 | bytes 67108864 | tf_op jit(solution)/shard_map/pallas_call | solution.py:79
  29.0 1.3 copy-done.7
  30.3 1.4 copy-done.9
  31.7 2.0 %collective-permute-done.10.refs_3_ = bf16[2,64,2048]{2,1,0:T(8,128)(2,1)} collective-permute-done((bf16[2,64,2048]{2,1,0:T(8,128)(2,1)S(1)}, bf16[2,64,2048]{2,1,0:T(8,128)(2,1)}, u32[]{:S(2)}, u32[]{:S(2)}) %collective-permute-start.10) | collective-permute-done | bytes 524320 | tf_op jit(solution)/shard_map/ppermute | solution.py:240
  33.7 3.1 %collective-permute-done.9.refs_2_ = bf16[2,64,2048]{2,1,0:T(8,128)(2,1)} collective-permute-done((bf16[2,64,2048]{2,1,0:T(8,128)(2,1)S(1)}, bf16[2,64,2048]{2,1,0:T(8,128)(2,1)}, u32[]{:S(2)}, u32[]{:S(2)}) %collective-permute-start.9) | collective-permute-done | bytes 524320 | tf_op jit(solution)/shard_map/ppermute | solution.py:239
  36.7 0.0 collective-permute-start.13
  36.7 2.7 %collective-permute-start.14 = (bf16[2,64,2048]{2,1,0:T(8,128)(2,1)}, bf16[2,64,2048]{2,1,0:T(8,128)(2,1)}, u32[]{:S(2)}, u32[]{:S(2)}) collective-permute-start(bf16[2,64,2048]{2,1,0:T(8,128)(2,1)} %collective-permute-done.10.refs_3_), channel_id=1, source_target_pairs={{0,28},{4,0},{8,4},{12,8},{16,12},{20,16},{24,20},{28,24},{1,29},{... | collective-permute-start | bytes 1572872 | tf_op jit(solution)/shard_map/ppermute | solution.py:240
  39.4 6.4 %all-to-all-start = ((f32[8,2,512,128]{3,2,1,0:T(8,128)}), f32[8,2,512,128]{3,2,1,0:T(8,128)}, u32[]{:S(2)}, u32[]{:S(2)}) async-start(f32[8,2,512,128]{3,2,1,0:T(8,128)} %copy-done), calls=%async_computation | async-start | bytes 8388608 | tf_op jit(solution)/shard_map/all_to_all | solution.py:246
  45.8 2.1 %collective-permute-done.3.refs_0_ = bf16[2,64,2048]{2,1,0:T(8,128)(2,1)S(1)} collective-permute-done((bf16[2,64,2048]{2,1,0:T(8,128)(2,1)S(1)}, bf16[2,64,2048]{2,1,0:T(8,128)(2,1)S(1)}, u32[]{:S(2)}, u32[]{:S(2)}) %collective-permute-start.3) | collective-permute-done | bytes 524320 | tf_op jit(solution)/shard_map/ppermute | solution.py:239
  47.9 0.0 collective-permute-start.4
  47.9 2.7 %collective-permute-start.7 = (bf16[2,64,2048]{2,1,0:T(8,128)(2,1)}, bf16[2,64,2048]{2,1,0:T(8,128)(2,1)S(1)}, u32[]{:S(2)}, u32[]{:S(2)}) collective-permute-start(bf16[2,64,2048]{2,1,0:T(8,128)(2,1)} %collective-permute-done.6.refs_1_), channel_id=1, source_target_pairs={{0,28},{4,0},{8,4},{12,8},{16,12},{20,16},{24,20},{28,24},{1,29},{... | collective-permute-start | bytes 1572872 | tf_op jit(solution)/shard_map/ppermute | solution.py:240
  50.5 1.6 copy-done.8
  52.1 1.6 copy-done.10
  53.7 3.7 %shard_map.149 = (f32[256,2048]{1,0:T(8,128)S(1)}, f32[256,2048]{1,0:T(8,128)S(1)}) custom-call(bf16[2,64,2048]{2,1,0:T(8,128)(2,1)S(1)} %collective-permute-done.refs_0_, bf16[2,64,2048]{2,1,0:T(8,128)(2,1)} %collective-permute-done.1.refs_1_, bf16[2,64,2048]{2,1,0:T(8,128)(2,1)} %collective-permute-done.9.refs_2_, ...), custom_call_target="tpu_custom_call" | custom-call | flops 20000000000 | bytes 67108864 | tf_op jit(solution)/shard_map/pallas_call | solution.py:79
  57.5 1.7 collective-permute-done.13.refs_2_
  59.2 2.7 %collective-permute-start.16 = (bf16[2,64,2048]{2,1,0:T(8,128)(2,1)}, bf16[2,64,2048]{2,1,0:T(8,128)(2,1)S(1)}, u32[]{:S(2)}, u32[]{:S(2)}) collective-permute-start(bf16[2,64,2048]{2,1,0:T(8,128)(2,1)} %collective-permute-done.14.refs_3_), channel_id=1, source_target_pairs={{0,28},{4,0},{8,4},{12,8},{16,12},{20,16},{24,20},{28,24},{1,29},{... | collective-permute-start | bytes 1572872 | tf_op jit(solution)/shard_map/ppermute | solution.py:240
  61.9 8.6 %collective-permute-done.4.refs_0_ = bf16[2,64,2048]{2,1,0:T(8,128)(2,1)S(1)} collective-permute-done((bf16[2,64,2048]{2,1,0:T(8,128)(2,1)S(1)}, bf16[2,64,2048]{2,1,0:T(8,128)(2,1)S(1)}, u32[]{:S(2)}, u32[]{:S(2)}) %collective-permute-start.4) | collective-permute-done | bytes 524320 | tf_op jit(solution)/shard_map/ppermute | solution.py:239
  70.5 0.1 collective-permute-start.5
  70.6 0.7 slice.17
  71.3 2.7 %collective-permute-start.8 = (bf16[2,32,2048]{2,1,0:T(8,128)(2,1)}, bf16[2,32,2048]{2,1,0:T(8,128)(2,1)S(1)}, u32[]{:S(2)}, u32[]{:S(2)}) collective-permute-start(bf16[2,32,2048]{2,1,0:T(8,128)(2,1)} %slice.17), channel_id=1, source_target_pairs={{0,28},{4,0},{8,4},{12,8},{16,12},{20,16},{24,20},{28,24},{1,29},{... | collective-permute-start | bytes 786440 | tf_op jit(solution)/shard_map/ppermute | solution.py:240
  73.9 3.7 %shard_map.150 = (f32[256,2048]{1,0:T(8,128)S(1)}, f32[256,2048]{1,0:T(8,128)S(1)}) custom-call(bf16[2,64,2048]{2,1,0:T(8,128)(2,1)S(1)} %collective-permute-done.3.refs_0_, bf16[2,64,2048]{2,1,0:T(8,128)(2,1)} %collective-permute-done.6.refs_1_, bf16[2,64,2048]{2,1,0:T(8,128)(2,1)} %collective-permute-done.13.refs_2_, ...), custom_call_target="tpu_custom_call" | custom-call | flops 20000000000 | bytes 67108864 | tf_op jit(solution)/shard_map/pallas_call | solution.py:79
  77.7 4.0 %collective-permute-done.15.refs_2_ = bf16[2,64,2048]{2,1,0:T(8,128)(2,1)S(1)} collective-permute-done((bf16[2,64,2048]{2,1,0:T(8,128)(2,1)}, bf16[2,64,2048]{2,1,0:T(8,128)(2,1)S(1)}, u32[]{:S(2)}, u32[]{:S(2)}) %collective-permute-start.15) | collective-permute-done | bytes 524320 | tf_op jit(solution)/shard_map/ppermute | solution.py:239
  81.7 0.1 collective-permute-start.17
  81.8 0.7 slice.15
  82.5 2.7 %collective-permute-start.18 = (bf16[2,32,2048]{2,1,0:T(8,128)(2,1)}, bf16[2,32,2048]{2,1,0:T(8,128)(2,1)S(1)}, u32[]{:S(2)}, u32[]{:S(2)}) collective-permute-start(bf16[2,32,2048]{2,1,0:T(8,128)(2,1)} %slice.15), channel_id=1, source_target_pairs={{0,28},{4,0},{8,4},{12,8},{16,12},{20,16},{24,20},{28,24},{1,29},{... | collective-permute-start | bytes 786440 | tf_op jit(solution)/shard_map/ppermute | solution.py:240
  85.2 2.4 %shard_map.151 = (f32[256,2048]{1,0:T(8,128)S(1)}, f32[256,2048]{1,0:T(8,128)S(1)}) custom-call(bf16[2,64,2048]{2,1,0:T(8,128)(2,1)S(1)} %collective-permute-done.4.refs_0_, bf16[2,64,2048]{2,1,0:T(8,128)(2,1)S(1)} %collective-permute-done.7.refs_1_, bf16[2,64,2048]{2,1,0:T(8,128)(2,1)S(1)} %collective-permute-done.15.refs_2_, ...), custom_call_target="tpu_custom_call" | custom-call | flops 20000000000 | bytes 67108864 | tf_op jit(solution)/shard_map/pallas_call | solution.py:79
  87.6 1.3 copy-done.11
  88.9 1.4 copy-done.13
  90.3 2.6 %collective-permute-done.17.refs_2_ = bf16[2,32,2048]{2,1,0:T(8,128)(2,1)S(1)} collective-permute-done((bf16[2,32,2048]{2,1,0:T(8,128)(2,1)S(1)}, bf16[2,32,2048]{2,1,0:T(8,128)(2,1)S(1)}, u32[]{:S(2)}, u32[]{:S(2)}) %collective-permute-start.17) | collective-permute-done | bytes 262176 | tf_op jit(solution)/shard_map/ppermute | solution.py:239
  92.9 0.5 all-to-all-done.a_ref
  93.5 1.6 copy-done.12
  95.1 1.6 copy-done.14
  96.7 1.9 %shard_map.152 = (f32[2,128,2048]{2,1,0:T(8,128)S(1)}, bf16[2,128,2048]{2,1,0:T(8,128)(2,1)S(1)}) custom-call(bf16[2,32,2048]{2,1,0:T(8,128)(2,1)S(1)} %collective-permute-done.5.refs_0_, bf16[2,32,2048]{2,1,0:T(8,128)(2,1)S(1)} %collective-permute-done.8.refs_1_, bf16[2,32,2048]{2,1,0:T(8,128)(2,1)S(1)} %collective-permute-done.17.refs_2_, ...), custom_call_target="tpu_custom_call" | custom-call | flops 20000000000 | bytes 67108864 | tf_op jit(solution)/shard_map/pallas_call | solution.py:79
  98.5 3.2 %collective-permute-start.19 = (bf16[2,128,2048]{2,1,0:T(8,128)(2,1)S(1)}, bf16[2,128,2048]{2,1,0:T(8,128)(2,1)S(1)}, u32[]{:S(2)}, u32[]{:S(2)}) collective-permute-start(bf16[2,128,2048]{2,1,0:T(8,128)(2,1)S(1)} %get-tuple-element.62), channel_id=1, source_target_pairs={{0,1},{1,0},{2,3},{3,2},{4,5},{5,4},{6,7},{7,6},{8,9},{9,8},{10,11... | collective-permute-start | bytes 3145736 | tf_op jit(solution)/shard_map/ppermute | solution.py:256
  101.7 2.3 %collective-permute-done.19.got_ref = bf16[2,128,2048]{2,1,0:T(8,128)(2,1)S(1)} collective-permute-done((bf16[2,128,2048]{2,1,0:T(8,128)(2,1)S(1)}, bf16[2,128,2048]{2,1,0:T(8,128)(2,1)S(1)}, u32[]{:S(2)}, u32[]{:S(2)}) %collective-permute-start.19) | collective-permute-done | bytes 1048608 | tf_op jit(solution)/shard_map/ppermute | solution.py:256
  104.0 1.6 shard_map.153
  105.6 6.5 %all-to-all-start.1 = ((bf16[8,512,128]{2,1,0:T(8,128)(2,1)}), bf16[8,512,128]{2,1,0:T(8,128)(2,1)S(1)}, u32[]{:S(2)}, u32[]{:S(2)}) async-start(bf16[8,512,128]{2,1,0:T(8,128)(2,1)} %shard_map.153), calls=%async_computation.1 | async-start | bytes 2097152 | tf_op jit(solution)/shard_map/all_to_all | solution.py:258
  112.1 0.2 select_reduce_fusion.target_ref
  112.2 0.1 convert_reduce_fusion
  112.3 14.2 %all-to-all-done.1.p_ref = bf16[8,512,128]{2,1,0:T(8,128)(2,1)S(1)} async-done(((bf16[8,512,128]{2,1,0:T(8,128)(2,1)}), bf16[8,512,128]{2,1,0:T(8,128)(2,1)S(1)}, u32[]{:S(2)}, u32[]{:S(2)}) %all-to-all-start.1) | async-done | bytes 1048608 | tf_op jit(solution)/shard_map/all_to_all | solution.py:258
  126.6 3.7 %shard_map.154 = bf16[8,3,512,128]{3,2,1,0:T(8,128)(2,1)S(1)} custom-call(s32[8]{0:T(128)S(1)} %select_reduce_fusion.target_ref, f32[16]{0:T(128)S(1)} %maximum_divide_fusion.factor_ref, bf16[8,512,128]{2,1,0:T(8,128)(2,1)S(1)} %all-to-all-done.1.p_ref, f32[8,2,512,128]{3,2,1,0:T(8,128)} %all-to-all-done.a_ref), custom_call_target="tpu_custom_call" | custom-call | tf_op jit(solution)/shard_map/pallas_call | solution.py:152
  130.3 43.5 %all_to_all.15.got_ref = bf16[8,3,512,128]{3,2,1,0:T(8,128)(2,1)S(1)} all-to-all(bf16[8,3,512,128]{3,2,1,0:T(8,128)(2,1)S(1)} %shard_map.154), channel_id=1, replica_groups=mesh['xh'=2,'y'=4,'z'=8,'xl'=2,'c'=2] {'xh','y'}, dimensions={0} | all-to-all | bytes 6291456 | tf_op jit(solution)/shard_map/all_to_all | solution.py:260
  173.8 2.1 %shard_map.155 = (bf16[2,2048,128]{2,1,0:T(8,128)(2,1)}, bf16[2,128,2048]{2,1,0:T(8,128)(2,1)}, bf16[1,2048,128]{2,1,0:T(8,128)(2,1)}, bf16[1,128,2048]{2,1,0:T(8,128)(2,1)}) custom-call(bf16[8,3,512,128]{3,2,1,0:T(8,128)(2,1)S(1)} %all_to_all.15.got_ref), custom_call_target="tpu_custom_call" | custom-call | tf_op jit(solution)/shard_map/pallas_call | solution.py:186
  (39 shorter events, 0.1 us)
Async XLA Ops:
  1.6 25.3 %copy-start.15 = (bf16[1,2048,128]{2,1,0:T(8,128)(2,1)S(1)}, bf16[1,2048,128]{2,1,0:T(8,128)(2,1)}, u32[]{:S(2)}) copy-start(bf16[1,2048,128]{2,1,0:T(8,128)(2,1)} %param.14) | copy-start | bytes 1572868
  2.6 17.6 %collective-permute-start.2 = (bf16[2,64,2048]{2,1,0:T(8,128)(2,1)S(1)}, bf16[2,64,2048]{2,1,0:T(8,128)(2,1)S(1)}, u32[]{:S(2)}, u32[]{:S(2)}) collective-permute-start(bf16[2,64,2048]{2,1,0:T(8,128)(2,1)S(1)} %constant_dynamic-update-slice_fusion.refs_0_), channel_id=1, source_target_pairs={{0,2},{2,0},{1,3},{3,1},{4,6},{6,4},{5,7},{7,5},{8,10},{10,8},{9,1... | collective-permute-start | bytes 1572872 | tf_op jit(solution)/shard_map/ppermute | solution.py:226
  4.8 16.9 %collective-permute-start = (bf16[2,64,2048]{2,1,0:T(8,128)(2,1)S(1)}, bf16[2,64,2048]{2,1,0:T(8,128)(2,1)S(1)}, u32[]{:S(2)}, u32[]{:S(2)}) collective-permute-start(bf16[2,64,2048]{2,1,0:T(8,128)(2,1)S(1)} %constant_dynamic-update-slice_fusion.refs_0_), channel_id=1, source_target_pairs={{0,4},{4,8},{8,12},{12,16},{16,20},{20,24},{24,28},{28,0},{1,5},{5... | collective-permute-start | bytes 1572872 | tf_op jit(solution)/shard_map/ppermute | solution.py:239
  6.4 15.3 %collective-permute-start.1 = (bf16[2,64,2048]{2,1,0:T(8,128)(2,1)S(1)}, bf16[2,64,2048]{2,1,0:T(8,128)(2,1)}, u32[]{:S(2)}, u32[]{:S(2)}) collective-permute-start(bf16[2,64,2048]{2,1,0:T(8,128)(2,1)S(1)} %constant_dynamic-update-slice_fusion.refs_0_), channel_id=1, source_target_pairs={{0,28},{4,0},{8,4},{12,8},{16,12},{20,16},{24,20},{28,24},{1,29},{... | collective-permute-start | bytes 1572872 | tf_op jit(solution)/shard_map/ppermute | solution.py:240
  10.4 13.8 %collective-permute-start.11 = (bf16[1,2048,128]{2,1,0:T(8,128)(2,1)}, bf16[1,2048,128]{2,1,0:T(8,128)(2,1)S(1)}, u32[]{:S(2)}, u32[]{:S(2)}) collective-permute-start(bf16[1,2048,128]{2,1,0:T(8,128)(2,1)} %param.14), channel_id=1, source_target_pairs={{0,1},{1,0},{2,3},{3,2},{4,5},{5,4},{6,7},{7,6},{8,9},{9,8},{10,11... | collective-permute-start | bytes 1572872 | tf_op jit(solution)/shard_map/ppermute | solution.py:227
  11.6 15.4 %collective-permute-start.12 = (bf16[1,128,2048]{2,1,0:T(8,128)(2,1)}, bf16[1,128,2048]{2,1,0:T(8,128)(2,1)S(1)}, u32[]{:S(2)}, u32[]{:S(2)}) collective-permute-start(bf16[1,128,2048]{2,1,0:T(8,128)(2,1)} %param.15), channel_id=1, source_target_pairs={{0,1},{1,0},{2,3},{3,2},{4,5},{5,4},{6,7},{7,6},{8,9},{9,8},{10,11... | collective-permute-start | bytes 1572872 | tf_op jit(solution)/shard_map/ppermute | solution.py:228
  11.6 1.6 copy-start.1
  13.2 1.6 copy-start.2
  14.8 1.2 copy-start.3
  16.0 1.2 copy-start.4
  18.2 2.0 %copy-start = (f32[8,2,512,128]{3,2,1,0:T(8,128)}, f32[8,2,512,128]{3,2,1,0:T(8,128)S(1)}, u32[]{:S(2)}) copy-start(f32[8,2,512,128]{3,2,1,0:T(8,128)S(1)} %shard_map.147) | copy-start | bytes 12582916
  20.2 6.7 %copy-start.16 = (bf16[1,128,2048]{2,1,0:T(8,128)(2,1)S(1)}, bf16[1,128,2048]{2,1,0:T(8,128)(2,1)}, u32[]{:S(2)}) copy-start(bf16[1,128,2048]{2,1,0:T(8,128)(2,1)} %param.15) | copy-start | bytes 1572868
  21.7 12.0 %collective-permute-start.10 = (bf16[2,64,2048]{2,1,0:T(8,128)(2,1)S(1)}, bf16[2,64,2048]{2,1,0:T(8,128)(2,1)}, u32[]{:S(2)}, u32[]{:S(2)}) collective-permute-start(bf16[2,64,2048]{2,1,0:T(8,128)(2,1)S(1)} %collective-permute-done.2.refs_1_), channel_id=1, source_target_pairs={{0,28},{4,0},{8,4},{12,8},{16,12},{20,16},{24,20},{28,24},{1,29},{... | collective-permute-start | bytes 1572872 | tf_op jit(solution)/shard_map/ppermute | solution.py:240
  24.1 12.6 %collective-permute-start.9 = (bf16[2,64,2048]{2,1,0:T(8,128)(2,1)S(1)}, bf16[2,64,2048]{2,1,0:T(8,128)(2,1)}, u32[]{:S(2)}, u32[]{:S(2)}) collective-permute-start(bf16[2,64,2048]{2,1,0:T(8,128)(2,1)S(1)} %collective-permute-done.2.refs_1_), channel_id=1, source_target_pairs={{0,4},{4,8},{8,12},{12,16},{16,20},{20,24},{24,28},{28,0},{1,5},{5... | collective-permute-start | bytes 1572872 | tf_op jit(solution)/shard_map/ppermute | solution.py:239
  24.1 23.7 %collective-permute-start.3 = (bf16[2,64,2048]{2,1,0:T(8,128)(2,1)S(1)}, bf16[2,64,2048]{2,1,0:T(8,128)(2,1)S(1)}, u32[]{:S(2)}, u32[]{:S(2)}) collective-permute-start(bf16[2,64,2048]{2,1,0:T(8,128)(2,1)S(1)} %collective-permute-done.refs_0_), channel_id=1, source_target_pairs={{0,4},{4,8},{8,12},{12,16},{16,20},{20,24},{24,28},{28,0},{1,5},{5... | collective-permute-start | bytes 1572872 | tf_op jit(solution)/shard_map/ppermute | solution.py:239
  24.2 23.7 %collective-permute-start.6 = (bf16[2,64,2048]{2,1,0:T(8,128)(2,1)}, bf16[2,64,2048]{2,1,0:T(8,128)(2,1)}, u32[]{:S(2)}, u32[]{:S(2)}) collective-permute-start(bf16[2,64,2048]{2,1,0:T(8,128)(2,1)} %collective-permute-done.1.refs_1_), channel_id=1, source_target_pairs={{0,28},{4,0},{8,4},{12,8},{16,12},{20,16},{24,20},{28,24},{1,29},{... | collective-permute-start | bytes 1572872 | tf_op jit(solution)/shard_map/ppermute | solution.py:240
  28.9 1.4 copy-start.7
  30.3 1.4 copy-start.9
  36.7 22.5 %collective-permute-start.13 = (bf16[2,64,2048]{2,1,0:T(8,128)(2,1)}, bf16[2,64,2048]{2,1,0:T(8,128)(2,1)}, u32[]{:S(2)}, u32[]{:S(2)}) collective-permute-start(bf16[2,64,2048]{2,1,0:T(8,128)(2,1)} %collective-permute-done.9.refs_2_), channel_id=1, source_target_pairs={{0,4},{4,8},{8,12},{12,16},{16,20},{20,24},{24,28},{28,0},{1,5},{5... | collective-permute-start | bytes 1572872 | tf_op jit(solution)/shard_map/ppermute | solution.py:239
  36.7 22.5 %collective-permute-start.14 = (bf16[2,64,2048]{2,1,0:T(8,128)(2,1)}, bf16[2,64,2048]{2,1,0:T(8,128)(2,1)}, u32[]{:S(2)}, u32[]{:S(2)}) collective-permute-start(bf16[2,64,2048]{2,1,0:T(8,128)(2,1)} %collective-permute-done.10.refs_3_), channel_id=1, source_target_pairs={{0,28},{4,0},{8,4},{12,8},{16,12},{20,16},{24,20},{28,24},{1,29},{... | collective-permute-start | bytes 1572872 | tf_op jit(solution)/shard_map/ppermute | solution.py:240
  39.4 54.0 %all-to-all-start = ((f32[8,2,512,128]{3,2,1,0:T(8,128)}), f32[8,2,512,128]{3,2,1,0:T(8,128)}, u32[]{:S(2)}, u32[]{:S(2)}) async-start(f32[8,2,512,128]{3,2,1,0:T(8,128)} %copy-done), calls=%async_computation | async-start | bytes 8388608 | tf_op jit(solution)/shard_map/all_to_all | solution.py:246
  47.9 22.6 %collective-permute-start.4 = (bf16[2,64,2048]{2,1,0:T(8,128)(2,1)S(1)}, bf16[2,64,2048]{2,1,0:T(8,128)(2,1)S(1)}, u32[]{:S(2)}, u32[]{:S(2)}) collective-permute-start(bf16[2,64,2048]{2,1,0:T(8,128)(2,1)S(1)} %collective-permute-done.3.refs_0_), channel_id=1, source_target_pairs={{0,4},{4,8},{8,12},{12,16},{16,20},{20,24},{24,28},{28,0},{1,5},{5... | collective-permute-start | bytes 1572872 | tf_op jit(solution)/shard_map/ppermute | solution.py:239
  47.9 22.7 %collective-permute-start.7 = (bf16[2,64,2048]{2,1,0:T(8,128)(2,1)}, bf16[2,64,2048]{2,1,0:T(8,128)(2,1)S(1)}, u32[]{:S(2)}, u32[]{:S(2)}) collective-permute-start(bf16[2,64,2048]{2,1,0:T(8,128)(2,1)} %collective-permute-done.6.refs_1_), channel_id=1, source_target_pairs={{0,28},{4,0},{8,4},{12,8},{16,12},{20,16},{24,20},{28,24},{1,29},{... | collective-permute-start | bytes 1572872 | tf_op jit(solution)/shard_map/ppermute | solution.py:240
  50.5 1.6 copy-start.8
  52.1 1.6 copy-start.10
  59.2 22.5 %collective-permute-start.15 = (bf16[2,64,2048]{2,1,0:T(8,128)(2,1)}, bf16[2,64,2048]{2,1,0:T(8,128)(2,1)S(1)}, u32[]{:S(2)}, u32[]{:S(2)}) collective-permute-start(bf16[2,64,2048]{2,1,0:T(8,128)(2,1)} %collective-permute-done.13.refs_2_), channel_id=1, source_target_pairs={{0,4},{4,8},{8,12},{12,16},{16,20},{20,24},{24,28},{28,0},{1,5},{5... | collective-permute-start | bytes 1572872 | tf_op jit(solution)/shard_map/ppermute | solution.py:239
  59.2 22.5 %collective-permute-start.16 = (bf16[2,64,2048]{2,1,0:T(8,128)(2,1)}, bf16[2,64,2048]{2,1,0:T(8,128)(2,1)S(1)}, u32[]{:S(2)}, u32[]{:S(2)}) collective-permute-start(bf16[2,64,2048]{2,1,0:T(8,128)(2,1)} %collective-permute-done.14.refs_3_), channel_id=1, source_target_pairs={{0,28},{4,0},{8,4},{12,8},{16,12},{20,16},{24,20},{28,24},{1,29},{... | collective-permute-start | bytes 1572872 | tf_op jit(solution)/shard_map/ppermute | solution.py:240
  70.5 23.0 %collective-permute-start.5 = (bf16[2,32,2048]{2,1,0:T(8,128)(2,1)S(1)}, bf16[2,32,2048]{2,1,0:T(8,128)(2,1)S(1)}, u32[]{:S(2)}, u32[]{:S(2)}) collective-permute-start(bf16[2,32,2048]{2,1,0:T(8,128)(2,1)S(1)} %slice.16), channel_id=1, source_target_pairs={{0,4},{4,8},{8,12},{12,16},{16,20},{20,24},{24,28},{28,0},{1,5},{5... | collective-permute-start | bytes 786440 | tf_op jit(solution)/shard_map/ppermute | solution.py:239
  71.3 22.2 %collective-permute-start.8 = (bf16[2,32,2048]{2,1,0:T(8,128)(2,1)}, bf16[2,32,2048]{2,1,0:T(8,128)(2,1)S(1)}, u32[]{:S(2)}, u32[]{:S(2)}) collective-permute-start(bf16[2,32,2048]{2,1,0:T(8,128)(2,1)} %slice.17), channel_id=1, source_target_pairs={{0,28},{4,0},{8,4},{12,8},{16,12},{20,16},{24,20},{28,24},{1,29},{... | collective-permute-start | bytes 786440 | tf_op jit(solution)/shard_map/ppermute | solution.py:240
  81.7 11.2 %collective-permute-start.17 = (bf16[2,32,2048]{2,1,0:T(8,128)(2,1)S(1)}, bf16[2,32,2048]{2,1,0:T(8,128)(2,1)S(1)}, u32[]{:S(2)}, u32[]{:S(2)}) collective-permute-start(bf16[2,32,2048]{2,1,0:T(8,128)(2,1)S(1)} %slice.14), channel_id=1, source_target_pairs={{0,4},{4,8},{8,12},{12,16},{16,20},{20,24},{24,28},{28,0},{1,5},{5... | collective-permute-start | bytes 786440 | tf_op jit(solution)/shard_map/ppermute | solution.py:239
  82.5 11.0 %collective-permute-start.18 = (bf16[2,32,2048]{2,1,0:T(8,128)(2,1)}, bf16[2,32,2048]{2,1,0:T(8,128)(2,1)S(1)}, u32[]{:S(2)}, u32[]{:S(2)}) collective-permute-start(bf16[2,32,2048]{2,1,0:T(8,128)(2,1)} %slice.15), channel_id=1, source_target_pairs={{0,28},{4,0},{8,4},{12,8},{16,12},{20,16},{24,20},{28,24},{1,29},{... | collective-permute-start | bytes 786440 | tf_op jit(solution)/shard_map/ppermute | solution.py:240
  87.6 1.4 copy-start.11
  88.9 1.4 copy-start.13
  93.5 1.6 copy-start.12
  95.1 1.6 copy-start.14
  96.7 7.3 %copy-start.5 = (bf16[1,2048,128]{2,1,0:T(8,128)(2,1)S(1)}, bf16[1,2048,128]{2,1,0:T(8,128)(2,1)}, u32[]{:S(2)}) copy-start(bf16[1,2048,128]{2,1,0:T(8,128)(2,1)} %du_ref.1) | copy-start | bytes 1572868
  96.7 7.3 %copy-start.6 = (bf16[1,128,2048]{2,1,0:T(8,128)(2,1)S(1)}, bf16[1,128,2048]{2,1,0:T(8,128)(2,1)}, u32[]{:S(2)}) copy-start(bf16[1,128,2048]{2,1,0:T(8,128)(2,1)} %dd_ref.1) | copy-start | bytes 1572868
  98.5 5.4 %collective-permute-start.19 = (bf16[2,128,2048]{2,1,0:T(8,128)(2,1)S(1)}, bf16[2,128,2048]{2,1,0:T(8,128)(2,1)S(1)}, u32[]{:S(2)}, u32[]{:S(2)}) collective-permute-start(bf16[2,128,2048]{2,1,0:T(8,128)(2,1)S(1)} %get-tuple-element.62), channel_id=1, source_target_pairs={{0,1},{1,0},{2,3},{3,2},{4,5},{5,4},{6,7},{7,6},{8,9},{9,8},{10,11... | collective-permute-start | bytes 3145736 | tf_op jit(solution)/shard_map/ppermute | solution.py:256
  105.6 6.5 %copy-start.17 = (s32[16]{0:T(128)S(1)}, s32[16]{0:T(128)}, u32[]{:S(2)}) copy-start(s32[16]{0:T(128)} %param.19) | copy-start | bytes 196
  105.6 6.5 %copy-start.18 = (s32[8]{0:T(128)S(1)}, s32[8]{0:T(128)}, u32[]{:S(2)}) copy-start(s32[8]{0:T(128)} %param.18) | copy-start | bytes 100
  105.6 21.0 %all-to-all-start.1 = ((bf16[8,512,128]{2,1,0:T(8,128)(2,1)}), bf16[8,512,128]{2,1,0:T(8,128)(2,1)S(1)}, u32[]{:S(2)}, u32[]{:S(2)}) async-start(bf16[8,512,128]{2,1,0:T(8,128)(2,1)} %shard_map.153), calls=%async_computation.1 | async-start | bytes 2097152 | tf_op jit(solution)/shard_map/all_to_all | solution.py:258

commit v3 on v2

v3 whole, which is shorter than its diff:
```python
import functools
import math

import jax
import jax.numpy as jnp
from jax import lax
from jax.experimental import pallas as pl
from jax.experimental.pallas import tpu as pltpu
from jax.sharding import Mesh
from jax.sharding import PartitionSpec as P

D = 2048
FF = 4096
REGION = ("xh", "y")
DEV = ("z", "xl", "c")
NR = 8
BF = jnp.bfloat16
F32 = jnp.float32
MIB = 1 << 20


def params(mib=16):
    return pltpu.CompilerParams(vmem_limit_bytes=mib * MIB)


def whole(count):
    return [pl.BlockSpec(memory_space=pltpu.VMEM)] * count


def grads_kernel(n_blocks, *refs):
    blocks = refs[:n_blocks]
    x_ref, g_ref, up_ref, down_ref, out_ref = refs[n_blocks:]
    x = jnp.concatenate([b[0] for b in blocks] + [x_ref[0]], axis=0)
    g = jnp.concatenate([b[1] for b in blocks] + [g_ref[0]], axis=0)
    root = math.sqrt(2.0 / math.pi)
    hid = jnp.dot(x, up_ref[...], preferred_element_type=F32) * D ** (-0.5)
    dact = lax.dot_general(
        g, down_ref[...], (((1,), (1,)), ((), ())), preferred_element_type=F32
    ) * FF ** (-0.5)
    sq = hid * hid
    t = jnp.tanh(root * (hid + 0.044715 * (sq * hid)))
    act = (0.5 * hid * (1.0 + t)).astype(BF)
    slope = 0.5 * (1.0 + t) + 0.5 * hid * (1.0 - t * t) * (root * (1.0 + 3 * 0.044715 * sq))
    dhid = (dact * slope).astype(BF)
    for i, (left, right, scale) in enumerate(((act, g, FF), (dhid, x, D))):
        total = lax.dot_general(left, right, (((0,), (0,)), ((), ())), preferred_element_type=F32)
        out_ref[i] = (total * (0.5 * scale ** (-0.5))).astype(out_ref.dtype)


def grads(blocks, last_x, last_g, up2, down2, dtype):
    return pl.pallas_call(
        functools.partial(grads_kernel, len(blocks)),
        out_shape=jax.ShapeDtypeStruct((2, 256, D), dtype),
        in_specs=whole(len(blocks) + 4),
        out_specs=pl.BlockSpec(memory_space=pltpu.VMEM),
        compiler_params=params(24),
        cost_estimate=pl.CostEstimate(
            flops=8 * 512 * D * 256, bytes_accessed=8 * MIB, transcendentals=512 * 256
        ),
    )(*blocks, last_x, last_g, up2, down2)


def down_in(eighth):
    return jnp.concatenate([eighth[:, j * 128 : (j + 1) * 128] for j in range(16)], axis=0)


def pseudo_kernel(side_ref, kept_ref, got_ref, du_ref, dd_ref, out_ref):
    side = side_ref[0]
    for part in range(2):
        at = side if part == 0 else 1 - side
        cut = slice(part * 128, part * 128 + 128)
        down = kept_ref[0, cut] + got_ref[0, cut].astype(F32)
        if part == 0:
            down = down + dd_ref[0].astype(F32)
        down = down.astype(BF)
        up = kept_ref[1, cut] + got_ref[1, cut].astype(F32)
        for r in range(NR):
            mine = up[:, r * 256 : (r + 1) * 256].T
            if part == 0:
                mine = mine + du_ref[0, r * 256 : (r + 1) * 256, :].astype(F32)
            out_ref[2 * r + at, 0:256, :] = mine.astype(BF)
            out_ref[2 * r + at, 256:512, :] = down_in(down[r * 16 : (r + 1) * 16, :])


def pseudo(side, kept, got, drift_up, drift_down):
    return pl.pallas_call(
        pseudo_kernel,
        out_shape=jax.ShapeDtypeStruct((2 * NR, 512, 128), BF),
        in_specs=[pl.BlockSpec(memory_space=pltpu.SMEM)] + whole(4),
        out_specs=pl.BlockSpec(memory_space=pltpu.VMEM),
        compiler_params=params(24),
    )(side, kept, got, drift_up, drift_down)


def state_kernel(gu_ref, gd_ref, mu_ref, md_ref, out_ref):
    for s in range(2):
        out_ref[0, s, 0:256, :] = gu_ref[s].astype(F32) - 0.567 * mu_ref[s]
        out_ref[0, s, 256:512, :] = down_in(gd_ref[s].astype(F32) - 0.567 * md_ref[s])


def state(global_up, global_down, mom_up, mom_down):
    up = pl.BlockSpec((2, 256, 128), lambda i: (0, i, 0))
    down = pl.BlockSpec((2, 16, D), lambda i: (0, i, 0))
    return pl.pallas_call(
        state_kernel,
        grid=(NR,),
        out_shape=jax.ShapeDtypeStruct((NR, 2, 512, 128), F32),
        in_specs=[up, down, up, down],
        out_specs=pl.BlockSpec((1, 2, 512, 128), lambda i: (i, 0, 0, 0)),
        compiler_params=params(),
        cost_estimate=pl.CostEstimate(flops=4 * MIB, bytes_accessed=10 * MIB, transcendentals=0),
    )(global_up, global_down, mom_up, mom_down)


def step_kernel(target_ref, factor_ref, p_ref, a_ref, out_ref, sum_ref):
    sum_ref[...] = jnp.zeros_like(sum_ref)
    for r in range(NR):
        at = target_ref[r]
        both = p_ref[2 * r].astype(F32) + p_ref[2 * r + 1].astype(F32)
        sum_ref[at] = sum_ref[at] + both
    for o in range(NR):
        for s in range(2):
            slot = 2 * o + s
            out_ref[o, s] = (a_ref[o, s] - factor_ref[slot] * sum_ref[slot]).astype(BF)
    for r in range(NR):
        at = target_ref[r]
        out_ref[r, 2] = out_ref[at // 2, at % 2]


def step(target, factor, pieces, base):
    rows = 128
    return pl.pallas_call(
        step_kernel,
        grid=(512 // rows,),
        out_shape=jax.ShapeDtypeStruct((NR, 3, 512, 128), BF),
        in_specs=[
            pl.BlockSpec(memory_space=pltpu.SMEM),
            pl.BlockSpec(memory_space=pltpu.SMEM),
            pl.BlockSpec((2 * NR, rows, 128), lambda i: (0, i, 0)),
            pl.BlockSpec((NR, 2, rows, 128), lambda i: (0, 0, i, 0)),
        ],
        out_specs=pl.BlockSpec((NR, 3, rows, 128), lambda i: (0, 0, i, 0)),
        scratch_shapes=[pltpu.VMEM((16, rows, 128), F32)],
        compiler_params=params(16),
    )(target, factor, pieces, base)


def place_kernel(got_ref, nu_ref, nd_ref, ru_ref, rd_ref):
    for p in range(2):
        up, down = slice(p * 256, p * 256 + 256), slice(p * 16, p * 16 + 16)
        for s in range(3):
            to_up, to_down = (nu_ref, nd_ref) if s < 2 else (ru_ref, rd_ref)
            to_up[s % 2, up] = got_ref[p, s, 0:256]
            to_down[s % 2, down] = jnp.concatenate(
                [got_ref[p, s, 256 + j * 16 : 272 + j * 16, :] for j in range(16)], axis=1
            )


def place(got):
    def up(n):
        return pl.BlockSpec((n, 512, 128), lambda i: (0, i, 0))

    def down(n):
        return pl.BlockSpec((n, 32, D), lambda i: (0, i, 0))

    return pl.pallas_call(
        place_kernel,
        grid=(NR // 2,),
        out_shape=(
            jax.ShapeDtypeStruct((2, D, 128), BF),
            jax.ShapeDtypeStruct((2, 128, D), BF),
            jax.ShapeDtypeStruct((1, D, 128), BF),
            jax.ShapeDtypeStruct((1, 128, D), BF),
        ),
        in_specs=[pl.BlockSpec((2, 3, 512, 128), lambda i: (i, 0, 0, 0))],
        out_specs=(up(2), down(2), up(1), down(1)),
        compiler_params=params(16),
    )(got)


RIGHT = [(i, (i + 1) % 8) for i in range(8)]
LEFT = [(i, (i + 7) % 8) for i in range(8)]
SWAP = [(0, 1), (1, 0)]


def on_device(
    acts,
    cotan,
    w_up,
    w_down,
    drift_up,
    drift_down,
    path,
    slot_of,
    global_up,
    global_down,
    mom_up,
    mom_down,
):
    module_ids = jnp.arange(slot_of.shape[0], dtype=jnp.int32)
    target = jnp.sum(jnp.where(path[:, None] == module_ids[None, :], slot_of[None, :], 0), axis=1)
    chosen = (target[:, None] == module_ids[None, :]).astype(F32)
    factor = 1.33 / jnp.maximum(jnp.sum(chosen, axis=0), 1.0)

    beside = [lax.ppermute(w, "xl", SWAP) for w in (w_up, w_down)]
    across = [lax.ppermute(w, "c", SWAP) for w in (w_up, w_down)]
    base = state(global_up, global_down, mom_up, mom_down)
    own = jnp.concatenate([acts, cotan], axis=0)
    right = left = own
    blocks = [own]
    for hop in range(3):
        right, left = lax.ppermute(right, "z", RIGHT), lax.ppermute(left, "z", LEFT)
        if hop == 0:
            right, left, base = lax.optimization_barrier((right, left, base))
        here = (right, left)
        if hop == 0:
            beside[1], base = lax.optimization_barrier((beside[1], base))
            base = lax.all_to_all(base, REGION, 0, 0, tiled=True)
        if hop == 1:
            right, left, beside[0] = lax.optimization_barrier((right, left, beside[0]))
        blocks += here
    corner = [lax.ppermute(w, "c", SWAP) for w in beside]
    mine = (jnp.concatenate([w_up[0], beside[0][0]], axis=1), jnp.concatenate([w_down[0], beside[1][0]], axis=0))
    theirs = (
        jnp.concatenate([across[0][0], corner[0][0]], axis=1),
        jnp.concatenate([across[1][0], corner[1][0]], axis=0),
    )
    last_x = lax.ppermute(right[0:1], "z", RIGHT)
    last_g = lax.ppermute(left[1:2], "z", LEFT)
    sent = grads(blocks, last_x, last_g, *theirs, BF)
    got = lax.ppermute(sent, "c", SWAP)
    kept = grads(blocks, last_x, last_g, *mine, F32)

    side = lax.axis_index("xl").astype(jnp.int32)[None]
    pieces = pseudo(side, kept, got, drift_up, drift_down)
    pieces = lax.all_to_all(pieces, REGION + ("xl",), 0, 0, tiled=True)
    reply = step(target, factor, pieces, base)
    reply = lax.all_to_all(reply, REGION, 0, 0, tiled=True)
    return place(reply)


def solution(mesh):
    fine = Mesh(mesh.devices.reshape(2, 4, 8, 2, 2), REGION + DEV)
    rows = P(REGION, DEV, None)
    cols = P(REGION, None, DEV)
    return jax.shard_map(
        on_device,
        mesh=fine,
        in_specs=(rows, rows, cols, rows, cols, rows, P(), P(), cols, rows, cols, rows),
        out_specs=(cols, rows, cols, rows),
        check_vma=False,
    )
```

time: 177 us -> 165 us (0.932)
  local copies, waits for them, and re-layouts: 22.9 us -> 9.74 us
  starting transfers between devices: 43.6 us -> 36.3 us
  waiting for transfers between devices: 42.5 us -> 49.1 us
  blocking collectives: 43.5 us -> 47 us
  Pallas kernels: 22 us -> 19.7 us
    all_to_all x1, waiting for transfers between devices: 14.2 us -> 26.6 us  [on_device(): pieces = lax.all_to_all(pieces, REGION + ('xl',), 0, 0, tiled=True)]
    unnamed x39 -> x29, local copies, waits for them, and re-layouts: 20.4 us -> 8.73 us
    ppermute x19 -> x14, waiting for transfers between devices: 25.5 us -> 16.4 us  [the longest x3 7.18 us: on_device(): lax.ppermute(right, 'z', RIGHT)]
    all_to_all x1, waiting for transfers between devices: 0.55 us -> 6.12 us  [on_device(): base = lax.all_to_all(base, REGION, 0, 0, tiled=True)]
    all_to_all x1, blocking collectives: 43.5 us -> 47 us  [on_device(): reply = lax.all_to_all(reply, REGION, 0, 0, tiled=True)]
    ppermute x19 -> x14, starting transfers between devices: 27.6 us -> 24.4 us  [the longest x3 8.37 us: on_device(): lax.ppermute(left, 'z', LEFT)]
    ppermute x1, starting transfers between devices: 3.15 us -> 0.68 us  [on_device(): got = lax.ppermute(sent, 'c', SWAP)]
    pallas_call x6 -> x3, Pallas kernels: 15.2 us -> 12.8 us  [the longest x2 8.96 us: grads(): pl.pallas_call(functools.partial(grads_kernel, len(blocks)), out_shape=ja...]
  transfers between devices with their start and end apart: 22 -> 17, of which waited for: 11 -> 7; matrix products, arithmetic and copies ran while one was open for 1% -> 1% of each run, Pallas kernels for 7% -> 8%
where the time goes in v3:
time: 165 us
  waiting for transfers between devices  49.1 us (30%)
  blocking collectives  47 us (28%)
  starting transfers between devices  36.3 us (22%)
  Pallas kernels  19.7 us (12%)
  local copies, waits for them, and re-layouts  9.74 us (6%)
  other arithmetic  2.02 us (1%)
    all_to_all x1, blocking collectives, on_device(): reply = lax.all_to_all(reply, REGION, 0, 0, tiled=True)  47 us
    all_to_all x1, waiting for transfers between devices, on_device(): pieces = lax.all_to_all(pieces, REGION + ('xl',), 0, 0, tiled=True)  26.6 us
    pallas_call x2, Pallas kernels, grads(): pl.pallas_call(functools.partial(grads_kernel, len(blocks)), out_shape=ja...  8.96 us
    unnamed x29, local copies, waits for them, and re-layouts  8.73 us
    ppermute x3, starting transfers between devices, on_device(): lax.ppermute(left, 'z', LEFT)  8.37 us
    ppermute x3, waiting for transfers between devices, on_device(): lax.ppermute(right, 'z', RIGHT)  7.18 us
    all_to_all x1, starting transfers between devices, on_device(): base = lax.all_to_all(base, REGION, 0, 0, tiled=True)  6.65 us
    all_to_all x1, waiting for transfers between devices, on_device(): base = lax.all_to_all(base, REGION, 0, 0, tiled=True)  6.12 us
  transfers between devices with their start and end apart: 17, of which 7 were waited for; matrix products, arithmetic and copies ran while one was open for 1% of the time, Pallas kernels for 8%

profile of v3, /device:TPU:1, one launch (start us, length us, event | category | flops | bytes accessed | tf_op | source)
XLA Modules:
  0.0 164.8 jit_solution(11810936098468759950)
XLA Ops:
  0.6 1.0 constant_dynamic-update-slice_fusion.1
  1.6 1.0 constant_dynamic-update-slice_fusion.refs_0_
  2.6 2.5 %collective-permute-start = (bf16[2,64,2048]{2,1,0:T(8,128)(2,1)S(1)}, bf16[2,64,2048]{2,1,0:T(8,128)(2,1)S(1)}, u32[]{:S(2)}, u32[]{:S(2)}) collective-permute-start(bf16[2,64,2048]{2,1,0:T(8,128)(2,1)S(1)} %constant_dynamic-update-slice_fusion.refs_0_), channel_id=1, source_target_pairs={{0,4},{4,8},{8,12},{12,16},{16,20},{20,24},{24,28},{28,0},{1,5},{5... | collective-permute-start | bytes 1572872 | tf_op jit(solution)/shard_map/ppermute | solution.py:212
  5.1 4.0 %collective-permute-start.1 = (bf16[2,64,2048]{2,1,0:T(8,128)(2,1)S(1)}, bf16[2,64,2048]{2,1,0:T(8,128)(2,1)S(1)}, u32[]{:S(2)}, u32[]{:S(2)}) collective-permute-start(bf16[2,64,2048]{2,1,0:T(8,128)(2,1)S(1)} %constant_dynamic-update-slice_fusion.refs_0_), channel_id=1, source_target_pairs={{0,28},{4,0},{8,4},{12,8},{16,12},{20,16},{24,20},{28,24},{1,29},{... | collective-permute-start | bytes 1572872 | tf_op jit(solution)/shard_map/ppermute | solution.py:212
  9.1 1.2 collective-permute-start.9
  10.4 0.3 collective-permute-start.4
  10.6 1.6 copy-done.1
  12.2 1.6 copy-done.2
  13.8 1.2 copy-done.3
  15.0 1.2 copy-done.4
  16.2 1.0 shard_map.147
  17.3 0.0 copy-start
  17.3 2.0 %copy-done = f32[8,2,512,128]{3,2,1,0:T(8,128)} copy-done((f32[8,2,512,128]{3,2,1,0:T(8,128)}, f32[8,2,512,128]{3,2,1,0:T(8,128)S(1)}, u32[]{:S(2)}) %copy-start) | copy-done | bytes 4194328
  19.3 1.4 collective-permute-done.refs_1_
  20.7 0.0 collective-permute-done.1.refs_2_
  20.7 0.0 collective-permute-start.2
  20.7 2.7 %collective-permute-start.3 = (bf16[2,64,2048]{2,1,0:T(8,128)(2,1)S(1)}, bf16[2,64,2048]{2,1,0:T(8,128)(2,1)}, u32[]{:S(2)}, u32[]{:S(2)}) collective-permute-start(bf16[2,64,2048]{2,1,0:T(8,128)(2,1)S(1)} %collective-permute-done.1.refs_2_), channel_id=1, source_target_pairs={{0,28},{4,0},{8,4},{12,8},{16,12},{20,16},{24,20},{28,24},{1,29},{... | collective-permute-start | bytes 1572872 | tf_op jit(solution)/shard_map/ppermute | solution.py:212
  23.4 0.0 collective-permute-done.9
  23.4 6.7 %all-to-all-start.1 = ((f32[8,2,512,128]{3,2,1,0:T(8,128)}), f32[8,2,512,128]{3,2,1,0:T(8,128)}, u32[]{:S(2)}, u32[]{:S(2)}) async-start(f32[8,2,512,128]{3,2,1,0:T(8,128)} %copy-done), calls=%async_computation.1 | async-start | bytes 8388608 | tf_op jit(solution)/shard_map/all_to_all | solution.py:218
  30.0 3.1 %collective-permute-done.4 = bf16[1,2048,128]{2,1,0:T(8,128)(2,1)S(1)} collective-permute-done((bf16[1,2048,128]{2,1,0:T(8,128)(2,1)}, bf16[1,2048,128]{2,1,0:T(8,128)(2,1)S(1)}, u32[]{:S(2)}, u32[]{:S(2)}) %collective-permute-start.4) | collective-permute-done | bytes 524320 | tf_op jit(solution)/shard_map/ppermute | solution.py:205
  33.2 0.9 collective-permute-done.2.refs_3_
  34.1 0.0 copy-done.10
  34.1 0.0 collective-permute-done.3.refs_4_
  34.1 1.0 collective-permute-start.5
  35.1 1.7 %collective-permute-start.6 = (bf16[2,64,2048]{2,1,0:T(8,128)(2,1)}, bf16[2,64,2048]{2,1,0:T(8,128)(2,1)S(1)}, u32[]{:S(2)}, u32[]{:S(2)}) collective-permute-start(bf16[2,64,2048]{2,1,0:T(8,128)(2,1)} %collective-permute-done.3.refs_4_), channel_id=1, source_target_pairs={{0,28},{4,0},{8,4},{12,8},{16,12},{20,16},{24,20},{28,24},{1,29},{... | collective-permute-start | bytes 1572872 | tf_op jit(solution)/shard_map/ppermute | solution.py:212
  36.8 3.6 %collective-permute-start.12 = (bf16[1,128,2048]{2,1,0:T(8,128)(2,1)}, bf16[1,128,2048]{2,1,0:T(8,128)(2,1)S(1)}, u32[]{:S(2)}, u32[]{:S(2)}) collective-permute-start(bf16[1,128,2048]{2,1,0:T(8,128)(2,1)} %param.15), channel_id=1, source_target_pairs={{0,1},{1,0},{2,3},{3,2},{4,5},{5,4},{6,7},{7,6},{8,9},{9,8},{10,11... | collective-permute-start | bytes 1572872 | tf_op jit(solution)/shard_map/ppermute | solution.py:206
  40.4 0.0 collective-permute-start.13
  40.4 0.5 collective-permute-start.10
  40.9 4.8 %collective-permute-done.5.refs_5_ = bf16[2,64,2048]{2,1,0:T(8,128)(2,1)S(1)} collective-permute-done((bf16[2,64,2048]{2,1,0:T(8,128)(2,1)S(1)}, bf16[2,64,2048]{2,1,0:T(8,128)(2,1)S(1)}, u32[]{:S(2)}, u32[]{:S(2)}) %collective-permute-start.5) | collective-permute-done | bytes 524320 | tf_op jit(solution)/shard_map/ppermute | solution.py:212
  45.8 3.9 %collective-permute-start.11 = (bf16[1,2048,128]{2,1,0:T(8,128)(2,1)}, bf16[1,2048,128]{2,1,0:T(8,128)(2,1)S(1)}, u32[]{:S(2)}, u32[]{:S(2)}) collective-permute-start(bf16[1,2048,128]{2,1,0:T(8,128)(2,1)} %copy-done.10), channel_id=1, source_target_pairs={{0,1},{1,0},{2,3},{3,2},{4,5},{5,4},{6,7},{7,6},{8,9},{9,8},{10,11... | collective-permute-start | bytes 1572872 | tf_op jit(solution)/shard_map/ppermute | solution.py:222
  49.7 0.0 collective-permute-done.6.refs_6_
  49.7 0.1 collective-permute-start.7
  49.8 0.0 collective-permute-done.12
  49.8 2.9 %collective-permute-start.8 = (bf16[1,64,2048]{2,1,0:T(8,128)(2,1)S(1)}, bf16[1,64,2048]{2,1,0:T(8,128)(2,1)S(1)}, u32[]{:S(2)}, u32[]{:S(2)}) collective-permute-start(bf16[1,64,2048]{2,1,0:T(8,128)(2,1)S(1)} %slice.9), channel_id=1, source_target_pairs={{0,28},{4,0},{8,4},{12,8},{16,12},{20,16},{24,20},{28,24},{1,29},{... | collective-permute-start | bytes 786440 | tf_op jit(solution)/shard_map/ppermute | solution.py:229
  52.7 0.0 collective-permute-done.13
  52.7 0.1 pad_maximum_fusion.3.refs_10_
  52.9 0.0 collective-permute-done.10
  52.9 0.0 collective-permute-done.11
  52.9 0.1 pad_maximum_fusion.2.refs_9_
  53.0 6.0 %collective-permute-done.7.refs_7_ = bf16[1,64,2048]{2,1,0:T(8,128)(2,1)S(1)} collective-permute-done((bf16[1,64,2048]{2,1,0:T(8,128)(2,1)S(1)}, bf16[1,64,2048]{2,1,0:T(8,128)(2,1)S(1)}, u32[]{:S(2)}, u32[]{:S(2)}) %collective-permute-start.7) | collective-permute-done | bytes 262176 | tf_op jit(solution)/shard_map/ppermute | solution.py:228
  59.0 0.0 collective-permute-done.8.refs_8_
  59.0 5.2 %shard_map.149 = bf16[2,256,2048]{2,1,0:T(8,128)(2,1)} custom-call(bf16[2,64,2048]{2,1,0:T(8,128)(2,1)S(1)} %constant_dynamic-update-slice_fusion.refs_0_, bf16[2,64,2048]{2,1,0:T(8,128)(2,1)S(1)} %collective-permute-done.refs_1_, bf16[2,64,2048]{2,1,0:T(8,128)(2,1)S(1)} %collective-permute-done.1.refs_2_, ...), custom_call_target="tpu_custom_call" | custom-call | flops 2147483648 | bytes 8388608 | tf_op jit(solution)/shard_map/pallas_call | solution.py:51
  64.2 0.0 copy-done.5
  64.2 0.7 collective-permute-start.14
  64.9 1.4 pad_maximum_fusion.1.refs_10_
  66.3 0.0 copy-done.9
  66.3 0.1 copy-done.11
  66.4 0.1 pad_maximum_fusion.refs_9_
  66.5 0.0 copy-done.6
  66.5 0.0 copy-start.7
  66.5 0.0 copy-start.8
  66.5 3.8 %shard_map.148.kept_ref = f32[2,256,2048]{2,1,0:T(8,128)S(1)} custom-call(bf16[2,64,2048]{2,1,0:T(8,128)(2,1)S(1)} %constant_dynamic-update-slice_fusion.refs_0_, bf16[2,64,2048]{2,1,0:T(8,128)(2,1)S(1)} %collective-permute-done.refs_1_, bf16[2,64,2048]{2,1,0:T(8,128)(2,1)S(1)} %collective-permute-done.1.refs_2_, ...), custom_call_target="tpu_custom_call" | custom-call | flops 2147483648 | bytes 8388608 | tf_op jit(solution)/shard_map/pallas_call | solution.py:51
  70.4 0.0 collective-permute-done.14.got_ref
  70.4 0.0 copy-done.7
  70.4 0.0 copy-done.8
  70.4 3.8 %shard_map.150 = bf16[16,512,128]{2,1,0:T(8,128)(2,1)} custom-call(s32[1]{0:T(128)} %bitcast.side_ref, f32[2,256,2048]{2,1,0:T(8,128)S(1)} %shard_map.148.kept_ref, bf16[2,256,2048]{2,1,0:T(8,128)(2,1)} %collective-permute-done.14.got_ref, bf16[1,2048,128]{2,1,0:T(8,128)(2,1)S(1)} %copy-done.7, bf16[1,128,2048]{2,1,0:T(8,128)(2,1)S(1)} %copy-done.8), custom_call_target="tpu_custom_call" | custom-call | tf_op jit(solution)/shard_map/pallas_call | solution.py:86
  74.2 6.1 %all-to-all-done.1.a_ref = f32[8,2,512,128]{3,2,1,0:T(8,128)} async-done(((f32[8,2,512,128]{3,2,1,0:T(8,128)}), f32[8,2,512,128]{3,2,1,0:T(8,128)}, u32[]{:S(2)}, u32[]{:S(2)}) %all-to-all-start.1) | async-done | bytes 4194336 | tf_op jit(solution)/shard_map/all_to_all | solution.py:218
  80.3 4.6 %all-to-all-start = ((bf16[16,512,128]{2,1,0:T(8,128)(2,1)}), bf16[16,512,128]{2,1,0:T(8,128)(2,1)S(1)}, u32[]{:S(2)}, u32[]{:S(2)}) async-start(bf16[16,512,128]{2,1,0:T(8,128)(2,1)} %shard_map.150), calls=%async_computation | async-start | bytes 4194304 | tf_op jit(solution)/shard_map/all_to_all | solution.py:236
  85.0 0.2 select_reduce_fusion.target_ref
  85.1 0.1 convert_reduce_fusion
  85.2 26.6 %all-to-all-done.p_ref = bf16[16,512,128]{2,1,0:T(8,128)(2,1)S(1)} async-done(((bf16[16,512,128]{2,1,0:T(8,128)(2,1)}), bf16[16,512,128]{2,1,0:T(8,128)(2,1)S(1)}, u32[]{:S(2)}, u32[]{:S(2)}) %all-to-all-start) | async-done | bytes 2097184 | tf_op jit(solution)/shard_map/all_to_all | solution.py:236
  111.8 3.8 %shard_map.151 = bf16[8,3,512,128]{3,2,1,0:T(8,128)(2,1)S(1)} custom-call(s32[8]{0:T(128)S(1)} %select_reduce_fusion.target_ref, f32[16]{0:T(128)S(1)} %maximum_divide_fusion.factor_ref, bf16[16,512,128]{2,1,0:T(8,128)(2,1)S(1)} %all-to-all-done.p_ref, f32[8,2,512,128]{3,2,1,0:T(8,128)} %all-to-all-done.1.a_ref), custom_call_target="tpu_custom_call" | custom-call | tf_op jit(solution)/shard_map/pallas_call | solution.py:132
  115.6 47.0 %all_to_all.15.got_ref = bf16[8,3,512,128]{3,2,1,0:T(8,128)(2,1)S(1)} all-to-all(bf16[8,3,512,128]{3,2,1,0:T(8,128)(2,1)S(1)} %shard_map.151), channel_id=1, replica_groups=mesh['xh'=2,'y'=4,'z'=8,'xl'=2,'c'=2] {'xh','y'}, dimensions={0} | all-to-all | bytes 6291456 | tf_op jit(solution)/shard_map/all_to_all | solution.py:238
  162.7 2.1 %shard_map.152 = (bf16[2,2048,128]{2,1,0:T(8,128)(2,1)}, bf16[2,128,2048]{2,1,0:T(8,128)(2,1)}, bf16[1,2048,128]{2,1,0:T(8,128)(2,1)}, bf16[1,128,2048]{2,1,0:T(8,128)(2,1)}) custom-call(bf16[8,3,512,128]{3,2,1,0:T(8,128)(2,1)S(1)} %all_to_all.15.got_ref), custom_call_target="tpu_custom_call" | custom-call | tf_op jit(solution)/shard_map/pallas_call | solution.py:166
  (16 shorter events, 0.1 us)
Async XLA Ops:
  2.6 18.1 %collective-permute-start = (bf16[2,64,2048]{2,1,0:T(8,128)(2,1)S(1)}, bf16[2,64,2048]{2,1,0:T(8,128)(2,1)S(1)}, u32[]{:S(2)}, u32[]{:S(2)}) collective-permute-start(bf16[2,64,2048]{2,1,0:T(8,128)(2,1)S(1)} %constant_dynamic-update-slice_fusion.refs_0_), channel_id=1, source_target_pairs={{0,4},{4,8},{8,12},{12,16},{16,20},{20,24},{24,28},{28,0},{1,5},{5... | collective-permute-start | bytes 1572872 | tf_op jit(solution)/shard_map/ppermute | solution.py:212
  5.1 15.6 %collective-permute-start.1 = (bf16[2,64,2048]{2,1,0:T(8,128)(2,1)S(1)}, bf16[2,64,2048]{2,1,0:T(8,128)(2,1)S(1)}, u32[]{:S(2)}, u32[]{:S(2)}) collective-permute-start(bf16[2,64,2048]{2,1,0:T(8,128)(2,1)S(1)} %constant_dynamic-update-slice_fusion.refs_0_), channel_id=1, source_target_pairs={{0,28},{4,0},{8,4},{12,8},{16,12},{20,16},{24,20},{28,24},{1,29},{... | collective-permute-start | bytes 1572872 | tf_op jit(solution)/shard_map/ppermute | solution.py:212
  9.1 14.2 %collective-permute-start.9 = (bf16[1,128,2048]{2,1,0:T(8,128)(2,1)}, bf16[1,128,2048]{2,1,0:T(8,128)(2,1)}, u32[]{:S(2)}, u32[]{:S(2)}) collective-permute-start(bf16[1,128,2048]{2,1,0:T(8,128)(2,1)} %param.15), channel_id=1, source_target_pairs={{0,2},{2,0},{1,3},{3,1},{4,6},{6,4},{5,7},{7,5},{8,10},{10,8},{9,1... | collective-permute-start | bytes 1572872 | tf_op jit(solution)/shard_map/ppermute | solution.py:205
  10.4 22.8 %collective-permute-start.4 = (bf16[1,2048,128]{2,1,0:T(8,128)(2,1)}, bf16[1,2048,128]{2,1,0:T(8,128)(2,1)S(1)}, u32[]{:S(2)}, u32[]{:S(2)}) collective-permute-start(bf16[1,2048,128]{2,1,0:T(8,128)(2,1)} %param.14), channel_id=1, source_target_pairs={{0,2},{2,0},{1,3},{3,1},{4,6},{6,4},{5,7},{7,5},{8,10},{10,8},{9,1... | collective-permute-start | bytes 1572872 | tf_op jit(solution)/shard_map/ppermute | solution.py:205
  10.6 1.6 copy-start.1
  12.2 1.6 copy-start.2
  13.8 1.2 copy-start.3
  15.0 1.2 copy-start.4
  17.3 2.0 %copy-start = (f32[8,2,512,128]{3,2,1,0:T(8,128)}, f32[8,2,512,128]{3,2,1,0:T(8,128)S(1)}, u32[]{:S(2)}) copy-start(f32[8,2,512,128]{3,2,1,0:T(8,128)S(1)} %shard_map.147) | copy-start | bytes 12582916
  20.7 13.4 %collective-permute-start.2 = (bf16[2,64,2048]{2,1,0:T(8,128)(2,1)S(1)}, bf16[2,64,2048]{2,1,0:T(8,128)(2,1)S(1)}, u32[]{:S(2)}, u32[]{:S(2)}) collective-permute-start(bf16[2,64,2048]{2,1,0:T(8,128)(2,1)S(1)} %collective-permute-done.refs_1_), channel_id=1, source_target_pairs={{0,4},{4,8},{8,12},{12,16},{16,20},{20,24},{24,28},{28,0},{1,5},{5... | collective-permute-start | bytes 1572872 | tf_op jit(solution)/shard_map/ppermute | solution.py:212
  20.7 13.4 %collective-permute-start.3 = (bf16[2,64,2048]{2,1,0:T(8,128)(2,1)S(1)}, bf16[2,64,2048]{2,1,0:T(8,128)(2,1)}, u32[]{:S(2)}, u32[]{:S(2)}) collective-permute-start(bf16[2,64,2048]{2,1,0:T(8,128)(2,1)S(1)} %collective-permute-done.1.refs_2_), channel_id=1, source_target_pairs={{0,28},{4,0},{8,4},{12,8},{16,12},{20,16},{24,20},{28,24},{1,29},{... | collective-permute-start | bytes 1572872 | tf_op jit(solution)/shard_map/ppermute | solution.py:212
  23.4 57.0 %all-to-all-start.1 = ((f32[8,2,512,128]{3,2,1,0:T(8,128)}), f32[8,2,512,128]{3,2,1,0:T(8,128)}, u32[]{:S(2)}, u32[]{:S(2)}) async-start(f32[8,2,512,128]{3,2,1,0:T(8,128)} %copy-done), calls=%async_computation.1 | async-start | bytes 8388608 | tf_op jit(solution)/shard_map/all_to_all | solution.py:218
  33.2 0.9 copy-start.10
  34.1 11.7 %collective-permute-start.5 = (bf16[2,64,2048]{2,1,0:T(8,128)(2,1)S(1)}, bf16[2,64,2048]{2,1,0:T(8,128)(2,1)S(1)}, u32[]{:S(2)}, u32[]{:S(2)}) collective-permute-start(bf16[2,64,2048]{2,1,0:T(8,128)(2,1)S(1)} %collective-permute-done.2.refs_3_), channel_id=1, source_target_pairs={{0,4},{4,8},{8,12},{12,16},{16,20},{20,24},{24,28},{28,0},{1,5},{5... | collective-permute-start | bytes 1572872 | tf_op jit(solution)/shard_map/ppermute | solution.py:212
  35.1 14.6 %collective-permute-start.6 = (bf16[2,64,2048]{2,1,0:T(8,128)(2,1)}, bf16[2,64,2048]{2,1,0:T(8,128)(2,1)S(1)}, u32[]{:S(2)}, u32[]{:S(2)}) collective-permute-start(bf16[2,64,2048]{2,1,0:T(8,128)(2,1)} %collective-permute-done.3.refs_4_), channel_id=1, source_target_pairs={{0,28},{4,0},{8,4},{12,8},{16,12},{20,16},{24,20},{28,24},{1,29},{... | collective-permute-start | bytes 1572872 | tf_op jit(solution)/shard_map/ppermute | solution.py:212
  36.8 13.0 %collective-permute-start.12 = (bf16[1,128,2048]{2,1,0:T(8,128)(2,1)}, bf16[1,128,2048]{2,1,0:T(8,128)(2,1)S(1)}, u32[]{:S(2)}, u32[]{:S(2)}) collective-permute-start(bf16[1,128,2048]{2,1,0:T(8,128)(2,1)} %param.15), channel_id=1, source_target_pairs={{0,1},{1,0},{2,3},{3,2},{4,5},{5,4},{6,7},{7,6},{8,9},{9,8},{10,11... | collective-permute-start | bytes 1572872 | tf_op jit(solution)/shard_map/ppermute | solution.py:206
  40.4 12.3 %collective-permute-start.13 = (bf16[1,128,2048]{2,1,0:T(8,128)(2,1)}, bf16[1,128,2048]{2,1,0:T(8,128)(2,1)S(1)}, u32[]{:S(2)}, u32[]{:S(2)}) collective-permute-start(bf16[1,128,2048]{2,1,0:T(8,128)(2,1)} %collective-permute-done.9), channel_id=1, source_target_pairs={{0,1},{1,0},{2,3},{3,2},{4,5},{5,4},{6,7},{7,6},{8,9},{9,8},{10,11... | collective-permute-start | bytes 1572872 | tf_op jit(solution)/shard_map/ppermute | solution.py:222
  40.4 12.4 %collective-permute-start.10 = (bf16[1,2048,128]{2,1,0:T(8,128)(2,1)}, bf16[1,2048,128]{2,1,0:T(8,128)(2,1)S(1)}, u32[]{:S(2)}, u32[]{:S(2)}) collective-permute-start(bf16[1,2048,128]{2,1,0:T(8,128)(2,1)} %param.14), channel_id=1, source_target_pairs={{0,1},{1,0},{2,3},{3,2},{4,5},{5,4},{6,7},{7,6},{8,9},{9,8},{10,11... | collective-permute-start | bytes 1572872 | tf_op jit(solution)/shard_map/ppermute | solution.py:206
  45.8 7.1 %collective-permute-start.11 = (bf16[1,2048,128]{2,1,0:T(8,128)(2,1)}, bf16[1,2048,128]{2,1,0:T(8,128)(2,1)S(1)}, u32[]{:S(2)}, u32[]{:S(2)}) collective-permute-start(bf16[1,2048,128]{2,1,0:T(8,128)(2,1)} %copy-done.10), channel_id=1, source_target_pairs={{0,1},{1,0},{2,3},{3,2},{4,5},{5,4},{6,7},{7,6},{8,9},{9,8},{10,11... | collective-permute-start | bytes 1572872 | tf_op jit(solution)/shard_map/ppermute | solution.py:222
  49.7 9.3 %collective-permute-start.7 = (bf16[1,64,2048]{2,1,0:T(8,128)(2,1)S(1)}, bf16[1,64,2048]{2,1,0:T(8,128)(2,1)S(1)}, u32[]{:S(2)}, u32[]{:S(2)}) collective-permute-start(bf16[1,64,2048]{2,1,0:T(8,128)(2,1)S(1)} %slice.8), channel_id=1, source_target_pairs={{0,4},{4,8},{8,12},{12,16},{16,20},{20,24},{24,28},{28,0},{1,5},{5... | collective-permute-start | bytes 786440 | tf_op jit(solution)/shard_map/ppermute | solution.py:228
  49.8 9.2 %collective-permute-start.8 = (bf16[1,64,2048]{2,1,0:T(8,128)(2,1)S(1)}, bf16[1,64,2048]{2,1,0:T(8,128)(2,1)S(1)}, u32[]{:S(2)}, u32[]{:S(2)}) collective-permute-start(bf16[1,64,2048]{2,1,0:T(8,128)(2,1)S(1)} %slice.9), channel_id=1, source_target_pairs={{0,28},{4,0},{8,4},{12,8},{16,12},{20,16},{24,20},{28,24},{1,29},{... | collective-permute-start | bytes 786440 | tf_op jit(solution)/shard_map/ppermute | solution.py:229
  59.0 5.2 %copy-start.5 = (bf16[1,64,2048]{2,1,0:T(8,128)(2,1)}, bf16[1,64,2048]{2,1,0:T(8,128)(2,1)S(1)}, u32[]{:S(2)}) copy-start(bf16[1,64,2048]{2,1,0:T(8,128)(2,1)S(1)} %collective-permute-done.8.refs_8_) | copy-start | bytes 786436
  64.2 6.2 %collective-permute-start.14 = (bf16[2,256,2048]{2,1,0:T(8,128)(2,1)}, bf16[2,256,2048]{2,1,0:T(8,128)(2,1)}, u32[]{:S(2)}, u32[]{:S(2)}) collective-permute-start(bf16[2,256,2048]{2,1,0:T(8,128)(2,1)} %shard_map.149), channel_id=1, source_target_pairs={{0,1},{1,0},{2,3},{3,2},{4,5},{5,4},{6,7},{7,6},{8,9},{9,8},{10,11... | collective-permute-start | bytes 6291464 | tf_op jit(solution)/shard_map/ppermute | solution.py:231
  64.9 1.4 copy-start.9
  64.9 1.5 copy-start.11
  64.9 1.6 copy-start.6
  66.5 3.9 %copy-start.7 = (bf16[1,2048,128]{2,1,0:T(8,128)(2,1)S(1)}, bf16[1,2048,128]{2,1,0:T(8,128)(2,1)}, u32[]{:S(2)}) copy-start(bf16[1,2048,128]{2,1,0:T(8,128)(2,1)} %du_ref.1) | copy-start | bytes 1572868
  66.5 3.9 %copy-start.8 = (bf16[1,128,2048]{2,1,0:T(8,128)(2,1)S(1)}, bf16[1,128,2048]{2,1,0:T(8,128)(2,1)}, u32[]{:S(2)}) copy-start(bf16[1,128,2048]{2,1,0:T(8,128)(2,1)} %dd_ref.1) | copy-start | bytes 1572868
  74.2 10.7 %copy-start.12 = (s32[16]{0:T(128)S(1)}, s32[16]{0:T(128)}, u32[]{:S(2)}) copy-start(s32[16]{0:T(128)} %param.19) | copy-start | bytes 196
  74.2 10.7 %copy-start.13 = (s32[8]{0:T(128)S(1)}, s32[8]{0:T(128)}, u32[]{:S(2)}) copy-start(s32[8]{0:T(128)} %param.18) | copy-start | bytes 100
  80.3 31.5 %all-to-all-start = ((bf16[16,512,128]{2,1,0:T(8,128)(2,1)}), bf16[16,512,128]{2,1,0:T(8,128)(2,1)S(1)}, u32[]{:S(2)}, u32[]{:S(2)}) async-start(bf16[16,512,128]{2,1,0:T(8,128)(2,1)} %shard_map.150), calls=%async_computation | async-start | bytes 4194304 | tf_op jit(solution)/shard_map/all_to_all | solution.py:236

commit v4 on v3

--- a/solution.py
+++ b/solution.py
@@ -92,24 +92,36 @@
     )(side, kept, got, drift_up, drift_down)
 
 
-def state_kernel(gu_ref, gd_ref, mu_ref, md_ref, out_ref):
+def state_kernel(gu_ref, gd_ref, mu_ref, md_ref, out_ref, plain_up_ref, plain_down_ref):
     for s in range(2):
-        out_ref[0, s, 0:256, :] = gu_ref[s].astype(F32) - 0.567 * mu_ref[s]
-        out_ref[0, s, 256:512, :] = down_in(gd_ref[s].astype(F32) - 0.567 * md_ref[s])
+        up = gu_ref[s].astype(F32) - 0.567 * mu_ref[s]
+        down = gd_ref[s].astype(F32) - 0.567 * md_ref[s]
+        out_ref[0, s, 0:256, :] = up
+        out_ref[0, s, 256:512, :] = down_in(down)
+        plain_up_ref[s] = up.astype(BF)
+        plain_down_ref[s] = down.astype(BF)
 
 
 def state(global_up, global_down, mom_up, mom_down):
     up = pl.BlockSpec((2, 256, 128), lambda i: (0, i, 0))
     down = pl.BlockSpec((2, 16, D), lambda i: (0, i, 0))
+    operands = [
+        pltpu.with_memory_space_constraint(t, pltpu.HBM)
+        for t in (global_up, global_down, mom_up, mom_down)
+    ]
     return pl.pallas_call(
         state_kernel,
         grid=(NR,),
-        out_shape=jax.ShapeDtypeStruct((NR, 2, 512, 128), F32),
+        out_shape=(
+            pltpu.HBM((NR, 2, 512, 128), F32),
+            pltpu.HBM((2, D, 128), BF),
+            pltpu.HBM((2, 128, D), BF),
+        ),
         in_specs=[up, down, up, down],
-        out_specs=pl.BlockSpec((1, 2, 512, 128), lambda i: (i, 0, 0, 0)),
+        out_specs=(pl.BlockSpec((1, 2, 512, 128), lambda i: (i, 0, 0, 0)), up, down),
         compiler_params=params(),
-        cost_estimate=pl.CostEstimate(flops=4 * MIB, bytes_accessed=10 * MIB, transcendentals=0),
-    )(global_up, global_down, mom_up, mom_down)
+        cost_estimate=pl.CostEstimate(flops=4 * MIB, bytes_accessed=12 * MIB, transcendentals=0),
+    )(*operands)
 
 
 def step_kernel(target_ref, factor_ref, p_ref, a_ref, out_ref, sum_ref):
@@ -143,6 +155,93 @@
         scratch_shapes=[pltpu.VMEM((16, rows, 128), F32)],
         compiler_params=params(16),
     )(target, factor, pieces, base)
+
+
+def short_step_kernel(target_ref, second_ref, factor_ref, p_ref, a_ref, out_ref, sum_ref):
+    sum_ref[...] = jnp.zeros_like(sum_ref)
+    for r in range(NR):
+        at = target_ref[r]
+        both = p_ref[2 * r].astype(F32) + p_ref[2 * r + 1].astype(F32)
+        sum_ref[at] = sum_ref[at] + both
+    for o in range(NR):
+        for m, slots_ref in enumerate((second_ref, target_ref)):
+            slot = slots_ref[o]
+            new = a_ref[slot // 2, slot % 2] - factor_ref[slot] * sum_ref[slot]
+            out_ref[o, m] = new.astype(BF)
+
+
+def short_step(target, second, factor, pieces, base):
+    rows = 128
+    return pl.pallas_call(
+        short_step_kernel,
+        grid=(512 // rows,),
+        out_shape=jax.ShapeDtypeStruct((NR, 2, 512, 128), BF),
+        in_specs=[
+            pl.BlockSpec(memory_space=pltpu.SMEM),
+            pl.BlockSpec(memory_space=pltpu.SMEM),
+            pl.BlockSpec(memory_space=pltpu.SMEM),
+            pl.BlockSpec((2 * NR, rows, 128), lambda i: (0, i, 0)),
+            pl.BlockSpec((NR, 2, rows, 128), lambda i: (0, 0, i, 0)),
+        ],
+        out_specs=pl.BlockSpec((NR, 2, rows, 128), lambda i: (0, 0, i, 0)),
+        scratch_shapes=[pltpu.VMEM((16, rows, 128), F32)],
+        compiler_params=params(16),
+    )(target, second, factor, pieces, base)
+
+
+def down_out(eighth):
+    return jnp.concatenate([eighth[256 + j * 16 : 272 + j * 16, :] for j in range(16)], axis=1)
+
+
+def short_place_kernel(plan_ref, got_ref, up_ref, down_ref, nu_ref, nd_ref, ru_ref, rd_ref):
+    for s in range(2):
+        source = plan_ref[s]
+
+        @pl.when(source == 2)
+        def _():
+            nu_ref[s] = up_ref[0]
+            nd_ref[s] = down_ref[0]
+
+        @pl.when(source != 2)
+        def _():
+            for p in range(2):
+                eighth = got_ref[p, jnp.minimum(source, 1)]
+                nu_ref[s, p * 256 : p * 256 + 256] = eighth[0:256]
+                nd_ref[s, p * 16 : p * 16 + 16] = down_out(eighth)
+
+    for p in range(2):
+        eighth = got_ref[p, 1]
+        ru_ref[0, p * 256 : p * 256 + 256] = eighth[0:256]
+        rd_ref[0, p * 16 : p * 16 + 16] = down_out(eighth)
+
+
+def short_place(plan, got, plain_up, plain_down):
+    def up(n):
+        return pl.BlockSpec((n, 512, 128), lambda i, plan: (0, i, 0))
+
+    def down(n):
+        return pl.BlockSpec((n, 32, D), lambda i, plan: (0, i, 0))
+
+    return pl.pallas_call(
+        short_place_kernel,
+        grid_spec=pltpu.PrefetchScalarGridSpec(
+            num_scalar_prefetch=1,
+            grid=(NR // 2,),
+            in_specs=[
+                pl.BlockSpec((2, 2, 512, 128), lambda i, plan: (i, 0, 0, 0)),
+                pl.BlockSpec((1, 512, 128), lambda i, plan: (plan[2], i, 0)),
+                pl.BlockSpec((1, 32, D), lambda i, plan: (plan[2], i, 0)),
+            ],
+            out_specs=(up(2), down(2), up(1), down(1)),
+        ),
+        out_shape=(
+            jax.ShapeDtypeStruct((2, D, 128), BF),
+            jax.ShapeDtypeStruct((2, 128, D), BF),
+            jax.ShapeDtypeStruct((1, D, 128), BF),
+            jax.ShapeDtypeStruct((1, 128, D), BF),
+        ),
+        compiler_params=params(16),
+    )(plan, got, plain_up, plain_down)
 
 
 def place_kernel(got_ref, nu_ref, nd_ref, ru_ref, rd_ref):
@@ -200,11 +299,22 @@
     module_ids = jnp.arange(slot_of.shape[0], dtype=jnp.int32)
     target = jnp.sum(jnp.where(path[:, None] == module_ids[None, :], slot_of[None, :], 0), axis=1)
     chosen = (target[:, None] == module_ids[None, :]).astype(F32)
-    factor = 1.33 / jnp.maximum(jnp.sum(chosen, axis=0), 1.0)
+    count = jnp.sum(chosen, axis=0)
+    factor = 1.33 / jnp.maximum(count, 1.0)
+    taken = (count > 0.0).reshape(NR, 2)
+    first = 2 * jnp.arange(NR, dtype=jnp.int32)
+    owned = target // 2 == first // 2
+    three = jnp.any(taken[:, 0] & taken[:, 1] & ~owned)
+    second = jnp.where(owned, first + 1 - target % 2, jnp.where(taken[:, 0], first, first + 1))
+    me = lax.axis_index(REGION)
+    slots = 2 * me + jnp.arange(2, dtype=jnp.int32)
+    source = jnp.where(slots == target[me], 1, jnp.where(slots == second[me], 0, 2))
+    plan = jnp.concatenate([source, 1 - second[me][None] % 2])
+    plan = plan.astype(jnp.int32)
 
     beside = [lax.ppermute(w, "xl", SWAP) for w in (w_up, w_down)]
     across = [lax.ppermute(w, "c", SWAP) for w in (w_up, w_down)]
-    base = state(global_up, global_down, mom_up, mom_down)
+    base, plain_up, plain_down = state(global_up, global_down, mom_up, mom_down)
     own = jnp.concatenate([acts, cotan], axis=0)
     right = left = own
     blocks = [own]
@@ -234,9 +344,16 @@
     side = lax.axis_index("xl").astype(jnp.int32)[None]
     pieces = pseudo(side, kept, got, drift_up, drift_down)
     pieces = lax.all_to_all(pieces, REGION + ("xl",), 0, 0, tiled=True)
-    reply = step(target, factor, pieces, base)
-    reply = lax.all_to_all(reply, REGION, 0, 0, tiled=True)
-    return place(reply)
+    def long_reply():
+        reply = step(target, factor, pieces, base)
+        return place(lax.all_to_all(reply, REGION, 0, 0, tiled=True))
+
+    def short_reply():
+        reply = short_step(target, second, factor, pieces, base)
+        reply = lax.all_to_all(reply, REGION, 0, 0, tiled=True)
+        return short_place(plan, reply, plain_up, plain_down)
+
+    return tuple(lax.cond(three, long_reply, short_reply))
 
 
 def solution(mesh):

time: 165 us -> 155 us (0.939)
  blocking collectives: 47 us -> 35.9 us
  Pallas kernels: 19.7 us -> 26.9 us
  local copies, waits for them, and re-layouts: 9.74 us -> 3.56 us
  waiting for transfers between devices: 49.1 us -> 43.9 us
  between operations: 0.85 us -> 3.45 us
  other arithmetic: 2.02 us -> 4.04 us
    all_to_all x1, blocking collectives: 47 us -> 35.9 us  [short_reply(): reply = lax.all_to_all(reply, REGION, 0, 0, tiled=True)]
    unnamed x29 -> x21, local copies, waits for them, and re-layouts: 8.73 us -> 1.1 us
    pallas_call x3, Pallas kernels: 6.92 us -> 14.1 us  [the longest x1 7.77 us: state(): pl.pallas_call(state_kernel, grid=(NR,), out_shape=(pltpu.HBM((NR, 2, 512...]
    all_to_all x1, waiting for transfers between devices: 26.6 us -> 20.5 us  [on_device(): pieces = lax.all_to_all(pieces, REGION + ('xl',), 0, 0, tiled=True)]
  transfers between devices with their start and end apart: 17 -> 17, of which waited for: 7 -> 7; matrix products, arithmetic and copies ran while one was open for 1% -> 4% of each run, Pallas kernels for 8% -> 13%
where the time goes in v4:
time: 155 us; the launch traced here: 154 us
  waiting for transfers between devices  43.9 us (28%)
  starting transfers between devices  36.3 us (23%)
  blocking collectives  35.9 us (23%)
  Pallas kernels  26.9 us (17%)
  other arithmetic  4.04 us (3%)
  local copies, waits for them, and re-layouts  3.56 us (2%)
  between operations  3.45 us (2%)
    all_to_all x1, blocking collectives, short_reply(): reply = lax.all_to_all(reply, REGION, 0, 0, tiled=True)  35.9 us
    all_to_all x1, waiting for transfers between devices, on_device(): pieces = lax.all_to_all(pieces, REGION + ('xl',), 0, 0, tiled=True)  20.5 us
    pallas_call x2, Pallas kernels, grads(): pl.pallas_call(functools.partial(grads_kernel, len(blocks)), out_shape=ja...  8.96 us
    ppermute x3, starting transfers between devices, on_device(): lax.ppermute(left, 'z', LEFT)  8.37 us
    ppermute x3, waiting for transfers between devices, on_device(): lax.ppermute(right, 'z', RIGHT)  8.09 us
    pallas_call x1, Pallas kernels, state(): pl.pallas_call(state_kernel, grid=(NR,), out_shape=(pltpu.HBM((NR, 2, 512...  7.77 us
    all_to_all x1, starting transfers between devices, on_device(): base = lax.all_to_all(base, REGION, 0, 0, tiled=True)  6.65 us
    all_to_all x1, waiting for transfers between devices, on_device(): base = lax.all_to_all(base, REGION, 0, 0, tiled=True)  6.14 us
  transfers between devices with their start and end apart: 17, of which 7 were waited for; matrix products, arithmetic and copies ran while one was open for 4% of the time, Pallas kernels for 13%

profile of v4, /device:TPU:1, one launch (start us, length us, event | category | flops | bytes accessed | tf_op | source)
XLA Modules:
  0.0 154.1 jit_solution(2010074608031366968)
XLA Ops:
  0.6 1.0 constant_dynamic-update-slice_fusion.1
  1.6 1.0 constant_dynamic-update-slice_fusion.refs_0_
  2.6 2.5 %collective-permute-start = (bf16[2,64,2048]{2,1,0:T(8,128)(2,1)S(1)}, bf16[2,64,2048]{2,1,0:T(8,128)(2,1)S(1)}, u32[]{:S(2)}, u32[]{:S(2)}) collective-permute-start(bf16[2,64,2048]{2,1,0:T(8,128)(2,1)S(1)} %constant_dynamic-update-slice_fusion.refs_0_), channel_id=1, source_target_pairs={{0,4},{4,8},{8,12},{12,16},{16,20},{20,24},{24,28},{28,0},{1,5},{5... | collective-permute-start | bytes 1572872 | tf_op jit(solution)/shard_map/ppermute | solution.py:322
  5.1 4.0 %collective-permute-start.1 = (bf16[2,64,2048]{2,1,0:T(8,128)(2,1)S(1)}, bf16[2,64,2048]{2,1,0:T(8,128)(2,1)S(1)}, u32[]{:S(2)}, u32[]{:S(2)}) collective-permute-start(bf16[2,64,2048]{2,1,0:T(8,128)(2,1)S(1)} %constant_dynamic-update-slice_fusion.refs_0_), channel_id=1, source_target_pairs={{0,28},{4,0},{8,4},{12,8},{16,12},{20,16},{24,20},{28,24},{1,29},{... | collective-permute-start | bytes 1572872 | tf_op jit(solution)/shard_map/ppermute | solution.py:322
  9.1 1.2 collective-permute-start.9
  10.4 0.3 collective-permute-start.4
  10.6 7.8 %shard_map.155 = (f32[8,2,512,128]{3,2,1,0:T(8,128)}, bf16[2,2048,128]{2,1,0:T(8,128)(2,1)}, bf16[2,128,2048]{2,1,0:T(8,128)(2,1)}) custom-call(bf16[2,2048,128]{2,1,0:T(8,128)(2,1)} %gu_ref.1, bf16[2,128,2048]{2,1,0:T(8,128)(2,1)} %gd_ref.1, f32[2,2048,128]{2,1,0:T(8,128)} %mu_ref.1, f32[2,128,2048]{2,1,0:T(8,128)} %md_ref.1), custom_call_target="tpu_custom_call" | custom-call | flops 4194304 | bytes 12582912 | tf_op jit(solution)/shard_map/pallas_call | solution.py:112
  18.4 2.3 %collective-permute-done.refs_1_ = bf16[2,64,2048]{2,1,0:T(8,128)(2,1)S(1)} collective-permute-done((bf16[2,64,2048]{2,1,0:T(8,128)(2,1)S(1)}, bf16[2,64,2048]{2,1,0:T(8,128)(2,1)S(1)}, u32[]{:S(2)}, u32[]{:S(2)}) %collective-permute-start) | collective-permute-done | bytes 524320 | tf_op jit(solution)/shard_map/ppermute | solution.py:322
  20.7 0.0 collective-permute-done.1.refs_2_
  20.7 0.0 collective-permute-start.2
  20.7 2.7 %collective-permute-start.3 = (bf16[2,64,2048]{2,1,0:T(8,128)(2,1)S(1)}, bf16[2,64,2048]{2,1,0:T(8,128)(2,1)}, u32[]{:S(2)}, u32[]{:S(2)}) collective-permute-start(bf16[2,64,2048]{2,1,0:T(8,128)(2,1)S(1)} %collective-permute-done.1.refs_2_), channel_id=1, source_target_pairs={{0,28},{4,0},{8,4},{12,8},{16,12},{20,16},{24,20},{28,24},{1,29},{... | collective-permute-start | bytes 1572872 | tf_op jit(solution)/shard_map/ppermute | solution.py:322
  23.4 0.0 collective-permute-done.9
  23.4 6.7 %all-to-all-start.3 = ((f32[8,2,512,128]{3,2,1,0:T(8,128)}), f32[8,2,512,128]{3,2,1,0:T(8,128)}, u32[]{:S(2)}, u32[]{:S(2)}) async-start(f32[8,2,512,128]{3,2,1,0:T(8,128)} %get-tuple-element.59), calls=%async_computation.3 | async-start | bytes 8388608 | tf_op jit(solution)/shard_map/all_to_all | solution.py:328
  30.0 3.1 %collective-permute-done.4 = bf16[1,2048,128]{2,1,0:T(8,128)(2,1)S(1)} collective-permute-done((bf16[1,2048,128]{2,1,0:T(8,128)(2,1)}, bf16[1,2048,128]{2,1,0:T(8,128)(2,1)S(1)}, u32[]{:S(2)}, u32[]{:S(2)}) %collective-permute-start.4) | collective-permute-done | bytes 524320 | tf_op jit(solution)/shard_map/ppermute | solution.py:315
  33.2 0.9 collective-permute-done.2.refs_3_
  34.1 0.0 copy-done.7
  34.1 0.0 collective-permute-done.3.refs_4_
  34.1 1.0 collective-permute-start.5
  35.1 1.7 %collective-permute-start.6 = (bf16[2,64,2048]{2,1,0:T(8,128)(2,1)}, bf16[2,64,2048]{2,1,0:T(8,128)(2,1)S(1)}, u32[]{:S(2)}, u32[]{:S(2)}) collective-permute-start(bf16[2,64,2048]{2,1,0:T(8,128)(2,1)} %collective-permute-done.3.refs_4_), channel_id=1, source_target_pairs={{0,28},{4,0},{8,4},{12,8},{16,12},{20,16},{24,20},{28,24},{1,29},{... | collective-permute-start | bytes 1572872 | tf_op jit(solution)/shard_map/ppermute | solution.py:322
  36.8 3.6 %collective-permute-start.12 = (bf16[1,128,2048]{2,1,0:T(8,128)(2,1)}, bf16[1,128,2048]{2,1,0:T(8,128)(2,1)S(1)}, u32[]{:S(2)}, u32[]{:S(2)}) collective-permute-start(bf16[1,128,2048]{2,1,0:T(8,128)(2,1)} %param.17), channel_id=1, source_target_pairs={{0,1},{1,0},{2,3},{3,2},{4,5},{5,4},{6,7},{7,6},{8,9},{9,8},{10,11... | collective-permute-start | bytes 1572872 | tf_op jit(solution)/shard_map/ppermute | solution.py:316
  40.4 0.0 collective-permute-start.13
  40.4 0.5 collective-permute-start.10
  40.9 4.8 %collective-permute-done.5.refs_5_ = bf16[2,64,2048]{2,1,0:T(8,128)(2,1)S(1)} collective-permute-done((bf16[2,64,2048]{2,1,0:T(8,128)(2,1)S(1)}, bf16[2,64,2048]{2,1,0:T(8,128)(2,1)S(1)}, u32[]{:S(2)}, u32[]{:S(2)}) %collective-permute-start.5) | collective-permute-done | bytes 524320 | tf_op jit(solution)/shard_map/ppermute | solution.py:322
  45.8 3.9 %collective-permute-start.11 = (bf16[1,2048,128]{2,1,0:T(8,128)(2,1)}, bf16[1,2048,128]{2,1,0:T(8,128)(2,1)S(1)}, u32[]{:S(2)}, u32[]{:S(2)}) collective-permute-start(bf16[1,2048,128]{2,1,0:T(8,128)(2,1)} %copy-done.7), channel_id=1, source_target_pairs={{0,1},{1,0},{2,3},{3,2},{4,5},{5,4},{6,7},{7,6},{8,9},{9,8},{10,11... | collective-permute-start | bytes 1572872 | tf_op jit(solution)/shard_map/ppermute | solution.py:332
  49.7 0.0 collective-permute-done.6.refs_6_
  49.7 0.1 collective-permute-start.7
  49.8 0.0 collective-permute-done.12
  49.8 2.9 %collective-permute-start.8 = (bf16[1,64,2048]{2,1,0:T(8,128)(2,1)S(1)}, bf16[1,64,2048]{2,1,0:T(8,128)(2,1)S(1)}, u32[]{:S(2)}, u32[]{:S(2)}) collective-permute-start(bf16[1,64,2048]{2,1,0:T(8,128)(2,1)S(1)} %slice.18), channel_id=1, source_target_pairs={{0,28},{4,0},{8,4},{12,8},{16,12},{20,16},{24,20},{28,24},{1,29},{... | collective-permute-start | bytes 786440 | tf_op jit(solution)/shard_map/ppermute | solution.py:339
  52.7 0.0 collective-permute-done.13
  52.7 0.1 pad_maximum_fusion.3.refs_10_
  52.9 0.0 collective-permute-done.10
  52.9 0.0 collective-permute-done.11
  52.9 0.1 pad_maximum_fusion.2.refs_9_
  53.0 6.0 %collective-permute-done.7.refs_7_ = bf16[1,64,2048]{2,1,0:T(8,128)(2,1)S(1)} collective-permute-done((bf16[1,64,2048]{2,1,0:T(8,128)(2,1)S(1)}, bf16[1,64,2048]{2,1,0:T(8,128)(2,1)S(1)}, u32[]{:S(2)}, u32[]{:S(2)}) %collective-permute-start.7) | collective-permute-done | bytes 262176 | tf_op jit(solution)/shard_map/ppermute | solution.py:338
  59.0 0.0 collective-permute-done.8.refs_8_
  59.0 5.1 %shard_map.157 = bf16[2,256,2048]{2,1,0:T(8,128)(2,1)} custom-call(bf16[2,64,2048]{2,1,0:T(8,128)(2,1)S(1)} %constant_dynamic-update-slice_fusion.refs_0_, bf16[2,64,2048]{2,1,0:T(8,128)(2,1)S(1)} %collective-permute-done.refs_1_, bf16[2,64,2048]{2,1,0:T(8,128)(2,1)S(1)} %collective-permute-done.1.refs_2_, ...), custom_call_target="tpu_custom_call" | custom-call | flops 2147483648 | bytes 8388608 | tf_op jit(solution)/shard_map/pallas_call | solution.py:51
  64.2 0.0 copy-done
  64.2 0.7 collective-permute-start.14
  64.9 1.4 pad_maximum_fusion.1.refs_10_
  66.3 0.1 copy-done.8
  66.4 0.1 pad_maximum_fusion.refs_9_
  66.5 0.0 copy-done.1
  66.5 0.0 copy-start.2
  66.5 0.0 copy-start.3
  66.5 3.8 %shard_map.156.kept_ref = f32[2,256,2048]{2,1,0:T(8,128)S(1)} custom-call(bf16[2,64,2048]{2,1,0:T(8,128)(2,1)S(1)} %constant_dynamic-update-slice_fusion.refs_0_, bf16[2,64,2048]{2,1,0:T(8,128)(2,1)S(1)} %collective-permute-done.refs_1_, bf16[2,64,2048]{2,1,0:T(8,128)(2,1)S(1)} %collective-permute-done.1.refs_2_, ...), custom_call_target="tpu_custom_call" | custom-call | flops 2147483648 | bytes 8388608 | tf_op jit(solution)/shard_map/pallas_call | solution.py:51
  70.3 0.0 collective-permute-done.14.got_ref
  70.4 3.8 %shard_map.158 = bf16[16,512,128]{2,1,0:T(8,128)(2,1)} custom-call(s32[1]{0:T(128)} %bitcast.side_ref, f32[2,256,2048]{2,1,0:T(8,128)S(1)} %shard_map.156.kept_ref, bf16[2,256,2048]{2,1,0:T(8,128)(2,1)} %collective-permute-done.14.got_ref, bf16[1,2048,128]{2,1,0:T(8,128)(2,1)S(1)} %copy-done.2, bf16[1,128,2048]{2,1,0:T(8,128)(2,1)S(1)} %copy-done.3), custom_call_target="tpu_custom_call" | custom-call | tf_op jit(solution)/shard_map/pallas_call | solution.py:86
  74.2 6.1 %all-to-all-done.3 = f32[8,2,512,128]{3,2,1,0:T(8,128)} async-done(((f32[8,2,512,128]{3,2,1,0:T(8,128)}), f32[8,2,512,128]{3,2,1,0:T(8,128)}, u32[]{:S(2)}, u32[]{:S(2)}) %all-to-all-start.3) | async-done | bytes 4194336 | tf_op jit(solution)/shard_map/all_to_all | solution.py:328
  80.3 4.6 %all-to-all-start.2 = ((bf16[16,512,128]{2,1,0:T(8,128)(2,1)}), bf16[16,512,128]{2,1,0:T(8,128)(2,1)S(1)}, u32[]{:S(2)}, u32[]{:S(2)}) async-start(bf16[16,512,128]{2,1,0:T(8,128)(2,1)} %shard_map.158), calls=%async_computation.2 | async-start | bytes 4194304 | tf_op jit(solution)/shard_map/all_to_all | solution.py:346
  85.0 0.2 select_reduce_fusion
  85.1 0.1 convert_reduce_fusion
  85.2 0.1 gt.8
  85.3 0.2 slice_reduce_fusion
  85.5 0.6 dynamic_slice.8
  88.1 0.6 dynamic_slice.7
  88.7 0.6 and_reduce_fusion
  90.0 1.3 compare_select_fusion.1
  91.3 0.1 pad_add_fusion
  91.4 20.5 %all-to-all-done.2 = bf16[16,512,128]{2,1,0:T(8,128)(2,1)S(1)} async-done(((bf16[16,512,128]{2,1,0:T(8,128)(2,1)}), bf16[16,512,128]{2,1,0:T(8,128)(2,1)S(1)}, u32[]{:S(2)}, u32[]{:S(2)}) %all-to-all-start.2) | async-done | bytes 2097184 | tf_op jit(solution)/shard_map/all_to_all | solution.py:346
  111.8 42.3 %conditional.1 = ((bf16[2,2048,128]{2,1,0:T(8,128)(2,1)}, bf16[2,128,2048]{2,1,0:T(8,128)(2,1)}, bf16[1,2048,128]{2,1,0:T(8,128)(2,1)}, bf16[1,128,2048]{2,1,0:T(8,128)(2,1)})) conditional(s32[]{:T(128)} %convert_element_type.7, (s32[8]{0:T(128)S(1)}, s32[8]{0:T(128)S(1)}, f32[16]{0:T(128)S(1)}, bf16[16,512,128]{2,1,0:T(8,128)(2,1)S(1)}, ...), branch_computations={%region_3.4_spmd, %region_4.5_spmd} | conditional | bytes 8388644 | solution.py:356
  111.8 3.6 %branch_0_fun.2 = bf16[8,2,512,128]{3,2,1,0:T(8,128)(2,1)S(1)} custom-call(s32[8]{0:T(128)S(1)} %get-tuple-element.25.target_ref, s32[8]{0:T(128)S(1)} %get-tuple-element.26.second_ref, f32[16]{0:T(128)S(1)} %get-tuple-element.27.factor_ref, bf16[16,512,128]{2,1,0:T(8,128)(2,1)S(1)} %get-tuple-element.28.p_ref, f32[8,2,512,128]{3,2,1,0:T(8,128)} %get-tuple-element.29.a_ref), custom_call_target="tpu_custom_call" | custom-call | tf_op jit(solution)/shard_map/cond/branch_0_fun/pallas_call | solution.py:175
  115.4 0.0 copy-start.5
  115.4 35.9 %all_to_all.18.got_ref = bf16[8,2,512,128]{3,2,1,0:T(8,128)(2,1)S(1)} all-to-all(bf16[8,2,512,128]{3,2,1,0:T(8,128)(2,1)S(1)} %branch_0_fun.2), channel_id=1, replica_groups=mesh['xh'=2,'y'=4,'z'=8,'xl'=2,'c'=2] {'xh','y'}, dimensions={0} | all-to-all | bytes 4194304 | tf_op jit(solution)/shard_map/cond/branch_0_fun/all_to_all | solution.py:353
  151.4 2.7 %branch_0_fun.3 = (bf16[2,2048,128]{2,1,0:T(8,128)(2,1)}, bf16[2,128,2048]{2,1,0:T(8,128)(2,1)}, bf16[1,2048,128]{2,1,0:T(8,128)(2,1)}, bf16[1,128,2048]{2,1,0:T(8,128)(2,1)}) custom-call(s32[3]{0:T(128)S(1)} %get-tuple-element.24.plan_ref, bf16[8,2,512,128]{3,2,1,0:T(8,128)(2,1)S(1)} %all_to_all.18.got_ref, ...), custom_call_target="tpu_custom_call" | custom-call | tf_op jit(solution)/shard_map/cond/branch_0_fun/pallas_call | solution.py:225
  (20 shorter events, 0.1 us)
Async XLA Ops:
  2.6 18.1 %collective-permute-start = (bf16[2,64,2048]{2,1,0:T(8,128)(2,1)S(1)}, bf16[2,64,2048]{2,1,0:T(8,128)(2,1)S(1)}, u32[]{:S(2)}, u32[]{:S(2)}) collective-permute-start(bf16[2,64,2048]{2,1,0:T(8,128)(2,1)S(1)} %constant_dynamic-update-slice_fusion.refs_0_), channel_id=1, source_target_pairs={{0,4},{4,8},{8,12},{12,16},{16,20},{20,24},{24,28},{28,0},{1,5},{5... | collective-permute-start | bytes 1572872 | tf_op jit(solution)/shard_map/ppermute | solution.py:322
  5.1 15.6 %collective-permute-start.1 = (bf16[2,64,2048]{2,1,0:T(8,128)(2,1)S(1)}, bf16[2,64,2048]{2,1,0:T(8,128)(2,1)S(1)}, u32[]{:S(2)}, u32[]{:S(2)}) collective-permute-start(bf16[2,64,2048]{2,1,0:T(8,128)(2,1)S(1)} %constant_dynamic-update-slice_fusion.refs_0_), channel_id=1, source_target_pairs={{0,28},{4,0},{8,4},{12,8},{16,12},{20,16},{24,20},{28,24},{1,29},{... | collective-permute-start | bytes 1572872 | tf_op jit(solution)/shard_map/ppermute | solution.py:322
  9.1 14.2 %collective-permute-start.9 = (bf16[1,128,2048]{2,1,0:T(8,128)(2,1)}, bf16[1,128,2048]{2,1,0:T(8,128)(2,1)}, u32[]{:S(2)}, u32[]{:S(2)}) collective-permute-start(bf16[1,128,2048]{2,1,0:T(8,128)(2,1)} %param.17), channel_id=1, source_target_pairs={{0,2},{2,0},{1,3},{3,1},{4,6},{6,4},{5,7},{7,5},{8,10},{10,8},{9,1... | collective-permute-start | bytes 1572872 | tf_op jit(solution)/shard_map/ppermute | solution.py:315
  10.4 22.8 %collective-permute-start.4 = (bf16[1,2048,128]{2,1,0:T(8,128)(2,1)}, bf16[1,2048,128]{2,1,0:T(8,128)(2,1)S(1)}, u32[]{:S(2)}, u32[]{:S(2)}) collective-permute-start(bf16[1,2048,128]{2,1,0:T(8,128)(2,1)} %param.16), channel_id=1, source_target_pairs={{0,2},{2,0},{1,3},{3,1},{4,6},{6,4},{5,7},{7,5},{8,10},{10,8},{9,1... | collective-permute-start | bytes 1572872 | tf_op jit(solution)/shard_map/ppermute | solution.py:315
  20.7 13.4 %collective-permute-start.2 = (bf16[2,64,2048]{2,1,0:T(8,128)(2,1)S(1)}, bf16[2,64,2048]{2,1,0:T(8,128)(2,1)S(1)}, u32[]{:S(2)}, u32[]{:S(2)}) collective-permute-start(bf16[2,64,2048]{2,1,0:T(8,128)(2,1)S(1)} %collective-permute-done.refs_1_), channel_id=1, source_target_pairs={{0,4},{4,8},{8,12},{12,16},{16,20},{20,24},{24,28},{28,0},{1,5},{5... | collective-permute-start | bytes 1572872 | tf_op jit(solution)/shard_map/ppermute | solution.py:322
  20.7 13.4 %collective-permute-start.3 = (bf16[2,64,2048]{2,1,0:T(8,128)(2,1)S(1)}, bf16[2,64,2048]{2,1,0:T(8,128)(2,1)}, u32[]{:S(2)}, u32[]{:S(2)}) collective-permute-start(bf16[2,64,2048]{2,1,0:T(8,128)(2,1)S(1)} %collective-permute-done.1.refs_2_), channel_id=1, source_target_pairs={{0,28},{4,0},{8,4},{12,8},{16,12},{20,16},{24,20},{28,24},{1,29},{... | collective-permute-start | bytes 1572872 | tf_op jit(solution)/shard_map/ppermute | solution.py:322
  23.4 57.0 %all-to-all-start.3 = ((f32[8,2,512,128]{3,2,1,0:T(8,128)}), f32[8,2,512,128]{3,2,1,0:T(8,128)}, u32[]{:S(2)}, u32[]{:S(2)}) async-start(f32[8,2,512,128]{3,2,1,0:T(8,128)} %get-tuple-element.59), calls=%async_computation.3 | async-start | bytes 8388608 | tf_op jit(solution)/shard_map/all_to_all | solution.py:328
  33.2 0.9 copy-start.7
  34.1 11.7 %collective-permute-start.5 = (bf16[2,64,2048]{2,1,0:T(8,128)(2,1)S(1)}, bf16[2,64,2048]{2,1,0:T(8,128)(2,1)S(1)}, u32[]{:S(2)}, u32[]{:S(2)}) collective-permute-start(bf16[2,64,2048]{2,1,0:T(8,128)(2,1)S(1)} %collective-permute-done.2.refs_3_), channel_id=1, source_target_pairs={{0,4},{4,8},{8,12},{12,16},{16,20},{20,24},{24,28},{28,0},{1,5},{5... | collective-permute-start | bytes 1572872 | tf_op jit(solution)/shard_map/ppermute | solution.py:322
  35.1 14.6 %collective-permute-start.6 = (bf16[2,64,2048]{2,1,0:T(8,128)(2,1)}, bf16[2,64,2048]{2,1,0:T(8,128)(2,1)S(1)}, u32[]{:S(2)}, u32[]{:S(2)}) collective-permute-start(bf16[2,64,2048]{2,1,0:T(8,128)(2,1)} %collective-permute-done.3.refs_4_), channel_id=1, source_target_pairs={{0,28},{4,0},{8,4},{12,8},{16,12},{20,16},{24,20},{28,24},{1,29},{... | collective-permute-start | bytes 1572872 | tf_op jit(solution)/shard_map/ppermute | solution.py:322
  36.8 13.0 %collective-permute-start.12 = (bf16[1,128,2048]{2,1,0:T(8,128)(2,1)}, bf16[1,128,2048]{2,1,0:T(8,128)(2,1)S(1)}, u32[]{:S(2)}, u32[]{:S(2)}) collective-permute-start(bf16[1,128,2048]{2,1,0:T(8,128)(2,1)} %param.17), channel_id=1, source_target_pairs={{0,1},{1,0},{2,3},{3,2},{4,5},{5,4},{6,7},{7,6},{8,9},{9,8},{10,11... | collective-permute-start | bytes 1572872 | tf_op jit(solution)/shard_map/ppermute | solution.py:316
  40.4 12.3 %collective-permute-start.13 = (bf16[1,128,2048]{2,1,0:T(8,128)(2,1)}, bf16[1,128,2048]{2,1,0:T(8,128)(2,1)S(1)}, u32[]{:S(2)}, u32[]{:S(2)}) collective-permute-start(bf16[1,128,2048]{2,1,0:T(8,128)(2,1)} %collective-permute-done.9), channel_id=1, source_target_pairs={{0,1},{1,0},{2,3},{3,2},{4,5},{5,4},{6,7},{7,6},{8,9},{9,8},{10,11... | collective-permute-start | bytes 1572872 | tf_op jit(solution)/shard_map/ppermute | solution.py:332
  40.4 12.4 %collective-permute-start.10 = (bf16[1,2048,128]{2,1,0:T(8,128)(2,1)}, bf16[1,2048,128]{2,1,0:T(8,128)(2,1)S(1)}, u32[]{:S(2)}, u32[]{:S(2)}) collective-permute-start(bf16[1,2048,128]{2,1,0:T(8,128)(2,1)} %param.16), channel_id=1, source_target_pairs={{0,1},{1,0},{2,3},{3,2},{4,5},{5,4},{6,7},{7,6},{8,9},{9,8},{10,11... | collective-permute-start | bytes 1572872 | tf_op jit(solution)/shard_map/ppermute | solution.py:316
  45.8 7.1 %collective-permute-start.11 = (bf16[1,2048,128]{2,1,0:T(8,128)(2,1)}, bf16[1,2048,128]{2,1,0:T(8,128)(2,1)S(1)}, u32[]{:S(2)}, u32[]{:S(2)}) collective-permute-start(bf16[1,2048,128]{2,1,0:T(8,128)(2,1)} %copy-done.7), channel_id=1, source_target_pairs={{0,1},{1,0},{2,3},{3,2},{4,5},{5,4},{6,7},{7,6},{8,9},{9,8},{10,11... | collective-permute-start | bytes 1572872 | tf_op jit(solution)/shard_map/ppermute | solution.py:332
  49.7 9.3 %collective-permute-start.7 = (bf16[1,64,2048]{2,1,0:T(8,128)(2,1)S(1)}, bf16[1,64,2048]{2,1,0:T(8,128)(2,1)S(1)}, u32[]{:S(2)}, u32[]{:S(2)}) collective-permute-start(bf16[1,64,2048]{2,1,0:T(8,128)(2,1)S(1)} %slice.17), channel_id=1, source_target_pairs={{0,4},{4,8},{8,12},{12,16},{16,20},{20,24},{24,28},{28,0},{1,5},{5... | collective-permute-start | bytes 786440 | tf_op jit(solution)/shard_map/ppermute | solution.py:338
  49.8 9.2 %collective-permute-start.8 = (bf16[1,64,2048]{2,1,0:T(8,128)(2,1)S(1)}, bf16[1,64,2048]{2,1,0:T(8,128)(2,1)S(1)}, u32[]{:S(2)}, u32[]{:S(2)}) collective-permute-start(bf16[1,64,2048]{2,1,0:T(8,128)(2,1)S(1)} %slice.18), channel_id=1, source_target_pairs={{0,28},{4,0},{8,4},{12,8},{16,12},{20,16},{24,20},{28,24},{1,29},{... | collective-permute-start | bytes 786440 | tf_op jit(solution)/shard_map/ppermute | solution.py:339
  59.0 5.2 %copy-start = (bf16[1,64,2048]{2,1,0:T(8,128)(2,1)}, bf16[1,64,2048]{2,1,0:T(8,128)(2,1)S(1)}, u32[]{:S(2)}) copy-start(bf16[1,64,2048]{2,1,0:T(8,128)(2,1)S(1)} %collective-permute-done.8.refs_8_) | copy-start | bytes 786436
  64.2 6.2 %collective-permute-start.14 = (bf16[2,256,2048]{2,1,0:T(8,128)(2,1)}, bf16[2,256,2048]{2,1,0:T(8,128)(2,1)}, u32[]{:S(2)}, u32[]{:S(2)}) collective-permute-start(bf16[2,256,2048]{2,1,0:T(8,128)(2,1)} %shard_map.157), channel_id=1, source_target_pairs={{0,1},{1,0},{2,3},{3,2},{4,5},{5,4},{6,7},{7,6},{8,9},{9,8},{10,11... | collective-permute-start | bytes 6291464 | tf_op jit(solution)/shard_map/ppermute | solution.py:341
  64.9 1.4 copy-start.6
  64.9 1.5 copy-start.8
  64.9 1.6 %copy-start.1 = (bf16[1,64,2048]{2,1,0:T(8,128)(2,1)S(1)}, bf16[1,64,2048]{2,1,0:T(8,128)(2,1)}, u32[]{:S(2)}) copy-start(bf16[1,64,2048]{2,1,0:T(8,128)(2,1)} %copy-done) | copy-start | bytes 786436
  66.5 3.9 %copy-start.2 = (bf16[1,2048,128]{2,1,0:T(8,128)(2,1)S(1)}, bf16[1,2048,128]{2,1,0:T(8,128)(2,1)}, u32[]{:S(2)}) copy-start(bf16[1,2048,128]{2,1,0:T(8,128)(2,1)} %du_ref.1) | copy-start | bytes 1572868
  66.5 3.9 %copy-start.3 = (bf16[1,128,2048]{2,1,0:T(8,128)(2,1)S(1)}, bf16[1,128,2048]{2,1,0:T(8,128)(2,1)}, u32[]{:S(2)}) copy-start(bf16[1,128,2048]{2,1,0:T(8,128)(2,1)} %dd_ref.1) | copy-start | bytes 1572868
  74.2 10.7 %copy-start.9 = (s32[16]{0:T(128)S(1)}, s32[16]{0:T(128)}, u32[]{:S(2)}) copy-start(s32[16]{0:T(128)} %param.21) | copy-start | bytes 196
  74.2 10.8 %copy-start.10 = (s32[8]{0:T(128)S(1)}, s32[8]{0:T(128)}, u32[]{:S(2)}) copy-start(s32[8]{0:T(128)} %param.20) | copy-start | bytes 100
  74.2 37.6 %copy-start.4 = (bf16[2,2048,128]{2,1,0:T(8,128)(2,1)S(1)}, bf16[2,2048,128]{2,1,0:T(8,128)(2,1)}, u32[]{:S(2)}) copy-start(bf16[2,2048,128]{2,1,0:T(8,128)(2,1)} %get-tuple-element.60) | copy-start | bytes 3145732
  80.3 31.5 %all-to-all-start.2 = ((bf16[16,512,128]{2,1,0:T(8,128)(2,1)}), bf16[16,512,128]{2,1,0:T(8,128)(2,1)S(1)}, u32[]{:S(2)}, u32[]{:S(2)}) async-start(bf16[16,512,128]{2,1,0:T(8,128)(2,1)} %shard_map.158), calls=%async_computation.2 | async-start | bytes 4194304 | tf_op jit(solution)/shard_map/all_to_all | solution.py:346
  115.4 36.0 %copy-start.5 = (bf16[2,128,2048]{2,1,0:T(8,128)(2,1)S(1)}, bf16[2,128,2048]{2,1,0:T(8,128)(2,1)}, u32[]{:S(2)}) copy-start(bf16[2,128,2048]{2,1,0:T(8,128)(2,1)} %get-tuple-element.31.down_ref) | copy-start | bytes 3145732 | tf_op jit(solution)/shard_map/cond
